TPU v7x, 128 devices: a whole 4x4x4 slice. The times are simulated.
128 devices in a mesh: section: 2 (over core), expert: 16 (over y, z), tensor: 4 (over x).
Axes of the slice: x: 4, y: 4, z: 4, core: 2. Of those that a mesh axis runs over, the one named last changes fastest.
Arguments:
- inputs: bfloat16 [2, 2048, 1536], P(None, 'expert'), may hold values from -6 to 6
- cotangent: bfloat16 [2, 2048, 1536], P(None, 'expert'), may hold values from -6 to 6
- documents: int32 [2, 16, 128], P(None, 'expert'), may hold values from 0 to 3, never falling along the last dimension, each value on 1 to 64 neighbouring positions
- routes: int32 [2, 2048, 8], P(None, 'expert'), may hold values from 0 to 31, all different within a row; in each aligned block of 128 rows (0 to 127, 128 to 255, ..., all dimensions but the last counted through in order) at most 48 rows name the same one
- gain_attn: bfloat16 [2, 1536], P('section'), may hold values from 0.25 to 1.75
- w_query: bfloat16 [2, 1536, 1536], P('section', None, 'tensor'), may hold values from -0.15625 to 0.15625
- w_key: bfloat16 [2, 1536, 512], P('section', None, 'tensor'), may hold values from -0.15625 to 0.15625
- w_value: bfloat16 [2, 1536, 512], P('section', None, 'tensor'), may hold values from -0.15625 to 0.15625
- w_out: bfloat16 [2, 1536, 1536], P('section', 'tensor'), may hold values from -0.625 to 0.625
- gain_moe: bfloat16 [2, 1536], P('section'), may hold values from 0.25 to 1.75
- w_router: bfloat16 [2, 1536, 32], P('section'), may hold values from -0.078125 to 0.078125
- w_gate: bfloat16 [2, 32, 1536, 512], P('section', 'expert', None, 'tensor'), may hold values from -0.15625 to 0.15625
- w_up: bfloat16 [2, 32, 1536, 512], P('section', 'expert', None, 'tensor'), may hold values from -0.15625 to 0.15625
- w_down: bfloat16 [2, 32, 512, 1536], P('section', 'expert', 'tensor'), may hold values from -1 to 1
Outputs:
- activations: bfloat16 [2, 2, 2048, 1536], P('section', None, 'expert')
- input_grads: bfloat16 [2, 2, 2048, 1536], P('section', None, 'expert')
- grad_gain_attn: float32 [2, 1536], P('section')
- grad_query: float32 [2, 1536, 1536], P('section', None, 'tensor')
- grad_key: float32 [2, 1536, 512], P('section', None, 'tensor')
- grad_value: float32 [2, 1536, 512], P('section', None, 'tensor')
- grad_out: float32 [2, 1536, 1536], P('section', 'tensor')
- grad_gain_moe: float32 [2, 1536], P('section')
- grad_router: float32 [2, 1536, 32], P('section')
- grad_gate: float32 [2, 32, 1536, 512], P('section', 'expert', None, 'tensor')
- grad_up: float32 [2, 32, 1536, 512], P('section', 'expert', None, 'tensor')
- grad_down: float32 [2, 32, 512, 1536], P('section', 'expert', 'tensor')
Inputs may be any that keep to these rules, and one draw needn't show every extreme that they name: `documents`: document numbers never fall within a sequence; a document has at most half of 128 tokens, and some document has exactly that many. `routes`: each token names 8 different experts. Among the tokens of one sequence no expert is named more than 48 times, and in every draw some expert is named exactly 48 times by the tokens of some sequence.
All inputs are finite; a program needn't handle non-finite values.
Results may differ from a plain program's by a relative error of at most 0.038.
Values may be sent and summed in bfloat16 or wider, within the bound.
No kernel may reach another device: no remote copies, remote signals or barrier semaphores. Data moves between devices by JAX's collectives and lax.ppermute only.
A program may use at most 256 MiB of HBM per device.

v0:
```python
import math

import jax
import jax.numpy as jnp
from jax import lax
from jax.sharding import PartitionSpec as P

HEADS = 24
KV_HEADS = 8
HEAD_DIM = 64


EPSILON = 1e-06


def copy_for_each(array, axis):
    copies = jnp.broadcast_to(array, (lax.axis_size(axis), *array.shape))
    return lax.all_to_all(copies, axis, split_axis=0, concat_axis=0, tiled=True)


def of_everyone(array, axis):
    everything = copy_for_each(array, axis)
    return jnp.sum(everything.astype(jnp.float32), axis=0)


def side_by_side(arrays, axis, dim, along):
    widths = [a.shape[along] for a in arrays]
    both = jnp.concatenate(arrays, axis=along)
    result = lax.all_gather(both, axis, axis=dim, tiled=True)
    return tuple(jnp.split(result, [sum(widths[:k]) for k in range(1, len(widths))], axis=along))


def from_behind(array, axis, by):
    length = lax.axis_size(axis)
    pairs = [(i, i + by) for i in range(length) if 0 <= i + by < length]
    return lax.ppermute(array, axis, pairs)


def in_blocks(array, dim, length):
    before, after = (array.shape[:dim], array.shape[dim + 1 :])
    return jnp.moveaxis(array.reshape(*before, length, -1, *after), dim, 0)


def summed_on_arrival(array, axis, dim):
    length = lax.axis_size(axis)
    pieces = lax.all_to_all(in_blocks(array, dim, length), axis, 0, 0, tiled=True)
    return jnp.sum(pieces.astype(jnp.float32), axis=0)


def side_by_side_2(arrays, axis, dim, along):
    widths = [a.shape[along] for a in arrays]
    both = jnp.concatenate(arrays, axis=along)
    result = summed_on_arrival(both, axis, dim)
    return tuple(jnp.split(result, [sum(widths[:k]) for k in range(1, len(widths))], axis=along))


def rotate_half(values, cosine_table, sine_table):
    middle_at = values.shape[-1] // 2
    turned = jnp.concatenate([-values[..., middle_at:], values[..., :middle_at]], axis=-1)
    return values * cosine_table + turned * sine_table


def rotate_back(values, cosine_table, sine_table):
    middle_at = values.shape[-1] // 2
    scaled = values * sine_table
    return values * cosine_table + jnp.concatenate(
        [scaled[..., middle_at:], -scaled[..., :middle_at]], axis=-1
    )


def rope_tables(document):
    places = jnp.arange(document.shape[0], dtype=jnp.int32)
    starts = jnp.sum((document[None, :] < document[:, None]).astype(jnp.int32), axis=1)
    offsets = (places - starts).astype(jnp.float32)
    frequency = jnp.exp(
        jnp.arange(HEAD_DIM // 2, dtype=jnp.float32) * (-2.0 * math.log(10000.0) / HEAD_DIM)
    )
    angle_table = offsets[:, None] * frequency[None, :]
    angle_table = jnp.concatenate([angle_table, angle_table], axis=-1)
    return (jnp.cos(angle_table), jnp.sin(angle_table))


def allowed_pairs(document):
    places = jnp.arange(document.shape[0], dtype=jnp.int32)
    return (document[:, None] == document[None, :]) & (places[None, :] <= places[:, None])


def slot_numbers(route_rows, expert_count):
    flat_routes = route_rows.reshape(-1)
    onehot_hits = (
        flat_routes[:, None] == jnp.arange(expert_count, dtype=jnp.int32)[None, :]
    ).astype(jnp.int32)
    earlier = jnp.cumsum(onehot_hits, axis=0) - onehot_hits
    return jnp.sum(earlier * onehot_hits, axis=1).reshape(route_rows.shape)


def norm_parts(level_rows, gain):
    inverse = lax.rsqrt(jnp.mean(level_rows * level_rows, axis=-1, keepdims=True) + EPSILON)
    unit_rows = level_rows * inverse
    return (inverse, unit_rows, unit_rows * gain.astype(jnp.float32))


def norm_back(back_scaled, inverse, unit_rows, gain):
    back_unit = back_scaled * gain.astype(jnp.float32)
    back_level = inverse * (
        back_unit - unit_rows * jnp.mean(back_unit * unit_rows, axis=-1, keepdims=True)
    )
    return (back_level, jnp.sum(back_scaled * unit_rows, axis=0))


def contract_rows(left_rows, right_rows):
    return lax.dot_general(
        left_rows, right_rows, (((0,), (0,)), ((), ())), preferred_element_type=jnp.float32
    )


def contract_cols(left_rows, right_rows):
    return lax.dot_general(
        left_rows, right_rows, (((1,), (1,)), ((), ())), preferred_element_type=jnp.float32
    )


def head_totals(partial_sum):
    return of_everyone(partial_sum.astype(jnp.bfloat16), "tensor").astype(jnp.float32)


def send_rows(buffer):
    share_rows = buffer.shape[1] // lax.axis_size("tensor")
    own_share = lax.dynamic_slice_in_dim(
        buffer, lax.axis_index("tensor") * share_rows, share_rows, 1
    )
    moved_rows = lax.all_to_all(own_share, "expert", split_axis=0, concat_axis=0, tiled=True)
    return moved_rows


def return_rows(partial_terms):
    reduced = partial_terms.astype(jnp.bfloat16)
    moved_rows = lax.all_to_all(reduced, "expert", split_axis=0, concat_axis=0, tiled=True)
    return lax.all_gather(moved_rows, "tensor", axis=1, tiled=True)


def score_table(queries, key_rows, document):
    raw_scores = jnp.einsum(
        "qkgd,pkd->kgqp", queries, key_rows, preferred_element_type=jnp.float32
    ) * HEAD_DIM ** (-0.5)
    return jnp.where(allowed_pairs(document)[None, None], raw_scores, -1e30)


def layer_sizes(entry_rows, route_ids, w_key, w_router):
    row_count = entry_rows.shape[0]
    expert_count = w_router.shape[1]
    top_count = route_ids.shape[1]
    capacity = min(row_count, row_count * top_count * 3 // (2 * expert_count))
    return (
        row_count,
        w_key.shape[1] // HEAD_DIM,
        HEADS // KV_HEADS,
        expert_count,
        top_count,
        capacity,
    )


def forward_layer(entry_rows, document, route_ids, params):
    gain_attn, w_query, w_key, w_value, w_out, gain_moe, w_router, w_gate, w_up, w_down = params
    row_count, groups, sharing, expert_count, top_count, capacity = layer_sizes(
        entry_rows, route_ids, w_key, w_router
    )
    model_width = entry_rows.shape[1]
    level_rows = entry_rows.astype(jnp.float32)
    first_inverse, first_unit, first_scaled = norm_parts(level_rows, gain_attn)
    normed = first_scaled.astype(jnp.bfloat16)
    cosine_table, sine_table = rope_tables(document)
    query_raw = jnp.dot(normed, w_query, preferred_element_type=jnp.float32).reshape(
        row_count, groups, sharing, HEAD_DIM
    )
    queries = rotate_half(
        query_raw, cosine_table[:, None, None, :], sine_table[:, None, None, :]
    ).astype(jnp.bfloat16)
    key_raw = jnp.dot(normed, w_key, preferred_element_type=jnp.float32).reshape(
        row_count, groups, HEAD_DIM
    )
    key_rows = rotate_half(key_raw, cosine_table[:, None, :], sine_table[:, None, :]).astype(
        jnp.bfloat16
    )
    value_rows = (
        jnp.dot(normed, w_value, preferred_element_type=jnp.float32)
        .astype(jnp.bfloat16)
        .reshape(row_count, groups, HEAD_DIM)
    )
    scores = score_table(queries, key_rows, document)
    row_peak = jnp.max(scores, axis=-1, keepdims=True)
    exp_scores = jnp.exp(scores - row_peak)
    row_total = jnp.sum(exp_scores, axis=-1, keepdims=True)
    probability = exp_scores / row_total
    log_total = row_peak + jnp.log(row_total)
    attended = jnp.einsum(
        "kgqp,pkd->qkgd",
        probability.astype(jnp.bfloat16),
        value_rows,
        preferred_element_type=jnp.float32,
    )
    attended = attended.astype(jnp.bfloat16).reshape(row_count, groups * sharing * HEAD_DIM)
    middle = level_rows + head_totals(jnp.dot(attended, w_out, preferred_element_type=jnp.float32))
    second_inverse, second_unit, second_scaled = norm_parts(middle, gain_moe)
    shaped = second_scaled.astype(jnp.bfloat16)
    logits = jnp.dot(shaped, w_router, preferred_element_type=jnp.float32)
    choose = (
        route_ids[:, :, None] == jnp.arange(expert_count, dtype=jnp.int32)[None, None, :]
    ).astype(jnp.float32)
    gate_weights = jax.nn.softmax(jnp.sum(choose * logits[:, None, :], axis=-1), axis=-1)
    position = (route_ids * capacity + slot_numbers(route_ids, expert_count)).reshape(-1)
    filler = (
        jnp.zeros((expert_count * capacity,), jnp.int32)
        .at[position]
        .set(jnp.arange(row_count * top_count, dtype=jnp.int32) + 1)
    )
    source_rows = jnp.maximum(filler - 1, 0) // top_count
    buffer = jnp.where((filler > 0)[:, None], shaped[source_rows], jnp.zeros((), jnp.bfloat16))
    moved = send_rows(buffer.reshape(expert_count, capacity, model_width))
    arrived = moved.reshape(-1, w_gate.shape[0], moved.shape[1], model_width)
    gate_act = jnp.einsum("secd,edf->secf", arrived, w_gate, preferred_element_type=jnp.float32)
    up_act = jnp.einsum("secd,edf->secf", arrived, w_up, preferred_element_type=jnp.float32)
    hidden = (jax.nn.silu(gate_act) * up_act).astype(jnp.bfloat16)
    expert_terms = jnp.einsum("secf,efd->secd", hidden, w_down, preferred_element_type=jnp.float32)
    result = return_rows(expert_terms.reshape(-1, expert_terms.shape[2], model_width))
    picked = result.reshape(expert_count * capacity, model_width)[position].reshape(
        row_count, top_count, model_width
    )
    output = middle + jnp.sum(gate_weights[..., None] * picked.astype(jnp.float32), axis=1)
    saved = (
        entry_rows,
        queries,
        key_rows,
        value_rows,
        log_total,
        attended,
        middle,
        shaped,
        gate_weights,
        filler,
        position,
        arrived,
        gate_act,
        up_act,
        hidden,
        picked,
    )
    return (output.astype(jnp.bfloat16), saved)


def backward_layer(flow_rows, saved, document, route_ids, params):
    gain_attn, w_query, w_key, w_value, w_out, gain_moe, w_router, w_gate, w_up, w_down = params
    (
        entry_rows,
        queries,
        key_rows,
        value_rows,
        log_total,
        attended,
        middle,
        shaped,
        gate_weights,
        filler,
        position,
        arrived,
        gate_act,
        up_act,
        hidden,
        picked,
    ) = saved
    row_count, groups, sharing, expert_count, top_count, capacity = layer_sizes(
        entry_rows, route_ids, w_key, w_router
    )
    model_width = entry_rows.shape[1]
    flowing = flow_rows.astype(jnp.float32)
    back_gates = jnp.sum(flowing[:, None, :] * picked.astype(jnp.float32), axis=-1)
    back_chosen = gate_weights * (
        back_gates - jnp.sum(gate_weights * back_gates, axis=-1, keepdims=True)
    )
    choose = (
        route_ids[:, :, None] == jnp.arange(expert_count, dtype=jnp.int32)[None, None, :]
    ).astype(jnp.float32)
    back_logits = jnp.sum(choose * back_chosen[:, :, None], axis=1).astype(jnp.bfloat16)
    grad_router = contract_rows(shaped, back_logits)
    back_shaped = contract_cols(back_logits, w_router)
    taken_index = jnp.maximum(filler - 1, 0)
    slot_gate = jnp.where(filler > 0, gate_weights.reshape(-1)[taken_index], 0.0)
    back_result = (slot_gate[:, None] * flowing[taken_index // top_count]).astype(jnp.bfloat16)
    back_arrived = send_rows(back_result.reshape(expert_count, capacity, model_width)).reshape(
        arrived.shape
    )
    back_hidden = jnp.einsum(
        "secd,efd->secf", back_arrived, w_down, preferred_element_type=jnp.float32
    )
    grad_down = jnp.einsum(
        "secf,secd->efd", hidden, back_arrived, preferred_element_type=jnp.float32
    )
    sigmoid_gate = jax.nn.sigmoid(gate_act)
    back_gate = (
        back_hidden * up_act * sigmoid_gate * (1.0 + gate_act * (1.0 - sigmoid_gate))
    ).astype(jnp.bfloat16)
    back_up = (back_hidden * jax.nn.silu(gate_act)).astype(jnp.bfloat16)
    grad_gate = jnp.einsum("secd,secf->edf", arrived, back_gate, preferred_element_type=jnp.float32)
    grad_up = jnp.einsum("secd,secf->edf", arrived, back_up, preferred_element_type=jnp.float32)
    back_rows = jnp.einsum("secf,edf->secd", back_gate, w_gate, preferred_element_type=jnp.float32)
    back_rows = back_rows + jnp.einsum(
        "secf,edf->secd", back_up, w_up, preferred_element_type=jnp.float32
    )
    returned = return_rows(back_rows.reshape(-1, back_rows.shape[2], model_width))
    gathered = returned.reshape(expert_count * capacity, model_width)[position].reshape(
        row_count, top_count, model_width
    )
    back_shaped = back_shaped + jnp.sum(gathered.astype(jnp.float32), axis=1)
    second_inverse, second_unit, second_scaled = norm_parts(middle, gain_moe)
    back_norm_two, grad_gain_moe = norm_back(back_shaped, second_inverse, second_unit, gain_moe)
    back_middle = flowing + back_norm_two
    back_branch = back_middle.astype(jnp.bfloat16)
    grad_out = contract_rows(attended, back_branch)
    back_attended = (
        contract_cols(back_branch, w_out)
        .astype(jnp.bfloat16)
        .reshape(row_count, groups, sharing, HEAD_DIM)
    )
    scores = score_table(queries, key_rows, document)
    probability = jnp.exp(scores - log_total)
    back_probs = jnp.einsum(
        "qkgd,pkd->kgqp", back_attended, value_rows, preferred_element_type=jnp.float32
    )
    back_values = jnp.einsum(
        "kgqp,qkgd->pkd",
        probability.astype(jnp.bfloat16),
        back_attended,
        preferred_element_type=jnp.float32,
    )
    row_delta = jnp.sum(back_probs * probability, axis=-1, keepdims=True)
    back_scores = (probability * (back_probs - row_delta)).astype(jnp.bfloat16)
    scale_factor = HEAD_DIM ** (-0.5)
    back_queries = (
        jnp.einsum("kgqp,pkd->qkgd", back_scores, key_rows, preferred_element_type=jnp.float32)
        * scale_factor
    )
    back_keys = (
        jnp.einsum("kgqp,qkgd->pkd", back_scores, queries, preferred_element_type=jnp.float32)
        * scale_factor
    )
    cosine_table, sine_table = rope_tables(document)
    back_queries = (
        rotate_back(back_queries, cosine_table[:, None, None, :], sine_table[:, None, None, :])
        .reshape(row_count, -1)
        .astype(jnp.bfloat16)
    )
    back_keys = (
        rotate_back(back_keys, cosine_table[:, None, :], sine_table[:, None, :])
        .reshape(row_count, -1)
        .astype(jnp.bfloat16)
    )
    back_values = back_values.reshape(row_count, -1).astype(jnp.bfloat16)
    level_rows = entry_rows.astype(jnp.float32)
    first_inverse, first_unit, first_scaled = norm_parts(level_rows, gain_attn)
    normed = first_scaled.astype(jnp.bfloat16)
    grad_query = contract_rows(normed, back_queries)
    grad_key = contract_rows(normed, back_keys)
    grad_value = contract_rows(normed, back_values)
    back_normed = (
        contract_cols(back_queries, w_query)
        + contract_cols(back_keys, w_key)
        + contract_cols(back_values, w_value)
    )
    back_normed = head_totals(back_normed)
    back_norm_one, grad_gain_attn = norm_back(back_normed, first_inverse, first_unit, gain_attn)
    back_input = back_middle + back_norm_one
    grads = (
        grad_gain_attn,
        grad_query,
        grad_key,
        grad_value,
        grad_out,
        grad_gain_moe,
        grad_router,
        grad_gate,
        grad_up,
        grad_down,
    )
    return (back_input.astype(jnp.bfloat16), grads)


def per_device(
    inputs,
    cotangent,
    documents,
    routes,
    gain_attn,
    w_query,
    w_key,
    w_value,
    w_out,
    gain_moe,
    w_router,
    w_gate,
    w_up,
    w_down,
):
    params = tuple(
        (
            piece_array[0]
            for piece_array in (
                gain_attn,
                w_query,
                w_key,
                w_value,
                w_out,
                gain_moe,
                w_router,
                w_gate,
                w_up,
                w_down,
            )
        )
    )
    whole_experts = side_by_side(
        (params[7], params[8], jnp.swapaxes(params[9], 1, 2)), "tensor", 2, 0
    )
    params = params[:7] + (whole_experts[0], whole_experts[1], jnp.swapaxes(whole_experts[2], 1, 2))
    section_index = lax.axis_index("section")
    micro_count = inputs.shape[0]
    doc_rows = documents[:, 0]
    activations = jnp.zeros_like(inputs)
    kept_states = []
    outgoing = None
    for tick_index in range(micro_count + 1):
        micro_index = tick_index - section_index
        valid_tick = (micro_index >= 0) & (micro_index < micro_count)
        picked_micro = jnp.clip(micro_index, 0, micro_count - 1)
        own_rows = lax.dynamic_index_in_dim(inputs, picked_micro, 0, keepdims=False)
        if outgoing is None:
            entry_rows = own_rows
        else:
            arriving = from_behind(outgoing, "section", 1)
            entry_rows = jnp.where(section_index == 0, own_rows, arriving)
        doc_now = lax.dynamic_index_in_dim(doc_rows, picked_micro, 0, keepdims=False)
        route_now = lax.dynamic_index_in_dim(routes, picked_micro, 0, keepdims=False)
        layer_out, saved = forward_layer(entry_rows, doc_now, route_now, params)
        previous = lax.dynamic_index_in_dim(activations, picked_micro, 0, keepdims=False)
        activations = lax.dynamic_update_index_in_dim(
            activations, jnp.where(valid_tick, layer_out, previous), picked_micro, 0
        )
        kept_states.append(saved)
        outgoing = layer_out
    stored = tuple(
        (
            jnp.stack([state[number] for state in kept_states])
            for number in range(len(kept_states[0]))
        )
    )
    grad_totals = tuple((jnp.zeros(piece_array.shape, jnp.float32) for piece_array in params))
    input_grads = jnp.zeros_like(cotangent)
    outgoing = None
    for tick_index in range(micro_count + 1):
        micro_index = tick_index - 1 + section_index
        valid_tick = (micro_index >= 0) & (micro_index < micro_count)
        picked_micro = jnp.clip(micro_index, 0, micro_count - 1)
        own_rows = lax.dynamic_index_in_dim(cotangent, picked_micro, 0, keepdims=False)
        if outgoing is None:
            entry_rows = own_rows
        else:
            arriving = from_behind(outgoing, "section", -1)
            entry_rows = jnp.where(section_index == 1, own_rows, arriving)
        doc_now = lax.dynamic_index_in_dim(doc_rows, picked_micro, 0, keepdims=False)
        route_now = lax.dynamic_index_in_dim(routes, picked_micro, 0, keepdims=False)
        state_tick = jnp.clip(micro_index + section_index, 0, micro_count)
        saved = tuple(
            (
                lax.dynamic_index_in_dim(stacked_state, state_tick, 0, keepdims=False)
                for stacked_state in stored
            )
        )
        back_input, grad_parts = backward_layer(entry_rows, saved, doc_now, route_now, params)
        previous = lax.dynamic_index_in_dim(input_grads, picked_micro, 0, keepdims=False)
        input_grads = lax.dynamic_update_index_in_dim(
            input_grads, jnp.where(valid_tick, back_input, previous), picked_micro, 0
        )
        grad_totals = tuple(
            (
                running + jnp.where(valid_tick, part_grad, 0.0)
                for running, part_grad in zip(grad_totals, grad_parts)
            )
        )
        outgoing = back_input
    shared_totals = (
        lax.psum(grad_totals[0].astype(jnp.bfloat16), "expert").astype(jnp.float32),
        lax.psum(grad_totals[1].astype(jnp.bfloat16), "expert").astype(jnp.float32),
        lax.psum(grad_totals[2].astype(jnp.bfloat16), "expert").astype(jnp.float32),
        lax.psum(grad_totals[3].astype(jnp.bfloat16), "expert").astype(jnp.float32),
        lax.psum(grad_totals[4].astype(jnp.bfloat16), "expert").astype(jnp.float32),
        lax.psum(grad_totals[5].astype(jnp.bfloat16), "expert").astype(jnp.float32),
        lax.psum(grad_totals[6].astype(jnp.bfloat16), "expert").astype(jnp.float32),
    )
    summed_experts = side_by_side_2(
        (
            grad_totals[7].astype(jnp.bfloat16),
            grad_totals[8].astype(jnp.bfloat16),
            jnp.swapaxes(grad_totals[9], 1, 2).astype(jnp.bfloat16),
        ),
        "tensor",
        2,
        0,
    )
    expert_grads = (summed_experts[0], summed_experts[1], jnp.swapaxes(summed_experts[2], 1, 2))
    return (
        activations[None],
        input_grads[None],
        shared_totals[0][None],
        shared_totals[1][None],
        shared_totals[2][None],
        shared_totals[3][None],
        shared_totals[4][None],
        shared_totals[5][None],
        shared_totals[6][None],
        expert_grads[0][None],
        expert_grads[1][None],
        expert_grads[2][None],
    )


def solution(mesh):
    in_specs = (
        P(None, "expert", None),
        P(None, "expert", None),
        P(None, "expert", None),
        P(None, "expert", None),
        P("section", None),
        P("section", None, "tensor"),
        P("section", None, "tensor"),
        P("section", None, "tensor"),
        P("section", "tensor", None),
        P("section", None),
        P("section", None, None),
        P("section", "expert", None, "tensor"),
        P("section", "expert", None, "tensor"),
        P("section", "expert", "tensor", None),
    )
    out_specs = (
        P("section", None, "expert", None),
        P("section", None, "expert", None),
        P("section", None),
        P("section", None, "tensor"),
        P("section", None, "tensor"),
        P("section", None, "tensor"),
        P("section", "tensor", None),
        P("section", None),
        P("section", None, None),
        P("section", "expert", None, "tensor"),
        P("section", "expert", None, "tensor"),
        P("section", "expert", "tensor", None),
    )
    return jax.shard_map(
        per_device, mesh=mesh, in_specs=in_specs, out_specs=out_specs, check_vma=False
    )
```

profile of v0, /device:TPU:0, one launch (start us, length us, event | category | flops | bytes accessed | tf_op | source)
XLA Modules:
  0.0 1323.8 jit_solution(2205495718040844706)
XLA Ops:
  43.8 22.2 %all-to-all-done = bf16[4,128,1536]{2,1,0:T(8,128)(2,1)} async-done(((bf16[4,128,1536]{2,1,0:T(8,128)(2,1)}), bf16[4,128,1536]{2,1,0:T(8,128)(2,1)}, u32[]{:S(2)}, u32[]{:S(2)}) %all-to-all-start) | async-done | bytes 1572896 | tf_op jit(solution)/shard_map/all_to_all | solution.py:18
  76.7 30.1 %all_to_all.95 = bf16[32,12,1536]{2,1,0:T(8,128)(2,1)} all-to-all(bf16[32,12,1536]{2,1,0:T(8,128)(2,1)S(1)} %dynamic-slice_select_fusion.2), channel_id=1, replica_groups=mesh['section'=2,'expert'=16,'tensor'=4] {'expert'}, dimensions={0} | all-to-all | bytes 2359296 | tf_op jit(solution)/shard_map/all_to_all | solution.py:132
  106.8 21.0 %all-gather.8.cloned.1.call-done = bf16[6,1536,512]{2,1,0:T(8,128)(2,1)} async-done(((bf16[6,1536,128]{2,1,0:T(8,128)(2,1)}), bf16[6,1536,512]{2,1,0:T(8,128)(2,1)}) %all-gather.8.cloned.1.call-update) | async-done | bytes 9437200 | tf_op jit(solution)/shard_map/all_gather | solution.py:29
  137.1 28.7 %all_to_all.96 = bf16[32,12,1536]{2,1,0:T(8,128)(2,1)S(1)} all-to-all(bf16[32,12,1536]{2,1,0:T(8,128)(2,1)S(1)} %bitcast.1220), channel_id=1, replica_groups=mesh['section'=2,'expert'=16,'tensor'=4] {'expert'}, dimensions={0} | all-to-all | bytes 2359296 | tf_op jit(solution)/shard_map/all_to_all | solution.py:138
  171.6 45.5 %all-gather.10.cloned.1.call-done = bf16[32,48,1536]{2,0,1:T(8,128)(2,1)} async-done(((bf16[32,12,1536]{2,0,1:T(8,128)(2,1)}), bf16[32,48,1536]{2,0,1:T(8,128)(2,1)}) %all-gather.10.cloned.1.call-update) | async-done | bytes 4718608 | tf_op jit(solution)/shard_map/all_gather | solution.py:139
  224.1 10.2 gather_fusion.1
  242.0 15.7 %reduce-window.26 = s32[32,8,128]{2,1,0:T(8,128)S(1)} reduce-window(s32[32,8,128]{2,1,0:T(8,128)} %fusion.308, s32[]{:T(128)} %constant.348.clone.1), window={size=1x1x128 pad=0_0x0_0x127_0}, to_apply=%region_37.38 | reduce-window | flops 4161536 | bytes 262148 | tf_op jit(solution)/shard_map/reduce-window.4
  290.5 14.1 %all-to-all-done.3 = bf16[4,128,1536]{2,1,0:T(8,128)(2,1)} async-done(((bf16[4,128,1536]{2,1,0:T(8,128)(2,1)}), bf16[4,128,1536]{2,1,0:T(8,128)(2,1)}, u32[]{:S(2)}, u32[]{:S(2)}) %all-to-all-start.3) | async-done | bytes 1572896 | tf_op jit(solution)/shard_map/all_to_all | solution.py:18
  316.8 28.2 %all_to_all.97 = bf16[32,12,1536]{2,1,0:T(8,128)(2,1)S(1)} all-to-all(bf16[32,12,1536]{2,1,0:T(8,128)(2,1)S(1)} %dynamic-slice_select_fusion.1), channel_id=1, replica_groups=mesh['section'=2,'expert'=16,'tensor'=4] {'expert'}, dimensions={0} | all-to-all | bytes 2359296 | tf_op jit(solution)/shard_map/all_to_all | solution.py:132
  352.7 23.5 %all_to_all.98 = bf16[32,12,1536]{2,1,0:T(8,128)(2,1)S(1)} all-to-all(bf16[32,12,1536]{2,1,0:T(8,128)(2,1)S(1)} %bitcast.1221), channel_id=1, replica_groups=mesh['section'=2,'expert'=16,'tensor'=4] {'expert'}, dimensions={0} | all-to-all | bytes 2359296 | tf_op jit(solution)/shard_map/all_to_all | solution.py:138
  388.4 38.4 %all-gather.12.cloned.1.call-done = bf16[32,48,1536]{2,0,1:T(8,128)(2,1)} async-done(((bf16[32,12,1536]{2,0,1:T(8,128)(2,1)}), bf16[32,48,1536]{2,0,1:T(8,128)(2,1)}) %all-gather.12.cloned.1.call-update) | async-done | bytes 4718608 | tf_op jit(solution)/shard_map/all_gather | solution.py:139
  433.8 10.2 gather_fusion.3
  470.7 12.3 all-to-all-done.6
  516.6 11.6 all-to-all-done.7
  543.8 9.3 all-to-all-done.9
  564.2 24.6 %all_to_all.99 = bf16[32,12,1536]{2,1,0:T(8,128)(2,1)S(1)} all-to-all(bf16[32,12,1536]{2,1,0:T(8,128)(2,1)S(1)} %bitcast.1222), channel_id=1, replica_groups=mesh['section'=2,'expert'=16,'tensor'=4] {'expert'}, dimensions={0} | all-to-all | bytes 2359296 | tf_op jit(solution)/shard_map/all_to_all | solution.py:138
  594.3 24.2 %all_to_all.100 = bf16[32,12,1536]{2,1,0:T(8,128)(2,1)S(1)} all-to-all(bf16[32,12,1536]{2,1,0:T(8,128)(2,1)S(1)} %bitcast.1223), channel_id=1, replica_groups=mesh['section'=2,'expert'=16,'tensor'=4] {'expert'}, dimensions={0} | all-to-all | bytes 2359296 | tf_op jit(solution)/shard_map/all_to_all | solution.py:138
  646.4 10.2 gather_fusion.8
  660.6 33.9 %all-gather.14.cloned.1.call-done = bf16[32,48,1536]{2,0,1:T(8,128)(2,1)} async-done(((bf16[32,12,1536]{2,0,1:T(8,128)(2,1)}), bf16[32,48,1536]{2,0,1:T(8,128)(2,1)}) %all-gather.14.cloned.1.call-update) | async-done | bytes 4718608 | tf_op jit(solution)/shard_map/all_gather | solution.py:139
  701.5 10.4 gather_fusion.5
  740.3 19.0 %all-to-all-done.11 = bf16[4,128,1536]{2,1,0:T(8,128)(2,1)} async-done(((bf16[4,128,1536]{2,1,0:T(8,128)(2,1)}), bf16[4,128,1536]{2,1,0:T(8,128)(2,1)}, u32[]{:S(2)}, u32[]{:S(2)}) %all-to-all-start.11) | async-done | bytes 1572896 | tf_op jit(solution)/shard_map/all_to_all | solution.py:18
  783.5 30.5 %all_to_all.101 = bf16[32,12,1536]{2,1,0:T(8,128)(2,1)S(1)} all-to-all(bf16[32,12,1536]{2,1,0:T(8,128)(2,1)S(1)} %fusion.16), channel_id=1, replica_groups=mesh['section'=2,'expert'=16,'tensor'=4] {'expert'}, dimensions={0} | all-to-all | bytes 2359296 | tf_op jit(solution)/shard_map/all_to_all | solution.py:132
  821.6 26.0 %all_to_all.102 = bf16[32,12,1536]{2,1,0:T(8,128)(2,1)S(1)} all-to-all(bf16[32,12,1536]{2,1,0:T(8,128)(2,1)S(1)} %bitcast.1224), channel_id=1, replica_groups=mesh['section'=2,'expert'=16,'tensor'=4] {'expert'}, dimensions={0} | all-to-all | bytes 2359296 | tf_op jit(solution)/shard_map/all_to_all | solution.py:138
  866.2 9.5 gather_fusion.12
  886.2 11.8 all-gather.18.cloned.1.call-done
  905.2 10.6 gather_fusion.11
  948.2 9.1 all-to-all-done.14
  996.1 13.3 %all-to-all-done.15 = bf16[32,12,1536]{2,1,0:T(8,128)(2,1)} async-done(((bf16[32,12,1536]{2,1,0:T(8,128)(2,1)}), bf16[32,12,1536]{2,1,0:T(8,128)(2,1)}, u32[]{:S(2)}, u32[]{:S(2)}) %all-to-all-start.15) | async-done | bytes 1179680 | tf_op jit(solution)/shard_map/all_to_all | solution.py:132
  1034.8 16.1 %all-to-all-done.16 = bf16[32,12,1536]{2,1,0:T(8,128)(2,1)} async-done(((bf16[32,12,1536]{2,1,0:T(8,128)(2,1)}), bf16[32,12,1536]{2,1,0:T(8,128)(2,1)}, u32[]{:S(2)}, u32[]{:S(2)}) %all-to-all-start.16) | async-done | bytes 1179680 | tf_op jit(solution)/shard_map/all_to_all | solution.py:138
  1119.1 10.4 gather_fusion.14
  1154.8 53.2 %all-to-all-done.18 = bf16[4,6,1536,128]{2,3,1,0:T(8,128)(2,1)} async-done(((bf16[4,6,1536,128]{2,3,1,0:T(8,128)(2,1)}), bf16[4,6,1536,128]{2,3,1,0:T(8,128)(2,1)}, u32[]{:S(2)}, u32[]{:S(2)}) %all-to-all-start.18) | async-done | bytes 9437216 | tf_op jit(solution)/shard_map/all_to_all | solution.py:46
  1233.9 72.1 %all-reduce = (bf16[1,1536]{1,0:T(2,128)(2,1)S(1)}, bf16[1,1536]{1,0:T(2,128)(2,1)S(1)}) all-reduce(bf16[1,1536]{1,0:T(2,128)(2,1)S(1)} %broadcast_in_dim.437, bf16[1,1536]{1,0:T(2,128)(2,1)S(1)} %broadcast_in_dim.450), channel_id=1, replica_groups=mesh['section'=2,'expert'=16,'tensor'=4] {'expert'}, use_global_device_ids=true, to_apply=%region_78.79 | all-reduce | flops 3072 | bytes 12288 | tf_op jit(solution)/shard_map/psum | solution.py:491
  (1083 shorter events, 599.0 us)
Async XLA Ops:
  7.2 120.6 %all-gather.8.cloned.1.call-start = ((), (), s32[]{:S(2)}) async-start(), calls=%async_computation.19 | async-start | bytes 11796480 | tf_op jit(solution)/shard_map/all_gather | solution.py:29
  16.6 222.5 %copy-start.9 = (bf16[1,128,1536]{2,1,0:T(8,128)(2,1)}, bf16[1,128,1536]{2,1,0:T(8,128)(2,1)S(1)}, u32[]{:S(2)}) copy-start(bf16[1,128,1536]{2,1,0:T(8,128)(2,1)S(1)} %get-tuple-element.87) | copy-start | bytes 1179652
  22.9 43.0 %all-to-all-start = ((bf16[4,128,1536]{2,1,0:T(8,128)(2,1)}), bf16[4,128,1536]{2,1,0:T(8,128)(2,1)}, u32[]{:S(2)}, u32[]{:S(2)}) async-start(bf16[4,128,1536]{2,1,0:T(8,128)(2,1)} %broadcast_in_dim.209), calls=%async_computation | async-start | bytes 3145728 | tf_op jit(solution)/shard_map/all_to_all | solution.py:18
  27.5 189.6 %all-gather.10.cloned.1.call-start = ((), (), s32[]{:S(2)}) async-start(), calls=%async_computation.20 | async-start | bytes 5898240 | tf_op jit(solution)/shard_map/all_gather | solution.py:139
  167.6 56.5 %copy-start.120 = (s32[1,128,8]{2,1,0:T(8,128)}, s32[1,128,8]{2,1,0:T(8,128)S(1)}, u32[]{:S(2)}) copy-start(s32[1,128,8]{2,1,0:T(8,128)S(1)} %copy.682) | copy-start | bytes 12292
  167.8 56.3 %copy-start.122 = (s32[1,128,8]{2,1,0:T(8,128)}, s32[1,128,8]{2,1,0:T(8,128)S(1)}, u32[]{:S(2)}) copy-start(s32[1,128,8]{2,1,0:T(8,128)S(1)} %copy.668) | copy-start | bytes 12292
  171.0 53.2 %copy-start.270 = (f32[128]{0:T(128)}, f32[128]{0:T(128)S(1)}, u32[]{:S(2)}) copy-start(f32[128]{0:T(128)S(1)} %reduce_max.55) | copy-start | bytes 1540
  171.5 52.6 %copy-start.278 = (f32[128]{0:T(128)}, f32[128]{0:T(128)S(1)}, u32[]{:S(2)}) copy-start(f32[128]{0:T(128)S(1)} %fusion.446) | copy-start | bytes 1540
  240.1 33.5 %collective-permute-start = (bf16[128,1536]{1,0:T(8,128)(2,1)}, bf16[128,1536]{1,0:T(8,128)(2,1)S(1)}, u32[]{:S(2)}, u32[]{:S(2)}) collective-permute-start(bf16[128,1536]{1,0:T(8,128)(2,1)} %add_convert_fusion.2), channel_id=1, source_target_pairs={{0,64},{1,65},{2,66},{3,67},{4,68},{5,69},{6,70},{7,71},{8,72},{9,... | collective-permute-start | bytes 1179656 | tf_op jit(solution)/shard_map/ppermute | solution.py:36
  274.8 174.1 %copy-start.18 = (bf16[128,1536]{1,0:T(8,128)(2,1)}, bf16[128,1536]{1,0:T(8,128)(2,1)S(1)}, u32[]{:S(2)}) copy-start(bf16[128,1536]{1,0:T(8,128)(2,1)S(1)} %get-tuple-element.81) | copy-start | bytes 1179652
  279.5 25.1 %all-to-all-start.3 = ((bf16[4,128,1536]{2,1,0:T(8,128)(2,1)}), bf16[4,128,1536]{2,1,0:T(8,128)(2,1)}, u32[]{:S(2)}, u32[]{:S(2)}) async-start(bf16[4,128,1536]{2,1,0:T(8,128)(2,1)} %broadcast_in_dim.215), calls=%async_computation.3 | async-start | bytes 3145728 | tf_op jit(solution)/shard_map/all_to_all | solution.py:18
  284.0 142.8 %all-gather.12.cloned.1.call-start = ((), (), s32[]{:S(2)}) async-start(), calls=%async_computation.21 | async-start | bytes 5898240 | tf_op jit(solution)/shard_map/all_gather | solution.py:139
  308.2 79.7 %copy-start.1 = (bf16[128,1536]{1,0:T(8,128)(2,1)}, bf16[128,1536]{1,0:T(8,128)(2,1)S(1)}, u32[]{:S(2)}) copy-start(bf16[128,1536]{1,0:T(8,128)(2,1)S(1)} %get-tuple-element.101) | copy-start | bytes 1179652
  384.0 49.8 %copy-start.176 = (s32[1536]{0:T(1024)}, s32[1536]{0:T(1024)S(1)}, u32[]{:S(2)}) copy-start(s32[1536]{0:T(1024)S(1)} %scatter_custom_fusion.2) | copy-start | bytes 18436
  388.2 45.6 %copy-start.184 = (f32[128,8]{0,1:T(8,128)}, f32[128,8]{0,1:T(8,128)S(1)}, u32[]{:S(2)}) copy-start(f32[128,8]{0,1:T(8,128)S(1)} %select_reduce_fusion.4) | copy-start | bytes 12292
  449.3 3.3 collective-permute-start.1
  456.9 26.1 %all-to-all-start.6 = ((bf16[4,128,1536]{2,1,0:T(8,128)(2,1)}), bf16[4,128,1536]{2,1,0:T(8,128)(2,1)}, u32[]{:S(2)}, u32[]{:S(2)}) async-start(bf16[4,128,1536]{2,1,0:T(8,128)(2,1)} %broadcast_in_dim.222), calls=%async_computation.6 | async-start | bytes 3145728 | tf_op jit(solution)/shard_map/all_to_all | solution.py:18
  497.6 30.6 %all-to-all-start.7 = ((bf16[32,12,1536]{2,1,0:T(8,128)(2,1)}), bf16[32,12,1536]{2,1,0:T(8,128)(2,1)}, u32[]{:S(2)}, u32[]{:S(2)}) async-start(bf16[32,12,1536]{2,1,0:T(8,128)(2,1)} %dynamic-slice_select_fusion), calls=%async_computation.7 | async-start | bytes 3145728 | tf_op jit(solution)/shard_map/all_to_all | solution.py:132
  528.2 24.9 %all-to-all-start.9 = ((bf16[32,12,1536]{2,1,0:T(8,128)(2,1)}), bf16[32,12,1536]{2,1,0:T(8,128)(2,1)}, u32[]{:S(2)}, u32[]{:S(2)}) async-start(bf16[32,12,1536]{2,1,0:T(8,128)(2,1)} %fusion.17), calls=%async_computation.9 | async-start | bytes 3145728 | tf_op jit(solution)/shard_map/all_to_all | solution.py:132
  532.6 106.7 %all-gather.16.cloned.1.call-start = ((), (), s32[]{:S(2)}) async-start(), calls=%async_computation.23 | async-start | bytes 5898240 | tf_op jit(solution)/shard_map/all_gather | solution.py:139
  590.5 104.0 %all-gather.14.cloned.1.call-start = ((), (), s32[]{:S(2)}) async-start(), calls=%async_computation.22 | async-start | bytes 5898240 | tf_op jit(solution)/shard_map/all_gather | solution.py:139
  734.0 25.4 %all-to-all-start.11 = ((bf16[4,128,1536]{2,1,0:T(8,128)(2,1)}), bf16[4,128,1536]{2,1,0:T(8,128)(2,1)}, u32[]{:S(2)}, u32[]{:S(2)}) async-start(bf16[4,128,1536]{2,1,0:T(8,128)(2,1)} %broadcast_in_dim.229), calls=%async_computation.11 | async-start | bytes 3145728 | tf_op jit(solution)/shard_map/all_to_all | solution.py:18
  738.3 159.7 %all-gather.18.cloned.1.call-start = ((), (), s32[]{:S(2)}) async-start(), calls=%async_computation.24 | async-start | bytes 5898240 | tf_op jit(solution)/shard_map/all_gather | solution.py:139
  764.3 8.3 collective-permute-start.2
  931.9 25.4 %all-to-all-start.14 = ((bf16[4,128,1536]{2,1,0:T(8,128)(2,1)}), bf16[4,128,1536]{2,1,0:T(8,128)(2,1)}, u32[]{:S(2)}, u32[]{:S(2)}) async-start(bf16[4,128,1536]{2,1,0:T(8,128)(2,1)} %broadcast_in_dim.430), calls=%async_computation.14 | async-start | bytes 3145728 | tf_op jit(solution)/shard_map/all_to_all | solution.py:18
  961.3 5.0 collective-permute-start.3
  977.2 32.2 %all-to-all-start.15 = ((bf16[32,12,1536]{2,1,0:T(8,128)(2,1)}), bf16[32,12,1536]{2,1,0:T(8,128)(2,1)}, u32[]{:S(2)}, u32[]{:S(2)}) async-start(bf16[32,12,1536]{2,1,0:T(8,128)(2,1)} %fusion.15), calls=%async_computation.15 | async-start | bytes 3145728 | tf_op jit(solution)/shard_map/all_to_all | solution.py:132
  1021.6 29.3 %all-to-all-start.16 = ((bf16[32,12,1536]{2,1,0:T(8,128)(2,1)}), bf16[32,12,1536]{2,1,0:T(8,128)(2,1)}, u32[]{:S(2)}, u32[]{:S(2)}) async-start(bf16[32,12,1536]{2,1,0:T(8,128)(2,1)} %bitcast.1219), calls=%async_computation.16 | async-start | bytes 3145728 | tf_op jit(solution)/shard_map/all_to_all | solution.py:138
  1026.9 85.2 %all-gather.20.cloned.1.call-start = ((), (), s32[]{:S(2)}) async-start(), calls=%async_computation.25 | async-start | bytes 5898240 | tf_op jit(solution)/shard_map/all_gather | solution.py:139
  1099.7 108.2 %all-to-all-start.18 = ((bf16[4,6,1536,128]{2,3,1,0:T(8,128)(2,1)}), bf16[4,6,1536,128]{2,3,1,0:T(8,128)(2,1)}, u32[]{:S(2)}, u32[]{:S(2)}) async-start(bf16[4,6,1536,128]{2,3,1,0:T(8,128)(2,1)} %bitcast.1187), calls=%async_computation.18 | async-start | bytes 18874368 | tf_op jit(solution)/shard_map/all_to_all | solution.py:46
  1105.5 203.9 %all-reduce.4.cloned.1.call-start = ((), (), s32[]{:S(2)}) async-start(), calls=%async_computation.26 | async-start | bytes 6488064 | tf_op jit(solution)/shard_map/psum | solution.py:492
  1209.2 21.6 %all-to-all-start.17 = ((bf16[4,128,1536]{2,1,0:T(8,128)(2,1)}), bf16[4,128,1536]{2,1,0:T(8,128)(2,1)}, u32[]{:S(2)}, u32[]{:S(2)}) async-start(bf16[4,128,1536]{2,1,0:T(8,128)(2,1)} %broadcast_in_dim.434), calls=%async_computation.17 | async-start | bytes 3145728 | tf_op jit(solution)/shard_map/all_to_all | solution.py:18
  (292 other events, 1610.9 us)
Sparse Core Ops, SparseCore 0:
  12.0 115.7 all-gather.7
  167.6 49.4 all-gather.9
  378.0 48.6 all-gather.11
  590.7 48.6 all-gather.15
  641.4 53.0 all-gather.13
  849.5 48.4 all-gather.17
  1054.2 48.4 all-gather.19
  1151.6 96.2 all-reduce.3
where the time goes:
time: 1340 us; the launch traced here: 1320 us
  waiting for transfers between devices  335 us (25%)
  local copies, waits for them, and re-layouts  292 us (22%)
  blocking collectives  288 us (21%)
  other arithmetic  186 us (14%)
  matrix products  142 us (11%)
  starting transfers between devices  63.1 us (5%)
  between operations  18.6 us (1%)
    all_gather x6, waiting for transfers between devices, return_rows(): return lax.all_gather(moved_rows, 'tensor', axis=1, tiled=True)  130 us
    all_to_all x5, blocking collectives, return_rows(): lax.all_to_all(reduced, 'expert', split_axis=0, concat_axis=0, tiled=True)  127 us
    all_to_all x3, blocking collectives, send_rows(): lax.all_to_all(own_share, 'expert', split_axis=0, concat_axis=0, tiled=True)  88.7 us
    all_to_all x6, waiting for transfers between devices, copy_for_each(): return lax.all_to_all(copies, axis, split_axis=0, concat_axis=0, tiled=True)  79.7 us
    psum x1, blocking collectives, per_device(): lax.psum(grad_totals[0].astype(jnp.bfloat16), 'expert').astype(jnp.float32)  72.1 us
    all_to_all x1, waiting for transfers between devices, summed_on_arrival(): lax.all_to_all(in_blocks(array, dim, length), axis, 0, 0, tiled=True)  53.2 us
    all_gather x6, local copies, waits for them, and re-layouts, return_rows(): return lax.all_gather(moved_rows, 'tensor', axis=1, tiled=True)  42.3 us
    another operation x9, other arithmetic  36.8 us
  transfers between devices with their start and end apart: 23, of which 18 were waited for; matrix products, arithmetic and copies ran while one was open for 27% of the time, Pallas kernels for 0%

commit v1 on v0

v1 whole, which is shorter than its diff:
```python
import math

import jax
import jax.numpy as jnp
from jax import lax
from jax.sharding import PartitionSpec as P

HEADS = 24
KV_HEADS = 8
HEAD_DIM = 64
EPSILON = 1e-06
BF = jnp.bfloat16
F32 = jnp.float32


def shifted(array, axis, by):
    length = lax.axis_size(axis)
    return lax.ppermute(array, axis, [(i, (i + by) % length) for i in range(length)])


def sibling(array):
    return shifted(array, "section", 1)


def gather_x(block):
    ahead = {k: shifted(block, "tensor", -k) for k in (1, 3, 2)}
    return [block, ahead[1], ahead[2], ahead[3]]


def gather_x_ring(block, dim):
    one, three = shifted(block, "tensor", -1), shifted(block, "tensor", 1)
    half = block.shape[dim] // 2
    low = shifted(lax.slice_in_dim(one, 0, half, axis=dim), "tensor", -1)
    high = shifted(lax.slice_in_dim(three, half, 2 * half, axis=dim), "tensor", 1)
    return [block, one, jnp.concatenate([low, high], dim), three]


def scatter_x(blocks):
    total = blocks[0].astype(F32)
    for k in (1, 3, 2):
        total = total + shifted(blocks[k].astype(BF), "tensor", k).astype(F32)
    return total


def spread_e(block):
    copies = jnp.broadcast_to(block[None], (lax.axis_size("expert"), *block.shape))
    return lax.all_to_all(copies, "expert", 0, 0, tiled=True)


def collect_e(blocks):
    pieces = lax.all_to_all(blocks, "expert", 0, 0, tiled=True)
    return jnp.sum(pieces.astype(F32), axis=0)


def rotate_half(values, cosine_table, sine_table):
    middle_at = values.shape[-1] // 2
    turned = jnp.concatenate([-values[..., middle_at:], values[..., :middle_at]], axis=-1)
    return values * cosine_table + turned * sine_table


def rotate_back(values, cosine_table, sine_table):
    middle_at = values.shape[-1] // 2
    scaled = values * sine_table
    return values * cosine_table + jnp.concatenate(
        [scaled[..., middle_at:], -scaled[..., :middle_at]], axis=-1
    )


def rope_tables(document, places):
    starts = jnp.sum((document[None, :] < document[:, None]).astype(jnp.int32), axis=1)
    offsets = (places - starts).astype(F32)
    frequency = jnp.exp(
        jnp.arange(HEAD_DIM // 2, dtype=F32) * (-2.0 * math.log(10000.0) / HEAD_DIM)
    )
    angle_table = offsets[:, None] * frequency[None, :]
    angle_table = jnp.concatenate([angle_table, angle_table], axis=-1)
    return (jnp.cos(angle_table), jnp.sin(angle_table))


def norm_parts(level_rows, gain):
    inverse = lax.rsqrt(jnp.mean(level_rows * level_rows, axis=-1, keepdims=True) + EPSILON)
    unit_rows = level_rows * inverse
    return (inverse, unit_rows, unit_rows * gain.astype(F32))


def norm_back(back_scaled, inverse, unit_rows, gain):
    back_unit = back_scaled * gain.astype(F32)
    back_level = inverse * (
        back_unit - unit_rows * jnp.mean(back_unit * unit_rows, axis=-1, keepdims=True)
    )
    return (back_level, jnp.sum(back_scaled * unit_rows, axis=0))


def dot(left, right):
    return jnp.dot(left, right, preferred_element_type=F32)


def contract_rows(left_rows, right_rows):
    return lax.dot_general(
        left_rows, right_rows, (((0,), (0,)), ((), ())), preferred_element_type=F32
    )


def contract_cols(left_rows, right_rows):
    return lax.dot_general(
        left_rows, right_rows, (((1,), (1,)), ((), ())), preferred_element_type=F32
    )


def score_table(queries, key_rows, allowed):
    raw_scores = jnp.einsum(
        "qkgd,pkd->kgqp", queries, key_rows, preferred_element_type=F32
    ) * HEAD_DIM ** (-0.5)
    return jnp.where(allowed[None, None], raw_scores, -1e30)


def attention_forward(entry, tables, allowed, w_qkv, w_out, gain):
    cosine_table, sine_table = tables
    rows = entry.shape[0]
    normed = norm_parts(entry.astype(F32), gain)[2].astype(BF)
    q_cols, kv_cols = w_out.shape[0], (w_qkv.shape[1] - w_out.shape[0]) // 2
    groups = kv_cols // HEAD_DIM
    raw = dot(normed, w_qkv)
    queries = rotate_half(
        raw[:, :q_cols].reshape(rows, groups, -1, HEAD_DIM),
        cosine_table[:, None, None, :],
        sine_table[:, None, None, :],
    ).astype(BF)
    keys = rotate_half(
        raw[:, q_cols : q_cols + kv_cols].reshape(rows, groups, HEAD_DIM),
        cosine_table[:, None, :],
        sine_table[:, None, :],
    ).astype(BF)
    values = raw[:, q_cols + kv_cols :].astype(BF).reshape(rows, groups, HEAD_DIM)
    scores = score_table(queries, keys, allowed)
    row_peak = jnp.max(scores, axis=-1, keepdims=True)
    exp_scores = jnp.exp(scores - row_peak)
    row_total = jnp.sum(exp_scores, axis=-1, keepdims=True)
    probability = exp_scores / row_total
    log_total = row_peak + jnp.log(row_total)
    attended = jnp.einsum(
        "kgqp,pkd->qkgd", probability.astype(BF), values, preferred_element_type=F32
    )
    attended = attended.astype(BF).reshape(rows, q_cols)
    partial = dot(attended, w_out)
    return partial, (normed, queries, keys, values, log_total, attended)


def attention_backward(back_branch, saved, tables, allowed, w_qkv, w_out):
    normed, queries, keys, values, log_total, attended = saved
    cosine_table, sine_table = tables
    rows = back_branch.shape[0]
    grad_out = contract_rows(attended, back_branch)
    back_attended = contract_cols(back_branch, w_out).astype(BF).reshape(queries.shape)
    scores = score_table(queries, keys, allowed)
    probability = jnp.exp(scores - log_total)
    back_probs = jnp.einsum("qkgd,pkd->kgqp", back_attended, values, preferred_element_type=F32)
    back_values = jnp.einsum(
        "kgqp,qkgd->pkd", probability.astype(BF), back_attended, preferred_element_type=F32
    )
    row_delta = jnp.sum(back_probs * probability, axis=-1, keepdims=True)
    back_scores = (probability * (back_probs - row_delta)).astype(BF)
    scale_factor = HEAD_DIM ** (-0.5)
    back_queries = (
        jnp.einsum("kgqp,pkd->qkgd", back_scores, keys, preferred_element_type=F32) * scale_factor
    )
    back_keys = (
        jnp.einsum("kgqp,qkgd->pkd", back_scores, queries, preferred_element_type=F32)
        * scale_factor
    )
    back_queries = rotate_back(
        back_queries, cosine_table[:, None, None, :], sine_table[:, None, None, :]
    ).reshape(rows, -1)
    back_keys = rotate_back(
        back_keys, cosine_table[:, None, :], sine_table[:, None, :]
    ).reshape(rows, -1)
    back_qkv = jnp.concatenate(
        [back_queries.astype(BF), back_keys.astype(BF), back_values.reshape(rows, -1).astype(BF)],
        axis=1,
    )
    grad_qkv = contract_rows(back_qkv, normed)
    partial = contract_cols(back_qkv, w_qkv)
    return partial, jnp.concatenate([grad_qkv, grad_out], axis=0)


def gate_table(rows, named, w_router, mine):
    logits = dot(rows, w_router)
    masked = jnp.where(named, logits, -1e30)
    peak = jnp.max(masked, axis=-1, keepdims=True)
    raised = jnp.where(named, jnp.exp(masked - peak), 0.0)
    gates = raised / jnp.sum(raised, axis=-1, keepdims=True)
    return jnp.einsum("re,ke->kr", gates, mine, precision=lax.Precision.HIGHEST)


def experts_forward(rows, gates, w_gu, w_down):
    total = 0.0
    kept = []
    for k in range(2):
        width = w_gu[k][0].shape[1] // 2
        for gate_up, down in zip(w_gu[k], w_down[k]):
            pre = dot(rows, gate_up)
            gate_act, up_act = pre[:, :width], pre[:, width:]
            hidden = (jax.nn.silu(gate_act) * up_act).astype(BF)
            kept.append((gate_act, up_act, hidden))
            total = total + gates[k][:, None] * dot(hidden, down)
    return total, kept


def experts_backward(rows, back, slope, gates, kept, w_gu, w_down):
    total = 0.0
    grads = []
    back_logits = []
    for k in range(2):
        kept_k = kept[4 * k : 4 * k + 4]
        raw = [contract_cols(back, down) for down in w_down[k]]
        back_gate = sum(
            jnp.sum(r * hidden.astype(F32), axis=1) for r, (_, _, hidden) in zip(raw, kept_k)
        )
        back_logits.append(gates[k] * (back_gate - slope))
        gate = gates[k][:, None]
        blocks = []
        for r, (gate_act, up_act, hidden), gate_up in zip(raw, kept_k, w_gu[k]):
            back_hidden = gate * r
            sigmoid = jax.nn.sigmoid(gate_act)
            back_pre = jnp.concatenate(
                [
                    (back_hidden * up_act * sigmoid * (1.0 + gate_act * (1.0 - sigmoid))).astype(BF),
                    (back_hidden * gate_act * sigmoid).astype(BF),
                ],
                axis=1,
            )
            total = total + contract_cols(back_pre, gate_up)
            grad_gu = contract_rows(rows, back_pre)
            grad_down = contract_rows((gate * hidden.astype(F32)).astype(BF), back)
            blocks.append((grad_gu, grad_down))
        grads.append(blocks)
    return total, grads, jnp.stack(back_logits)


def per_device(
    inputs,
    cotangent,
    documents,
    routes,
    gain_attn,
    w_query,
    w_key,
    w_value,
    w_out,
    gain_moe,
    w_router,
    w_gate,
    w_up,
    w_down,
):
    section = lax.axis_index("section")
    expert = lax.axis_index("expert")
    tensor = lax.axis_index("tensor")
    first = section == 0
    rows, width = inputs.shape[1:]
    own_rows = rows // 4
    expert_count = w_router.shape[2]

    def turned(array):
        array = lax.dynamic_index_in_dim(array, section, 0, keepdims=False)
        return jnp.roll(array, -own_rows * tensor, axis=0)

    def both_layers(own):
        other = sibling(own)
        return jnp.where(first, own, other), jnp.where(first, other, own)

    w_qkv = jnp.concatenate([w_query[0], w_key[0], w_value[0]], axis=1)
    w_qkvs = both_layers(w_qkv)
    w_outs = both_layers(w_out[0])
    small = jnp.concatenate([gain_attn, gain_moe, w_router[0].T], axis=0)
    smalls = both_layers(small)

    w_gu = jnp.concatenate([w_gate[0], w_up[0]], axis=2)
    quarter = []
    for array in (w_gu, w_down[0]):
        kept = lax.dynamic_index_in_dim(array, section, 0, keepdims=False)
        given = sibling(lax.dynamic_index_in_dim(array, 1 - section, 0, keepdims=False))
        quarter.append((jnp.where(first, kept, given), jnp.where(first, given, kept)))
    w_gus, w_downs = [], []
    for layer in range(2):
        mine = gather_x_ring(quarter[0][layer], 0)
        w_gus.append((mine, [sibling(block) for block in mine]))
        mine = gather_x_ring(quarter[1][layer], 0)
        w_downs.append((mine, [sibling(block) for block in mine]))

    places = (jnp.arange(rows, dtype=jnp.int32) + own_rows * tensor) % rows
    document = turned(documents[:, 0])
    allowed = (document[:, None] == document[None, :]) & (places[None, :] <= places[:, None])
    tables = rope_tables(document, places)
    names = spread_e(turned(routes)[:own_rows]).reshape(-1, routes.shape[2])
    named = jnp.any(
        names[:, :, None] == jnp.arange(expert_count, dtype=jnp.int32)[None, None, :], axis=1
    )
    mine = jnp.stack(
        [
            (jnp.arange(expert_count) == 2 * expert + section).astype(F32),
            (jnp.arange(expert_count) == 2 * expert + 1 - section).astype(F32),
        ]
    )

    state = []
    outputs = []
    entry = turned(inputs)
    for layer in range(2):
        gain_a, gain_m, router = smalls[layer][0], smalls[layer][1], smalls[layer][2:].T
        partial, attn_saved = attention_forward(
            entry, tables, allowed, w_qkvs[layer], w_outs[layer], gain_a
        )
        entry_own = entry[:own_rows].astype(F32)
        middle = entry_own + scatter_x([partial[own_rows * k : own_rows * (k + 1)] for k in range(4)])
        shaped = norm_parts(middle, gain_m)[2].astype(BF)
        arrived = spread_e(shaped).reshape(-1, width)
        gates = gate_table(arrived, named, router, mine)
        terms, kept = experts_forward(arrived, gates, w_gus[layer], w_downs[layer])
        moe = collect_e(terms.astype(BF).reshape(-1, own_rows, width))
        out_own = (middle + moe).astype(BF)
        entry_saved = entry_own
        entry = jnp.concatenate(gather_x(out_own), axis=0)
        outputs.append(entry)
        state.append((entry_saved, attn_saved, middle, arrived, gates, kept, moe))

    flow = turned(cotangent)[:own_rows]
    in_grads = [None, None]
    expert_grads = [None, None]
    packs = [None, None]
    small_grads = [None, None]
    for layer in (1, 0):
        gain_a, gain_m, router = smalls[layer][0], smalls[layer][1], smalls[layer][2:].T
        entry_own, attn_saved, middle, arrived, gates, kept, moe = state[layer]
        flowing = flow.astype(F32)
        slope = jnp.sum(flowing * moe, axis=-1, keepdims=True)
        slope_high = slope.astype(BF)
        slope_low = (slope - slope_high.astype(F32)).astype(BF)
        extra = jnp.concatenate(
            [slope_high, slope_low, jnp.zeros((own_rows, 126), BF)], axis=1
        )
        moved = spread_e(jnp.concatenate([flow, extra], axis=1)).reshape(-1, width + 128)
        back = moved[:, :width]
        slope_all = moved[:, width].astype(F32) + moved[:, width + 1].astype(F32)
        terms, grads, back_logits = experts_backward(
            arrived, back, slope_all, gates, kept, w_gus[layer], w_downs[layer]
        )
        back_table = dot(back_logits.T, mine).astype(BF)
        terms = terms + contract_cols(back_table, router)
        grad_router = contract_rows(back_table, arrived)
        back_shaped = collect_e(terms.astype(BF).reshape(-1, own_rows, width))
        inverse, unit, _ = norm_parts(middle, gain_m)
        back_norm, grad_gain_m = norm_back(back_shaped, inverse, unit, gain_m)
        back_middle = flowing + back_norm
        branch = jnp.concatenate(gather_x(back_middle.astype(BF)), axis=0)
        partial, packs[layer] = attention_backward(
            branch, attn_saved, tables, allowed, w_qkvs[layer], w_outs[layer]
        )
        back_normed = scatter_x([partial[own_rows * k : own_rows * (k + 1)] for k in range(4)])
        inverse, unit, _ = norm_parts(entry_own, gain_a)
        back_norm, grad_gain_a = norm_back(back_normed, inverse, unit, gain_a)
        flow = (back_middle + back_norm).astype(BF)
        in_grads[layer] = jnp.concatenate(gather_x(flow), axis=0)
        padding = jnp.zeros((64 - 2 - expert_count, width), F32)
        small_grads[layer] = jnp.concatenate(
            [grad_gain_a[None], grad_gain_m[None], grad_router, padding], axis=0
        )
        sums = []
        for number in range(2):
            own = [block[number] for block in grads[0]]
            other = [sibling(block[number].astype(BF)).astype(F32) for block in grads[1]]
            sums.append(scatter_x([a + b for a, b in zip(own, other)]))
        expert_grads[layer] = sums

    def owners(of_first, of_second):
        own = jnp.where(first, of_first, of_second)
        other = sibling(jnp.where(first, of_second, of_first).astype(BF)).astype(F32)
        return own, other

    def in_order(own, other):
        return jnp.where(first, jnp.stack([own, other]), jnp.stack([other, own]))

    whole = []
    for number in range(2):
        whole.append(in_order(*owners(expert_grads[0][number], expert_grads[1][number])))
    half_width = w_gate.shape[3]
    grad_gate, grad_up = whole[0][:, :, :half_width], whole[0][:, :, half_width:]
    grad_down = whole[1]

    halves = []
    for layer in range(2):
        half = packs[layer].shape[0] // 2
        kept_half = lax.dynamic_slice_in_dim(packs[layer], section * half, half, 0)
        given = lax.dynamic_slice_in_dim(packs[layer], (1 - section) * half, half, 0)
        joined = kept_half + sibling(given.astype(BF)).astype(F32)
        piece = collect_e(joined.astype(BF).reshape(16, -1, width))
        halves.append(spread_e(piece.astype(BF)).reshape(half, width).astype(F32))
    pack = in_order(*owners(halves[0], halves[1])).reshape(-1, width)
    q_cols, kv_cols = w_query.shape[2], w_key.shape[2]
    bounds = [0, q_cols, q_cols + kv_cols, q_cols + 2 * kv_cols, pack.shape[0]]
    grad_query, grad_key, grad_value, grad_out = (
        pack[a:b] for a, b in zip(bounds[:-1], bounds[1:])
    )

    small_own, small_other = owners(small_grads[0], small_grads[1])
    small_sum = jnp.roll(small_own + small_other, -16 * tensor, axis=0)
    small_sum = scatter_x([small_sum[16 * k : 16 * (k + 1)] for k in range(4)])
    small_sum = jnp.sum(spread_e(small_sum.astype(BF)).astype(F32), axis=0)
    small_total = jnp.concatenate(gather_x(small_sum.astype(BF)), axis=0)
    small_total = jnp.roll(small_total, 16 * tensor, axis=0).astype(F32)

    def straight(array):
        return jnp.roll(array, own_rows * tensor, axis=0)

    def by_batch(of_first, of_second):
        own = straight(jnp.where(first, of_first, of_second))
        other = sibling(straight(jnp.where(first, of_second, of_first)))
        return jnp.where(first, jnp.stack([own, other]), jnp.stack([other, own]))

    activations = by_batch(outputs[0], outputs[1])
    input_grads = by_batch(in_grads[0], in_grads[1])
    return (
        activations[None],
        input_grads[None],
        small_total[:1],
        grad_query.T[None],
        grad_key.T[None],
        grad_value.T[None],
        grad_out[None],
        small_total[1:2],
        small_total[2 : 2 + expert_count].T[None],
        grad_gate[None],
        grad_up[None],
        grad_down[None],
    )


def solution(mesh):
    in_specs = (
        P(None, "expert", None),
        P(None, "expert", None),
        P(None, "expert", None),
        P(None, "expert", None),
        P("section", None),
        P("section", None, "tensor"),
        P("section", None, "tensor"),
        P("section", None, "tensor"),
        P("section", "tensor", None),
        P("section", None),
        P("section", None, None),
        P("section", "expert", None, "tensor"),
        P("section", "expert", None, "tensor"),
        P("section", "expert", "tensor", None),
    )
    out_specs = (
        P("section", None, "expert", None),
        P("section", None, "expert", None),
        P("section", None),
        P("section", None, "tensor"),
        P("section", None, "tensor"),
        P("section", None, "tensor"),
        P("section", "tensor", None),
        P("section", None),
        P("section", None, None),
        P("section", "expert", None, "tensor"),
        P("section", "expert", None, "tensor"),
        P("section", "expert", "tensor", None),
    )
    return jax.shard_map(
        per_device, mesh=mesh, in_specs=in_specs, out_specs=out_specs, check_vma=False
    )
```

time: 1340 us -> 809 us (0.60)
  blocking collectives: 288 us -> 30.1 us
  local copies, waits for them, and re-layouts: 292 us -> 80.8 us
  waiting for transfers between devices: 335 us -> 216 us
  starting transfers between devices: 63.1 us -> 171 us
  other arithmetic: 186 us -> 90.2 us
  matrix products: 142 us -> 200 us
    all_to_all x8 -> x1, blocking collectives: 216 us -> 30.1 us  [collect_e(): pieces = lax.all_to_all(blocks, 'expert', 0, 0, tiled=True)]
    all_gather x7 -> x0, waiting for transfers between devices: 151 us -> none  [the longest x6 130 us: return_rows(): return lax.all_gather(moved_rows, 'tensor', axis=1, tiled=True)]
    ppermute x4 -> x109, waiting for transfers between devices: 0.47 us -> 129 us  [shifted(): lax.ppermute(array, axis, [(i, (i + by) % length) for i in range(length)])]
    gather x18 -> x0, local copies, waits for them, and re-layouts: 124 us -> none  [the longest x3 31.2 us: backward_layer(): returned.reshape(expert_count * capacity, model_width)[position]]
    all_to_all x11 -> x13, waiting for transfers between devices: 183 us -> 87 us  [the longest x8 53.4 us: spread_e(): return lax.all_to_all(copies, 'expert', 0, 0, tiled=True)]
    ppermute x4 -> x109, starting transfers between devices: 6.39 us -> 95.5 us  [shifted(): lax.ppermute(array, axis, [(i, (i + by) % length) for i in range(length)])]
    psum x1 -> x0, blocking collectives: 72.1 us -> none  [per_device(): lax.psum(grad_totals[0].astype(jnp.bfloat16), 'expert').astype(jnp.float32)]
    dot_general x15 -> x38, matrix products: 13 us -> 66.9 us  [contract_cols(): lax.dot_general(left_rows, right_rows, (((1,), (1,)), ((), ())), preferre...]
  transfers between devices with their start and end apart: 23 -> 122, of which waited for: 18 -> 36; matrix products, arithmetic and copies ran while one was open for 27% -> 39% of each run, Pallas kernels for 0% -> 0%
where the time goes in v1:
time: 809 us; the launch traced here: 794 us
  waiting for transfers between devices  216 us (27%)
  matrix products  200 us (25%)
  starting transfers between devices  171 us (21%)
  other arithmetic  90.2 us (11%)
  local copies, waits for them, and re-layouts  80.8 us (10%)
  blocking collectives  30.1 us (4%)
    ppermute x109, waiting for transfers between devices, shifted(): lax.ppermute(array, axis, [(i, (i + by) % length) for i in range(length)])  129 us
    ppermute x109, starting transfers between devices, shifted(): lax.ppermute(array, axis, [(i, (i + by) % length) for i in range(length)])  95.5 us
    dot_general x38, matrix products, contract_rows(): lax.dot_general(left_rows, right_rows, (((0,), (0,)), ((), ())), preferre...  72.4 us
    dot_general x38, matrix products, contract_cols(): lax.dot_general(left_rows, right_rows, (((1,), (1,)), ((), ())), preferre...  66.9 us
    dot_general x40, matrix products, dot(): return jnp.dot(left, right, preferred_element_type=F32)  54.7 us
    all_to_all x8, waiting for transfers between devices, spread_e(): return lax.all_to_all(copies, 'expert', 0, 0, tiled=True)  53.4 us
    all_to_all x8, starting transfers between devices, spread_e(): return lax.all_to_all(copies, 'expert', 0, 0, tiled=True)  46.6 us
    all_to_all x5, waiting for transfers between devices, collect_e(): pieces = lax.all_to_all(blocks, 'expert', 0, 0, tiled=True)  33.5 us
  transfers between devices with their start and end apart: 122, of which 36 were waited for; matrix products, arithmetic and copies ran while one was open for 39% of the time, Pallas kernels for 0%

profile of v1, /device:TPU:0, one launch (start us, length us, event | category | flops | bytes accessed | tf_op | source)
XLA Modules:
  0.0 793.7 jit_solution(5686956255459670446)
XLA Ops:
  8.3 8.2 %all-to-all-start = ((s32[16,1,256]{2,1,0:T(1,128)}), s32[16,1,256]{2,1,0:T(1,128)}, u32[]{:S(2)}, u32[]{:S(2)}) async-start(s32[16,1,256]{2,1,0:T(1,128)} %reshape.919), calls=%async_computation | async-start | bytes 32768 | tf_op jit(solution)/shard_map/all_to_all | solution.py:47
  48.4 7.2 all-to-all-start.1
  59.7 11.6 %collective-permute-done.9 = bf16[128,1536]{1,0:T(8,128)(2,1)} collective-permute-done((bf16[128,1536]{1,0:T(8,128)(2,1)}, bf16[128,1536]{1,0:T(8,128)(2,1)}, u32[]{:S(2)}, u32[]{:S(2)}) %collective-permute-start.9) | collective-permute-done | bytes 393248 | tf_op jit(solution)/shard_map/ppermute | solution.py:18
  92.9 4.1 collective-permute-done.12
  124.5 30.1 %all_to_all.70 = bf16[16,32,1536]{2,1,0:T(8,128)(2,1)S(1)} all-to-all(bf16[16,32,1536]{2,1,0:T(8,128)(2,1)S(1)} %bitcast.393), channel_id=1, replica_groups=mesh['section'=2,'expert'=16,'tensor'=4] {'expert'}, dimensions={0} | all-to-all | bytes 3145728 | tf_op jit(solution)/shard_map/all_to_all | solution.py:51
  188.1 11.2 %collective-permute-done.31 = bf16[128,1536]{1,0:T(8,128)(2,1)} collective-permute-done((bf16[128,1536]{1,0:T(8,128)(2,1)}, bf16[128,1536]{1,0:T(8,128)(2,1)}, u32[]{:S(2)}, u32[]{:S(2)}) %collective-permute-start.31) | collective-permute-done | bytes 393248 | tf_op jit(solution)/shard_map/ppermute | solution.py:18
  212.3 3.9 collective-permute-done.32
  217.0 3.7 collective-permute-done.34
  251.4 4.4 all-to-all-start.4
  257.6 23.0 %all-to-all-done.4 = bf16[16,32,1536]{2,1,0:T(8,128)(2,1)} async-done(((bf16[16,32,1536]{2,1,0:T(8,128)(2,1)}), bf16[16,32,1536]{2,1,0:T(8,128)(2,1)}, u32[]{:S(2)}, u32[]{:S(2)}) %all-to-all-start.4) | async-done | bytes 1572896 | tf_op jit(solution)/shard_map/all_to_all | solution.py:51
  289.0 4.5 all-to-all-start.5
  299.2 19.0 %all-to-all-done.5 = bf16[16,32,1664]{2,1,0:T(8,128)(2,1)} async-done(((bf16[16,32,1664]{2,1,0:T(8,128)(2,1)}), bf16[16,32,1664]{2,1,0:T(8,128)(2,1)}, u32[]{:S(2)}, u32[]{:S(2)}) %all-to-all-start.5) | async-done | bytes 1703968 | tf_op jit(solution)/shard_map/all_to_all | solution.py:47
  371.2 4.6 all-to-all-start.6
  390.3 10.5 %all-to-all-done.6 = bf16[16,32,1536]{2,1,0:T(8,128)(2,1)} async-done(((bf16[16,32,1536]{2,1,0:T(8,128)(2,1)}), bf16[16,32,1536]{2,1,0:T(8,128)(2,1)}, u32[]{:S(2)}, u32[]{:S(2)}) %all-to-all-start.6) | async-done | bytes 1572896 | tf_op jit(solution)/shard_map/all_to_all | solution.py:51
  444.6 4.4 all-to-all-start.7
  457.2 3.9 fusion.29
  461.1 13.5 %all-to-all-done.7 = bf16[16,32,1664]{2,1,0:T(8,128)(2,1)} async-done(((bf16[16,32,1664]{2,1,0:T(8,128)(2,1)}), bf16[16,32,1664]{2,1,0:T(8,128)(2,1)}, u32[]{:S(2)}, u32[]{:S(2)}) %all-to-all-start.7) | async-done | bytes 1703968 | tf_op jit(solution)/shard_map/all_to_all | solution.py:47
  527.6 4.4 all-to-all-start.8
  542.0 12.1 %collective-permute-done.105 = bf16[128,1536]{1,0:T(8,128)(2,1)S(1)} collective-permute-done((bf16[128,1536]{1,0:T(8,128)(2,1)S(1)}, bf16[128,1536]{1,0:T(8,128)(2,1)S(1)}, u32[]{:S(2)}, u32[]{:S(2)}) %collective-permute-start.105) | collective-permute-done | bytes 393248 | tf_op jit(solution)/shard_map/ppermute | solution.py:18
  561.1 12.4 %collective-permute-done.98 = bf16[128,1536]{1,0:T(8,128)(2,1)S(1)} collective-permute-done((bf16[128,1536]{1,0:T(8,128)(2,1)S(1)}, bf16[128,1536]{1,0:T(8,128)(2,1)S(1)}, u32[]{:S(2)}, u32[]{:S(2)}) %collective-permute-start.98) | collective-permute-done | bytes 393248 | tf_op jit(solution)/shard_map/ppermute | solution.py:18
  576.1 8.0 %all-to-all-start.12 = ((bf16[16,32,1536]{2,1,0:T(8,128)(2,1)}), bf16[16,32,1536]{2,1,0:T(8,128)(2,1)}, u32[]{:S(2)}, u32[]{:S(2)}) async-start(bf16[16,32,1536]{2,1,0:T(8,128)(2,1)} %bitcast.390), calls=%async_computation.12 | async-start | bytes 3145728 | tf_op jit(solution)/shard_map/all_to_all | solution.py:51
  587.6 3.8 collective-permute-start.56
  634.9 13.8 %collective-permute-done.72 = bf16[16,1536]{1,0:T(8,128)(2,1)S(1)} collective-permute-done((bf16[16,1536]{1,0:T(8,128)(2,1)}, bf16[16,1536]{1,0:T(8,128)(2,1)S(1)}, u32[]{:S(2)}, u32[]{:S(2)}) %collective-permute-start.72) | collective-permute-done | bytes 49184 | tf_op jit(solution)/shard_map/ppermute | solution.py:18
  652.3 7.4 all-to-all-start.9
  665.5 4.7 fusion.34
  674.4 7.7 all-to-all-start.10
  683.3 20.9 %collective-permute-done.65 = bf16[32,1536]{1,0:T(8,128)(2,1)} collective-permute-done((bf16[32,1536]{1,0:T(8,128)(2,1)}, bf16[32,1536]{1,0:T(8,128)(2,1)}, u32[]{:S(2)}, u32[]{:S(2)}) %collective-permute-start.65) | collective-permute-done | bytes 98336 | tf_op jit(solution)/shard_map/ppermute | solution.py:18
  711.8 5.1 select_bitcast_fusion
  721.2 7.5 all-to-all-start.13
  737.3 15.6 %all-to-all-done.13 = bf16[16,32,1536]{2,1,0:T(8,128)(2,1)S(1)} async-done(((bf16[16,32,1536]{2,1,0:T(8,128)(2,1)}), bf16[16,32,1536]{2,1,0:T(8,128)(2,1)S(1)}, u32[]{:S(2)}, u32[]{:S(2)}) %all-to-all-start.13) | async-done | bytes 1572896 | tf_op jit(solution)/shard_map/all_to_all | solution.py:47
  757.9 3.7 slice_bitcast_fusion.1
  774.6 5.3 all-to-all-done.11
  (1140 shorter events, 487.5 us)
Async XLA Ops:
  8.3 38.8 %all-to-all-start = ((s32[16,1,256]{2,1,0:T(1,128)}), s32[16,1,256]{2,1,0:T(1,128)}, u32[]{:S(2)}, u32[]{:S(2)}) async-start(s32[16,1,256]{2,1,0:T(1,128)} %reshape.919), calls=%async_computation | async-start | bytes 32768 | tf_op jit(solution)/shard_map/all_to_all | solution.py:47
  18.6 37.0 %collective-permute-start.7 = (bf16[128,1536]{1,0:T(8,128)(2,1)}, bf16[128,1536]{1,0:T(8,128)(2,1)}, u32[]{:S(2)}, u32[]{:S(2)}) collective-permute-start(bf16[128,1536]{1,0:T(8,128)(2,1)} %dynamic-slice_bitcast_fusion.1), channel_id=1, source_target_pairs={{0,64},{64,0},{1,65},{65,1},{2,66},{66,2},{3,67},{67,3},{4,68},{68... | collective-permute-start | bytes 1179656 | tf_op jit(solution)/shard_map/ppermute | solution.py:18
  43.7 36.3 %collective-permute-start.8 = (bf16[1536,256]{1,0:T(8,128)(2,1)S(1)}, bf16[1536,256]{1,0:T(8,128)(2,1)S(1)}, u32[]{:S(2)}, u32[]{:S(2)}) collective-permute-start(bf16[1536,256]{1,0:T(8,128)(2,1)S(1)} %get-tuple-element.66), channel_id=1, source_target_pairs={{0,3},{1,0},{2,1},{3,2},{4,7},{5,4},{6,5},{7,6},{8,11},{9,8},{10,9... | collective-permute-start | bytes 2359304 | tf_op jit(solution)/shard_map/ppermute | solution.py:18
  44.8 35.4 %collective-permute-start.11 = (bf16[1536,256]{1,0:T(8,128)(2,1)S(1)}, bf16[1536,256]{1,0:T(8,128)(2,1)}, u32[]{:S(2)}, u32[]{:S(2)}) collective-permute-start(bf16[1536,256]{1,0:T(8,128)(2,1)S(1)} %get-tuple-element.66), channel_id=1, source_target_pairs={{0,1},{1,2},{2,3},{3,0},{4,5},{5,6},{6,7},{7,4},{8,9},{9,10},{10,1... | collective-permute-start | bytes 2359304 | tf_op jit(solution)/shard_map/ppermute | solution.py:18
  48.4 49.8 %all-to-all-start.1 = ((bf16[16,32,1536]{2,1,0:T(8,128)(2,1)}), bf16[16,32,1536]{2,1,0:T(8,128)(2,1)S(1)}, u32[]{:S(2)}, u32[]{:S(2)}) async-start(bf16[16,32,1536]{2,1,0:T(8,128)(2,1)} %broadcast_in_dim.74), calls=%async_computation.1 | async-start | bytes 3145728 | tf_op jit(solution)/shard_map/all_to_all | solution.py:47
  78.0 36.5 %collective-permute-start.17 = (bf16[128,1536]{1,0:T(8,128)(2,1)}, bf16[128,1536]{1,0:T(8,128)(2,1)}, u32[]{:S(2)}, u32[]{:S(2)}) collective-permute-start(bf16[128,1536]{1,0:T(8,128)(2,1)} %get-tuple-element.68), channel_id=1, source_target_pairs={{0,64},{64,0},{1,65},{65,1},{2,66},{66,2},{3,67},{67,3},{4,68},{68... | collective-permute-start | bytes 1179656 | tf_op jit(solution)/shard_map/ppermute | solution.py:18
  88.8 32.1 %collective-permute-start.23 = (bf16[128,1536]{1,0:T(8,128)(2,1)}, bf16[128,1536]{1,0:T(8,128)(2,1)}, u32[]{:S(2)}, u32[]{:S(2)}) collective-permute-start(bf16[128,1536]{1,0:T(8,128)(2,1)} %collective-permute-done.14), channel_id=1, source_target_pairs={{0,64},{64,0},{1,65},{65,1},{2,66},{66,2},{3,67},{67,3},{4,68},{68... | collective-permute-start | bytes 1179656 | tf_op jit(solution)/shard_map/ppermute | solution.py:18
  182.3 39.2 %all-to-all-start.3 = ((bf16[16,32,1536]{2,1,0:T(8,128)(2,1)}), bf16[16,32,1536]{2,1,0:T(8,128)(2,1)S(1)}, u32[]{:S(2)}, u32[]{:S(2)}) async-start(bf16[16,32,1536]{2,1,0:T(8,128)(2,1)} %broadcast_in_dim.77), calls=%async_computation.3 | async-start | bytes 3145728 | tf_op jit(solution)/shard_map/all_to_all | solution.py:47
  202.1 39.2 %collective-permute-start.39 = (bf16[128,1536]{1,0:T(8,128)(2,1)}, bf16[128,1536]{1,0:T(8,128)(2,1)}, u32[]{:S(2)}, u32[]{:S(2)}) collective-permute-start(bf16[128,1536]{1,0:T(8,128)(2,1)} %get-tuple-element.67), channel_id=1, source_target_pairs={{0,64},{64,0},{1,65},{65,1},{2,66},{66,2},{3,67},{67,3},{4,68},{68... | collective-permute-start | bytes 1179656 | tf_op jit(solution)/shard_map/ppermute | solution.py:18
  211.7 35.1 %collective-permute-start.45 = (bf16[128,1536]{1,0:T(8,128)(2,1)}, bf16[128,1536]{1,0:T(8,128)(2,1)}, u32[]{:S(2)}, u32[]{:S(2)}) collective-permute-start(bf16[128,1536]{1,0:T(8,128)(2,1)} %collective-permute-done.36), channel_id=1, source_target_pairs={{0,64},{64,0},{1,65},{65,1},{2,66},{66,2},{3,67},{67,3},{4,68},{68... | collective-permute-start | bytes 1179656 | tf_op jit(solution)/shard_map/ppermute | solution.py:18
  216.2 32.1 %collective-permute-start.41 = (bf16[128,1536]{1,0:T(8,128)(2,1)}, bf16[128,1536]{1,0:T(8,128)(2,1)}, u32[]{:S(2)}, u32[]{:S(2)}) collective-permute-start(bf16[128,1536]{1,0:T(8,128)(2,1)} %collective-permute-done.31), channel_id=1, source_target_pairs={{0,64},{64,0},{1,65},{65,1},{2,66},{66,2},{3,67},{67,3},{4,68},{68... | collective-permute-start | bytes 1179656 | tf_op jit(solution)/shard_map/ppermute | solution.py:18
  332.1 48.6 %collective-permute-start.102 = (bf16[128,1536]{1,0:T(8,128)(2,1)}, bf16[128,1536]{1,0:T(8,128)(2,1)}, u32[]{:S(2)}, u32[]{:S(2)}) collective-permute-start(bf16[128,1536]{1,0:T(8,128)(2,1)} %convolution_convert_fusion.10), channel_id=1, source_target_pairs={{0,64},{64,0},{1,65},{65,1},{2,66},{66,2},{3,67},{67,3},{4,68},{68... | collective-permute-start | bytes 1179656 | tf_op jit(solution)/shard_map/ppermute | solution.py:18
  380.6 71.3 %collective-permute-start.91 = (bf16[1536,256]{1,0:T(8,128)(2,1)}, bf16[1536,256]{1,0:T(8,128)(2,1)}, u32[]{:S(2)}, u32[]{:S(2)}) collective-permute-start(bf16[1536,256]{1,0:T(8,128)(2,1)} %convolution_convert_fusion), channel_id=1, source_target_pairs={{0,64},{64,0},{1,65},{65,1},{2,66},{66,2},{3,67},{67,3},{4,68},{68... | collective-permute-start | bytes 2359304 | tf_op jit(solution)/shard_map/ppermute | solution.py:18
  449.0 92.0 %collective-permute-start.101 = (bf16[128,1536]{1,0:T(8,128)(2,1)}, bf16[128,1536]{1,0:T(8,128)(2,1)}, u32[]{:S(2)}, u32[]{:S(2)}) collective-permute-start(bf16[128,1536]{1,0:T(8,128)(2,1)} %convolution_convert_fusion.11), channel_id=1, source_target_pairs={{0,64},{64,0},{1,65},{65,1},{2,66},{66,2},{3,67},{67,3},{4,68},{68... | collective-permute-start | bytes 1179656 | tf_op jit(solution)/shard_map/ppermute | solution.py:18
  449.2 92.0 %collective-permute-start.103 = (bf16[128,1536]{1,0:T(8,128)(2,1)}, bf16[128,1536]{1,0:T(8,128)(2,1)}, u32[]{:S(2)}, u32[]{:S(2)}) collective-permute-start(bf16[128,1536]{1,0:T(8,128)(2,1)} %add_convert_fusion.8), channel_id=1, source_target_pairs={{0,1},{1,2},{2,3},{3,0},{4,5},{5,6},{6,7},{7,4},{8,9},{9,10},{10,1... | collective-permute-start | bytes 1179656 | tf_op jit(solution)/shard_map/ppermute | solution.py:18
  491.1 40.9 %collective-permute-start.95 = (bf16[128,1536]{1,0:T(8,128)(2,1)}, bf16[128,1536]{1,0:T(8,128)(2,1)}, u32[]{:S(2)}, u32[]{:S(2)}) collective-permute-start(bf16[128,1536]{1,0:T(8,128)(2,1)} %convolution_convert_fusion.14), channel_id=1, source_target_pairs={{0,64},{64,0},{1,65},{65,1},{2,66},{66,2},{3,67},{67,3},{4,68},{68... | collective-permute-start | bytes 1179656 | tf_op jit(solution)/shard_map/ppermute | solution.py:18
  491.2 43.3 %collective-permute-start.97 = (bf16[128,1536]{1,0:T(8,128)(2,1)}, bf16[128,1536]{1,0:T(8,128)(2,1)}, u32[]{:S(2)}, u32[]{:S(2)}) collective-permute-start(bf16[128,1536]{1,0:T(8,128)(2,1)} %convolution_convert_fusion.13), channel_id=1, source_target_pairs={{0,64},{64,0},{1,65},{65,1},{2,66},{66,2},{3,67},{67,3},{4,68},{68... | collective-permute-start | bytes 1179656 | tf_op jit(solution)/shard_map/ppermute | solution.py:18
  491.7 47.3 %collective-permute-start.99 = (bf16[128,1536]{1,0:T(8,128)(2,1)}, bf16[128,1536]{1,0:T(8,128)(2,1)}, u32[]{:S(2)}, u32[]{:S(2)}) collective-permute-start(bf16[128,1536]{1,0:T(8,128)(2,1)} %convolution_convert_fusion.12), channel_id=1, source_target_pairs={{0,64},{64,0},{1,65},{65,1},{2,66},{66,2},{3,67},{67,3},{4,68},{68... | collective-permute-start | bytes 1179656 | tf_op jit(solution)/shard_map/ppermute | solution.py:18
  527.6 48.5 %all-to-all-start.8 = ((bf16[16,32,1536]{2,1,0:T(8,128)(2,1)}), bf16[16,32,1536]{2,1,0:T(8,128)(2,1)}, u32[]{:S(2)}, u32[]{:S(2)}) async-start(bf16[16,32,1536]{2,1,0:T(8,128)(2,1)} %bitcast.394), calls=%async_computation.8 | async-start | bytes 3145728 | tf_op jit(solution)/shard_map/all_to_all | solution.py:51
  560.5 100.4 %collective-permute-start.86 = (bf16[1536,256]{1,0:T(8,128)(2,1)}, bf16[1536,256]{1,0:T(8,128)(2,1)}, u32[]{:S(2)}, u32[]{:S(2)}) collective-permute-start(bf16[1536,256]{1,0:T(8,128)(2,1)} %convolution_convert_fusion.3), channel_id=1, source_target_pairs={{0,64},{64,0},{1,65},{65,1},{2,66},{66,2},{3,67},{67,3},{4,68},{68... | collective-permute-start | bytes 2359304 | tf_op jit(solution)/shard_map/ppermute | solution.py:18
  561.0 61.5 %collective-permute-start.84 = (bf16[1536,256]{1,0:T(8,128)(2,1)}, bf16[1536,256]{1,0:T(8,128)(2,1)}, u32[]{:S(2)}, u32[]{:S(2)}) collective-permute-start(bf16[1536,256]{1,0:T(8,128)(2,1)} %convolution_convert_fusion.4), channel_id=1, source_target_pairs={{0,64},{64,0},{1,65},{65,1},{2,66},{66,2},{3,67},{67,3},{4,68},{68... | collective-permute-start | bytes 2359304 | tf_op jit(solution)/shard_map/ppermute | solution.py:18
  576.1 56.5 %all-to-all-start.12 = ((bf16[16,32,1536]{2,1,0:T(8,128)(2,1)}), bf16[16,32,1536]{2,1,0:T(8,128)(2,1)}, u32[]{:S(2)}, u32[]{:S(2)}) async-start(bf16[16,32,1536]{2,1,0:T(8,128)(2,1)} %bitcast.390), calls=%async_computation.12 | async-start | bytes 3145728 | tf_op jit(solution)/shard_map/all_to_all | solution.py:51
  621.3 42.9 %collective-permute-start.76 = (bf16[512,1536]{1,0:T(8,128)(2,1)}, bf16[512,1536]{1,0:T(8,128)(2,1)}, u32[]{:S(2)}, u32[]{:S(2)}) collective-permute-start(bf16[512,1536]{1,0:T(8,128)(2,1)} %fusion.31), channel_id=1, source_target_pairs={{0,64},{64,0},{1,65},{65,1},{2,66},{66,2},{3,67},{67,3},{4,68},{68... | collective-permute-start | bytes 4718600 | tf_op jit(solution)/shard_map/ppermute | solution.py:18
  628.4 32.5 %collective-permute-start.88 = (bf16[1536,256]{1,0:T(8,128)(2,1)}, bf16[1536,256]{1,0:T(8,128)(2,1)S(1)}, u32[]{:S(2)}, u32[]{:S(2)}) collective-permute-start(bf16[1536,256]{1,0:T(8,128)(2,1)} %add_convert_fusion.2), channel_id=1, source_target_pairs={{0,1},{1,2},{2,3},{3,0},{4,5},{5,6},{6,7},{7,4},{8,9},{9,10},{10,1... | collective-permute-start | bytes 2359304 | tf_op jit(solution)/shard_map/ppermute | solution.py:18
  628.4 34.5 %collective-permute-start.90 = (bf16[1536,256]{1,0:T(8,128)(2,1)}, bf16[1536,256]{1,0:T(8,128)(2,1)}, u32[]{:S(2)}, u32[]{:S(2)}) collective-permute-start(bf16[1536,256]{1,0:T(8,128)(2,1)} %add_convert_fusion.1), channel_id=1, source_target_pairs={{0,3},{1,0},{2,1},{3,2},{4,7},{5,4},{6,5},{7,6},{8,11},{9,8},{10,9... | collective-permute-start | bytes 2359304 | tf_op jit(solution)/shard_map/ppermute | solution.py:18
  660.9 46.0 %collective-permute-start.79 = (bf16[1536,256]{1,0:T(8,128)(2,1)}, bf16[1536,256]{1,0:T(8,128)(2,1)}, u32[]{:S(2)}, u32[]{:S(2)}) collective-permute-start(bf16[1536,256]{1,0:T(8,128)(2,1)} %convolution_convert_fusion.7), channel_id=1, source_target_pairs={{0,64},{64,0},{1,65},{65,1},{2,66},{66,2},{3,67},{67,3},{4,68},{68... | collective-permute-start | bytes 2359304 | tf_op jit(solution)/shard_map/ppermute | solution.py:18
  660.9 46.9 %collective-permute-start.81 = (bf16[1536,256]{1,0:T(8,128)(2,1)}, bf16[1536,256]{1,0:T(8,128)(2,1)}, u32[]{:S(2)}, u32[]{:S(2)}) collective-permute-start(bf16[1536,256]{1,0:T(8,128)(2,1)} %add_convert_fusion.5), channel_id=1, source_target_pairs={{0,1},{1,2},{2,3},{3,0},{4,5},{5,6},{6,7},{7,4},{8,9},{9,10},{10,1... | collective-permute-start | bytes 2359304 | tf_op jit(solution)/shard_map/ppermute | solution.py:18
  662.9 47.3 %collective-permute-start.83 = (bf16[1536,256]{1,0:T(8,128)(2,1)}, bf16[1536,256]{1,0:T(8,128)(2,1)}, u32[]{:S(2)}, u32[]{:S(2)}) collective-permute-start(bf16[1536,256]{1,0:T(8,128)(2,1)} %add_convert_fusion.4), channel_id=1, source_target_pairs={{0,3},{1,0},{2,1},{3,2},{4,7},{5,4},{6,5},{7,6},{8,11},{9,8},{10,9... | collective-permute-start | bytes 2359304 | tf_op jit(solution)/shard_map/ppermute | solution.py:18
  664.2 46.3 %collective-permute-start.85 = (bf16[1536,256]{1,0:T(8,128)(2,1)}, bf16[1536,256]{1,0:T(8,128)(2,1)}, u32[]{:S(2)}, u32[]{:S(2)}) collective-permute-start(bf16[1536,256]{1,0:T(8,128)(2,1)} %add_convert_fusion.3), channel_id=1, source_target_pairs={{0,2},{1,3},{2,0},{3,1},{4,6},{5,7},{6,4},{7,5},{8,10},{9,11},{10,... | collective-permute-start | bytes 2359304 | tf_op jit(solution)/shard_map/ppermute | solution.py:18
  670.1 34.1 %collective-permute-start.65 = (bf16[32,1536]{1,0:T(8,128)(2,1)}, bf16[32,1536]{1,0:T(8,128)(2,1)}, u32[]{:S(2)}, u32[]{:S(2)}) collective-permute-start(bf16[32,1536]{1,0:T(8,128)(2,1)} %get-tuple-element.41), channel_id=1, source_target_pairs={{0,3},{1,0},{2,1},{3,2},{4,7},{5,4},{6,5},{7,6},{8,11},{9,8},{10,9... | collective-permute-start | bytes 294920 | tf_op jit(solution)/shard_map/ppermute | solution.py:18
  674.4 45.5 %all-to-all-start.10 = ((bf16[16,32,1536]{2,1,0:T(8,128)(2,1)}), bf16[16,32,1536]{2,1,0:T(8,128)(2,1)}, u32[]{:S(2)}, u32[]{:S(2)}) async-start(bf16[16,32,1536]{2,1,0:T(8,128)(2,1)} %bitcast.391), calls=%async_computation.10 | async-start | bytes 3145728 | tf_op jit(solution)/shard_map/all_to_all | solution.py:51
  721.2 31.7 %all-to-all-start.13 = ((bf16[16,32,1536]{2,1,0:T(8,128)(2,1)}), bf16[16,32,1536]{2,1,0:T(8,128)(2,1)S(1)}, u32[]{:S(2)}, u32[]{:S(2)}) async-start(bf16[16,32,1536]{2,1,0:T(8,128)(2,1)} %broadcast_in_dim.86), calls=%async_computation.13 | async-start | bytes 3145728 | tf_op jit(solution)/shard_map/all_to_all | solution.py:47
  (381 other events, 2992.9 us)

commit v2 on v1

v2 whole, which is shorter than its diff:
```python
import math

import jax
import jax.numpy as jnp
from jax import lax
from jax.experimental import pallas as pl
from jax.experimental.pallas import tpu as pltpu
from jax.sharding import PartitionSpec as P

HEADS = 24
KV_HEADS = 8
HEAD_DIM = 64
SHARING = HEADS // KV_HEADS
EPSILON = 1e-06
LOWEST = -1e30
BF = jnp.bfloat16
F32 = jnp.float32
ANY = pl.BlockSpec(memory_space=pl.ANY)
WHOLE = pl.BlockSpec(memory_space=pltpu.VMEM)
SCALARS = pl.BlockSpec(memory_space=pltpu.SMEM)
BESIDE = 128


def shifted(array, axis, by):
    length = lax.axis_size(axis)
    return lax.ppermute(array, axis, [(i, (i + by) % length) for i in range(length)])


def sibling(array):
    return shifted(array, "section", 1)


def to_core(array, core):
    return lax.ppermute(array, "section", [(1 - core, core)])


def after(value, *others):
    return lax.optimization_barrier((value, *others))[0]


def gather_x(block):
    ahead = {k: shifted(block, "tensor", -k) for k in (1, 3, 2)}
    return [block, ahead[1], ahead[2], ahead[3]]


def arrivals(blocks):
    return [blocks[0]] + [shifted(blocks[k], "tensor", k) for k in (1, 2, 3)]


def sum_of(blocks):
    return sum(block.astype(F32) for block in blocks).astype(BF)


def spread_e(block):
    return exchange_e(jnp.broadcast_to(block[None], (lax.axis_size("expert"), *block.shape)))


def exchange_e(blocks):
    return lax.all_to_all(blocks, "expert", 0, 0, tiled=True)


def collect_e(blocks):
    return jnp.sum(exchange_e(blocks).astype(F32), axis=0).astype(BF)


def dot(left, right):
    return jnp.dot(left, right, preferred_element_type=F32)


def contract_rows(left, right):
    return lax.dot_general(left, right, (((0,), (0,)), ((), ())), preferred_element_type=F32)


def contract_cols(left, right):
    return lax.dot_general(left, right, (((1,), (1,)), ((), ())), preferred_element_type=F32)


def call(kernel, outs, args, specs, scratch=(), grid=None, out_specs=None):
    extra = {} if grid is None else {"grid": grid}
    return pl.pallas_call(
        kernel,
        out_shape=[jax.ShapeDtypeStruct(shape, kind) for shape, kind in outs],
        in_specs=specs,
        out_specs=out_specs or [WHOLE] * len(outs),
        scratch_shapes=list(scratch),
        compiler_params=pltpu.CompilerParams(vmem_limit_bytes=60 * 2**20),
        cost_estimate=pl.CostEstimate(flops=1, bytes_accessed=1, transcendentals=0),
        **extra,
    )(*args)


def inverse_level(rows):
    return lax.rsqrt(jnp.mean(rows * rows, axis=-1, keepdims=True) + EPSILON)


def norm_back(back_scaled, rows, gain):
    inverse = inverse_level(rows)
    unit = rows * inverse
    back_unit = back_scaled * gain
    level = inverse * (back_unit - unit * jnp.mean(back_unit * unit, axis=-1, keepdims=True))
    return level, jnp.sum(back_scaled * unit, axis=0, keepdims=True)


def of_layer(layer, section, own, other):
    return jnp.where(section == layer, own[...].astype(F32), other[...].astype(F32))


def prepare_tables(place, documents, columns):
    rows = documents.shape[2]
    share = rows // 4

    def kernel(at, doc_ref, cos, sin, mask):
        turn = share * at[1]
        doc = pltpu.roll(doc_ref[at[0]].astype(F32), lax.rem(rows - turn, rows), 1)
        along = jnp.broadcast_to(doc, (rows, rows))
        down = along.T
        place_along = lax.rem(lax.broadcasted_iota(jnp.int32, (rows, rows), 1) + turn, rows)
        place_down = lax.rem(lax.broadcasted_iota(jnp.int32, (rows, rows), 0) + turn, rows)
        mask[...] = jnp.where((along == down) & (place_along <= place_down), 0.0, LOWEST)
        starts = jnp.sum(jnp.where(along < down, 1.0, 0.0), axis=1, keepdims=True)
        lane = lax.broadcasted_iota(jnp.int32, (rows, 128), 1)
        frequency = jnp.exp(lax.rem(lane, HEAD_DIM // 2).astype(F32) * (-2.0 * math.log(10000.0) / HEAD_DIM))
        offset = place_down[:, :1].astype(F32) - starts
        angle = offset * frequency
        for ref, table in ((cos, jnp.cos(angle)), (sin, jnp.sin(angle))):
            for a in range(0, columns, 128):
                ref[:, a : a + 128] = table

    return call(
        kernel,
        [((rows, columns), F32), ((rows, columns), F32), ((rows, rows), F32)],
        [place, documents],
        [SCALARS, WHOLE],
    )


def half_turn(values):
    lane = lax.broadcasted_iota(jnp.int32, values.shape, 1)
    width = values.shape[1]
    behind = pltpu.roll(values, width - HEAD_DIM // 2, 1)
    before = pltpu.roll(values, HEAD_DIM // 2, 1)
    return jnp.where(lane % HEAD_DIM < HEAD_DIM // 2, -behind, before)


def pick(layer, section, own, other, target, sem, start):
    for here, source in ((True, own), (False, other)):

        @pl.when((section == layer) == here)
        def _():
            copy = pltpu.make_async_copy(source, target, sem)
            copy.start() if start else copy.wait()


def pick_all(layer, section, weights, qkv, out, sems, which, start):
    at = 0
    for i in range(4):
        width = weights[i].shape[1]
        target = out if i == 3 else qkv.at[:, at : at + width]
        at += width
        if i in which:
            pick(layer, section, weights[i], weights[4 + i], target, sems.at[i], start)


def attention_forward(source, tables, weights, gains, place, layer):
    width, q_cols = weights[0].shape
    kv_cols = weights[1].shape[1]
    all_cols = q_cols + 2 * kv_cols
    heads = q_cols // HEAD_DIM
    rows = tables[0].shape[0]
    share = rows // 4
    entries = len(source)

    def kernel(at, *refs):
        entry, refs = refs[:entries], refs[entries:]
        (cos, sin, allowed, gain_own, gain_other), refs = refs[:5], refs[5:]
        parts, refs = refs[:8], refs[8:]
        (p0, p1, p2, p3, normed, qkv, lse, attended, w_qkv, w_out, staged, sems) = refs
        section = at[0]
        if entries == 1:
            copies = [
                pltpu.make_async_copy(
                    entry[0].at[section, pl.ds(pl.multiple_of(share * lax.rem(at[1] + k, 4), share), share)],
                    staged.at[share * k : share * (k + 1)],
                    sems.at[4 + k],
                )
                for k in range(4)
            ]
            for copy in copies:
                copy.start()
        pick_all(layer, section, parts, w_qkv, w_out, sems, range(4), True)
        gain = of_layer(layer, section, gain_own, gain_other)
        for k in range(4):
            if entries == 1:
                copies[k].wait()
                x = staged[share * k : share * (k + 1), :].astype(F32)
            else:
                x = entry[k][...].astype(F32)
            normed[share * k : share * (k + 1), :] = (x * inverse_level(x) * gain).astype(BF)
        pick_all(layer, section, parts, w_qkv, w_out, sems, range(3), False)
        raw = dot(normed[...], w_qkv[...])
        turned = raw[:, : q_cols + kv_cols]
        turned = turned * cos[...] + half_turn(turned) * sin[...]
        qkv[:, : q_cols + kv_cols] = turned.astype(BF)
        qkv[:, q_cols + kv_cols :] = raw[:, q_cols + kv_cols :].astype(BF)
        sums = jnp.zeros((rows, 128), F32)
        lane = lax.broadcasted_iota(jnp.int32, (rows, 128), 1)
        for h in range(heads):
            g = h // SHARING
            q = qkv[:, HEAD_DIM * h : HEAD_DIM * (h + 1)]
            key = qkv[:, q_cols + HEAD_DIM * g : q_cols + HEAD_DIM * (g + 1)]
            value = qkv[:, q_cols + kv_cols + HEAD_DIM * g : q_cols + kv_cols + HEAD_DIM * (g + 1)]
            scores = contract_cols(q, key) * HEAD_DIM**-0.5 + allowed[...]
            peak = jnp.max(scores, axis=-1, keepdims=True)
            raised = jnp.exp(scores - peak)
            total = jnp.sum(raised, axis=-1, keepdims=True)
            sums = jnp.where(lane == h, peak + jnp.log(total), sums)
            probability = (raised / total).astype(BF)
            attended[:, HEAD_DIM * h : HEAD_DIM * (h + 1)] = dot(probability, value).astype(BF)
        lse[...] = sums
        pick_all(layer, section, parts, w_qkv, w_out, sems, (3,), False)
        for k, ref in enumerate((p0, p1, p2, p3)):
            ref[...] = dot(attended[share * k : share * (k + 1), :], w_out[...]).astype(BF)

    results = call(
        kernel,
        [((share, width), BF)] * 4
        + [((rows, width), BF), ((rows, all_cols), BF), ((rows, 128), F32), ((rows, q_cols), BF)],
        [place, *source, *tables, *gains, *weights],
        [SCALARS] + [ANY if entries == 1 else WHOLE] * entries + [WHOLE] * 5 + [ANY] * 8,
        [
            pltpu.VMEM((width, all_cols), BF),
            pltpu.VMEM((q_cols, width), BF),
            pltpu.VMEM((rows, width), BF),
            pltpu.SemaphoreType.DMA((8,)),
        ],
    )
    return results[:4], results[4:]


def attention_backward(blocks, saved, tables, weights, place, layer):
    normed, qkv, lse, attended = saved
    rows, width = normed.shape
    q_cols = weights[0].shape[1]
    kv_cols = weights[1].shape[1]
    all_cols = q_cols + 2 * kv_cols
    groups = kv_cols // HEAD_DIM
    share = rows // 4

    def kernel(at, b0, b1, b2, b3, qkv_ref, lse_ref, cos, sin, allowed, *refs):
        parts, refs = refs[:8], refs[8:]
        p0, p1, p2, p3, branch, back_qkv, w_qkv, w_out, back_o, back_qk, sems = refs
        section = at[0]
        pick_all(layer, section, parts, w_qkv, w_out, sems, (3, 0, 1, 2), True)
        for k, ref in enumerate((b0, b1, b2, b3)):
            branch[share * k : share * (k + 1), :] = ref[...]
        pick_all(layer, section, parts, w_qkv, w_out, sems, (3,), False)
        back_o[...] = contract_cols(branch[...], w_out[...]).astype(BF)
        for g in range(groups):
            at_k = q_cols + HEAD_DIM * g
            at_v = q_cols + kv_cols + HEAD_DIM * g
            key = qkv_ref[:, at_k : at_k + HEAD_DIM]
            value = qkv_ref[:, at_v : at_v + HEAD_DIM]
            back_value = jnp.zeros((rows, HEAD_DIM), F32)
            back_key = jnp.zeros((rows, HEAD_DIM), F32)
            for h in range(SHARING * g, SHARING * (g + 1)):
                q = qkv_ref[:, HEAD_DIM * h : HEAD_DIM * (h + 1)]
                back = back_o[:, HEAD_DIM * h : HEAD_DIM * (h + 1)]
                scores = contract_cols(q, key) * HEAD_DIM**-0.5 + allowed[...]
                probability = jnp.exp(scores - lse_ref[:, h : h + 1])
                back_p = contract_cols(back, value)
                back_value = back_value + contract_rows(probability.astype(BF), back)
                delta = jnp.sum(back_p * probability, axis=-1, keepdims=True)
                back_s = (probability * (back_p - delta)).astype(BF)
                back_qk[:, HEAD_DIM * h : HEAD_DIM * (h + 1)] = dot(back_s, key)
                back_key = back_key + contract_rows(back_s, q)
            back_qk[:, at_k : at_k + HEAD_DIM] = back_key
            back_qkv[:, at_v : at_v + HEAD_DIM] = back_value.astype(BF)
        scaled = back_qk[...] * HEAD_DIM**-0.5
        turned = scaled * cos[...] - half_turn(scaled * sin[...])
        back_qkv[:, : q_cols + kv_cols] = turned.astype(BF)
        pick_all(layer, section, parts, w_qkv, w_out, sems, range(3), False)
        for k, ref in enumerate((p0, p1, p2, p3)):
            ref[...] = contract_cols(back_qkv[share * k : share * (k + 1), :], w_qkv[...]).astype(BF)

    results = call(
        kernel,
        [((share, width), BF)] * 4 + [((rows, width), BF), ((rows, all_cols), BF)],
        [place, *blocks, qkv, lse, *tables, *weights],
        [SCALARS] + [WHOLE] * 9 + [ANY] * 8,
        [
            pltpu.VMEM((width, all_cols), BF),
            pltpu.VMEM((q_cols, width), BF),
            pltpu.VMEM((rows, q_cols), BF),
            pltpu.VMEM((rows, q_cols + kv_cols), F32),
            pltpu.SemaphoreType.DMA((4,)),
        ],
    )
    return results[:4], results[4], results[5]


def attention_grads(place, back_qkv, saved, branch):
    normed, attended = saved[0], saved[3]
    rows, width = normed.shape
    all_cols, q_cols = back_qkv.shape[1], attended.shape[1]
    half = width // 2

    def kernel(at, back_ref, normed_ref, attended_ref, branch_ref, mine, other):
        for out, which in ((other, 1 - at[0]), (mine, at[0])):
            for a in range(0, half, 256):
                columns = pl.ds(pl.multiple_of(half * which + a, 256), 256)
                out[a : a + 256, :all_cols] = contract_rows(normed_ref[:, columns], back_ref[...]).astype(BF)
                out[a : a + 256, all_cols:] = contract_rows(branch_ref[:, columns], attended_ref[...]).astype(BF)

    return call(
        kernel,
        [((half, all_cols + q_cols), BF)] * 2,
        [place, back_qkv, normed, attended, branch],
        [SCALARS] + [WHOLE] * 4,
    )


def attention_finish(place, halves, widths):
    half = halves[0].shape[0]
    q_cols = widths[0]
    ends = [sum(widths[:k]) for k in range(4)]

    def kernel(at, h0, h1, h2, h3, grad_q, grad_k, grad_v, grad_o):
        def store(ref, which):
            rows = pl.ds(half * which, half)
            for out, start, width in zip((grad_q, grad_k, grad_v), ends, widths):
                out[0, rows, :] = ref[:, start : start + width].astype(F32)
            grad_o[0, :, rows] = ref[:, ends[3] : ends[3] + q_cols].astype(F32).T

        @pl.when(at[0] == 0)
        def _():
            store(h0, 0)
            store(h2, 1)

        @pl.when(at[0] == 1)
        def _():
            store(h1, 1)
            store(h3, 0)

    return call(
        kernel,
        [((1, 2 * half, w), F32) for w in widths] + [((1, q_cols, 2 * half), F32)],
        [place, *halves],
        [SCALARS] + [WHOLE] * 4,
    )


def small_finish(blocks, count):
    chunks = blocks[0].shape[0] // 65
    width = chunks * 128

    def kernel(a, b, c, d, router, gain_m, gain_a):
        total = a[...].astype(F32) + b[...].astype(F32) + c[...].astype(F32) + d[...].astype(F32)
        for i in range(chunks):
            columns = slice(128 * i, 128 * (i + 1))
            router[:, columns] = total[64 * i : 64 * i + count, :]
            gain_m[:, columns] = total[64 * i + count : 64 * i + count + 1, :]
            gain_a[:, columns] = total[64 * chunks + i : 64 * chunks + i + 1, :]

    return call(
        kernel,
        [((count, width), F32), ((1, width), F32), ((1, width), F32)],
        blocks,
        [WHOLE] * 4,
    )


def prepare_experts(place, w_gate, w_up, w_down):
    _, width, deep = w_gate.shape
    half = width // 2

    def kernel(at, gate, up, down, kept_low, kept_high, given_low, given_high):
        for outs, which in (((given_low, given_high), 1 - at[0]), ((kept_low, kept_high), at[0])):
            for out, start in zip(outs, (0, half)):
                out[:, :deep] = gate[which, start : start + half, :]
                out[:, deep : 2 * deep] = up[which, start : start + half, :]
                out[:, 2 * deep :] = down[which, :, start : start + half].T

    results = call(
        kernel,
        [((half, 3 * deep), BF)] * 4,
        [place, w_gate, w_up, w_down],
        [SCALARS] + [WHOLE] * 3,
    )
    return results[:2], results[2:]


def load_experts(refs, gate_up, down, sems):
    each = len(refs) // 2
    width, deep = down.shape[0], refs[0].shape[1] // 3
    half = width // 2
    spots = [(block, low, low + half) for block in (0, 1, 3, 2) for low in (0, half)]
    up_copies, down_copies = [[], []], [[], []]
    sem = 0
    for k in range(2):
        for ref, (block, low, high) in zip(refs[each * k : each * (k + 1)], spots):
            at = 4 * k + block
            if gate_up is not None:
                target = gate_up.at[low:high, 2 * deep * at : 2 * deep * (at + 1)]
                up_copies[k].append(pltpu.make_async_copy(ref.at[:, : 2 * deep], target, sems.at[sem]))
            target = down.at[low:high, deep * at : deep * (at + 1)]
            down_copies[k].append(pltpu.make_async_copy(ref.at[:, 2 * deep :], target, sems.at[sem + 1]))
            sem += 2
    return up_copies, down_copies


def start_all(*groups):
    for group in groups:
        for copies in group:
            for copy in copies:
                copy.start()


def wait_all(copies):
    for copy in copies:
        copy.wait()


def gate_table(rows, names, router):
    count, width = rows.shape[0], router.shape[0]
    number = lax.broadcasted_iota(jnp.int32, (count, width), 1).astype(F32)
    chosen = jnp.zeros((count, width), F32)
    for j in range(names.shape[1]):
        chosen = jnp.where(number == names[:, j : j + 1], 1.0, chosen)
    logits = jnp.where(chosen > 0, contract_cols(rows, router), LOWEST)
    raised = jnp.where(chosen > 0, jnp.exp(logits - jnp.max(logits, axis=-1, keepdims=True)), 0.0)
    return raised / jnp.sum(raised, axis=-1, keepdims=True)


def expert_gates(x, names, router, at):
    table = gate_table(x, names, router)
    number = lax.broadcasted_iota(jnp.int32, table.shape, 1)
    wanted = (2 * at[2] + at[0], 2 * at[2] + 1 - at[0])
    return [jnp.sum(jnp.where(number == e, table, 0.0), axis=-1, keepdims=True) for e in wanted]


def keep_gates(gates, own):
    lane = lax.broadcasted_iota(jnp.int32, gates.shape, 1)
    gates[...] = jnp.where(lane == 0, own[0], jnp.where(lane == 1, own[1], 0.0))


def expert_down(hidden, down, out):
    width = down.shape[0]
    for a in range(0, width, 256):
        out[:, a : a + 256] = contract_cols(hidden[...], down[a : a + 256, :]).astype(BF)


def expert_backs(back, gate_up, down, waits, pre, gates, out, back_pre, hidden):
    count, width = back.shape
    deep = hidden.shape[1] // 8
    lane = lax.broadcasted_iota(jnp.int32, (count, BESIDE), 1)
    beside = jnp.zeros((count, BESIDE), F32)
    for k in range(2):
        wait_all(waits[0][k])
        gate_weight = gates[:, k : k + 1]
        inner = jnp.zeros((count, 1), F32)
        for b in range(0, 4, 2):
            first = deep * (4 * k + b)
            raw = dot(back[...], down[:, first : first + 2 * deep])
            for c in range(2):
                gate, up = pre(k, b + c)
                piece = raw[:, deep * c : deep * (c + 1)]
                sigma = 1.0 / (1.0 + jnp.exp(-gate))
                smooth = gate * sigma
                full = smooth * up
                inner = inner + jnp.sum(piece * full, axis=-1, keepdims=True)
                at = first + deep * c
                hidden[:, at : at + deep] = (gate_weight * full).astype(BF)
                flow = gate_weight * piece
                back_pre[:, 2 * at : 2 * at + deep] = (
                    flow * up * sigma * (1.0 + gate * (1.0 - sigma))
                ).astype(BF)
                back_pre[:, 2 * at + deep : 2 * at + 2 * deep] = (flow * smooth).astype(BF)
        high = inner.astype(BF).astype(F32)
        beside = jnp.where(lane == 2 * k, high, jnp.where(lane == 2 * k + 1, inner - high, beside))
    out[:, width:] = beside.astype(BF)
    for k in range(2):
        wait_all(waits[1][k])
    for a in range(0, width, 256):
        out[:, a : a + 256] = contract_cols(back_pre[...], gate_up[a : a + 256, :]).astype(BF)


def experts_forward(rows, top, router, weights, place, layer):
    count, width = rows.shape[0], rows.shape[1] - BESIDE
    deep = weights[0].shape[1] // 3
    used = len(weights)

    def kernel(at, x, router_own, router_other, *refs):
        parts, outs, scratch = refs[:used], refs[used : used + 4], refs[used + 4 :]
        (out, pre, gates, names), (gate_up, down, hidden, sems) = outs, scratch
        up_copies, down_copies = load_experts(parts, gate_up, down, sems)
        start_all(up_copies, down_copies)
        table = of_layer(layer, at[0], router_own, router_other).astype(BF)
        names[...] = x[:, width:]
        numbers = x[:, width:].astype(F32)[:, :top]
        keep_gates(gates, expert_gates(x[:, :width], numbers, table, at))
        for k in range(2):
            wait_all(up_copies[k])
            for b in range(4):
                at_b = deep * (4 * k + b)
                both = dot(x[:, :width], gate_up[:, 2 * at_b : 2 * at_b + 2 * deep])
                pre[:, 2 * at_b : 2 * at_b + 2 * deep] = both.astype(BF)
                gate, up = both[:, :deep], both[:, deep:]
                value = gates[:, k : k + 1] * gate * up / (1.0 + jnp.exp(-gate))
                hidden[:, at_b : at_b + deep] = value.astype(BF)
        for k in range(2):
            wait_all(down_copies[k])
        expert_down(hidden, down, out)

    return call(
        kernel,
        [((count, width), BF), ((count, 16 * deep), BF), ((count, 128), F32), ((count, BESIDE), BF)],
        [place, rows, *router, *weights],
        [SCALARS] + [WHOLE] * 3 + [ANY] * used,
        [
            pltpu.VMEM((width, 16 * deep), BF),
            pltpu.VMEM((width, 8 * deep), BF),
            pltpu.VMEM((count, 8 * deep), BF),
            pltpu.SemaphoreType.DMA((2 * used,)),
        ],
    )


def experts_backward(back, pre, gates, weights):
    count, width = back.shape
    deep = weights[0].shape[1] // 3
    used = len(weights)

    def kernel(back_ref, pre_ref, gates_ref, *refs):
        parts, (out, back_pre, hidden), (gate_up, down, sems) = refs[:used], refs[used : used + 3], refs[used + 3 :]
        up_copies, down_copies = load_experts(parts, gate_up, down, sems)
        start_all(down_copies, up_copies)

        def acts(k, b):
            at = 2 * deep * (4 * k + b)
            both = pre_ref[:, at : at + 2 * deep].astype(F32)
            return both[:, :deep], both[:, deep:]

        expert_backs(back_ref, gate_up, down, (down_copies, up_copies), acts, gates_ref, out, back_pre, hidden)

    return call(
        kernel,
        [((count, width + BESIDE), BF), ((count, 16 * deep), BF), ((count, 8 * deep), BF)],
        [back, pre, gates, *weights],
        [WHOLE] * 3 + [ANY] * used,
        [
            pltpu.VMEM((width, 16 * deep), BF),
            pltpu.VMEM((width, 8 * deep), BF),
            pltpu.SemaphoreType.DMA((2 * used,)),
        ],
    )


def experts_both(rows, names, top, router, back, weights, place, layer):
    count, width = rows.shape
    deep = weights[0].shape[1] // 3
    used = len(weights)

    def kernel(at, x, names_ref, router_own, router_other, back_ref, *refs):
        parts, (out, back_pre, hidden), (gate_up, down, pre, gates, sems) = (
            refs[:used],
            refs[used : used + 3],
            refs[used + 3 :],
        )
        up_copies, down_copies = load_experts(parts, gate_up, down, sems)
        start_all(up_copies, down_copies)
        table = of_layer(layer, at[0], router_own, router_other).astype(BF)
        numbers = names_ref[...].astype(F32)[:, :top]
        keep_gates(gates, expert_gates(x[...], numbers, table, at))
        for k in range(2):
            wait_all(up_copies[k])
            for b in range(4):
                at_b = 2 * deep * (4 * k + b)
                pre[:, at_b : at_b + 2 * deep] = dot(x[...], gate_up[:, at_b : at_b + 2 * deep])

        def acts(k, b):
            at_b = 2 * deep * (4 * k + b)
            return pre[:, at_b : at_b + deep], pre[:, at_b + deep : at_b + 2 * deep]

        expert_backs(back_ref, gate_up, down, (down_copies, ([], [])), acts, gates, out, back_pre, hidden)

    return call(
        kernel,
        [((count, width + BESIDE), BF), ((count, 16 * deep), BF), ((count, 8 * deep), BF)],
        [place, rows, names, *router, back, *weights],
        [SCALARS] + [WHOLE] * 5 + [ANY] * used,
        [
            pltpu.VMEM((width, 16 * deep), BF),
            pltpu.VMEM((width, 8 * deep), BF),
            pltpu.VMEM((count, 16 * deep), F32),
            pltpu.VMEM((count, 128), F32),
            pltpu.SemaphoreType.DMA((2 * used,)),
        ],
    )


def experts_out(hidden, weights):
    count = hidden.shape[0]
    width, deep = 2 * weights[0].shape[0], weights[0].shape[1] // 3
    used = len(weights)

    def kernel(hidden_ref, *refs):
        parts, out, down, sems = refs[:used], *refs[used:]
        _, down_copies = load_experts(parts, None, down, sems)
        start_all(down_copies)
        wait_all(down_copies[0] + down_copies[1])
        expert_down(hidden_ref, down, out)

    return call(
        kernel,
        [((count, width), BF)],
        [hidden, *weights],
        [WHOLE] + [ANY] * used,
        [pltpu.VMEM((width, 8 * deep), BF), pltpu.SemaphoreType.DMA((2 * used,))],
    )[0]


def experts_grads(rows, back, back_pre, hidden, which):
    count, width = back.shape
    deep = hidden.shape[1] // 8

    def kernel(x, back_ref, pre_ref, hidden_ref, out, rows_turned, back_turned):
        @pl.when(pl.program_id(0) == 0)
        def _():
            rows_turned[...] = x[:, :width].T
            back_turned[...] = back_ref[...].T

        for a in range(0, width, 512):
            out[0, a : a + 512, : 2 * deep] = dot(rows_turned[a : a + 512, :], pre_ref[...]).astype(BF)
            out[0, a : a + 512, 2 * deep :] = dot(back_turned[a : a + 512, :], hidden_ref[...]).astype(BF)

    return call(
        kernel,
        [((4, width, 3 * deep), BF)],
        [rows, back, back_pre, hidden],
        [
            WHOLE,
            WHOLE,
            pl.BlockSpec((count, 2 * deep), lambda i: (0, i + 4 * which)),
            pl.BlockSpec((count, deep), lambda i: (0, i + 4 * which)),
        ],
        [pltpu.VMEM((width, count), BF)] * 2,
        grid=(4,),
        out_specs=[pl.BlockSpec((1, width, 3 * deep), lambda i: (i, 0, 0))],
    )[0]


def experts_finish(place, sums):
    half, deep = sums[0].shape[0], sums[0].shape[1] // 3

    def kernel(at, *refs):
        sums, (grad_gate, grad_up, grad_down) = refs[:8], refs[8:]

        def store(halves, which):
            for ref, rows in zip(halves, (slice(0, half), slice(half, 2 * half))):
                grad_gate[0, which, rows, :] = ref[:, :deep].astype(F32)
                grad_up[0, which, rows, :] = ref[:, deep : 2 * deep].astype(F32)
                grad_down[0, which, :, rows] = ref[:, 2 * deep :].astype(F32).T

        @pl.when(at[0] == 0)
        def _():
            store(sums[0:2], 0)
            store(sums[4:6], 1)

        @pl.when(at[0] == 1)
        def _():
            store(sums[2:4], 1)
            store(sums[6:8], 0)

    return call(
        kernel,
        [((1, 2, 2 * half, deep), F32)] * 2 + [((1, 2, deep, 2 * half), F32)],
        [place, *sums],
        [SCALARS] + [WHOLE] * 8,
    )


def middle_rows(entry, pieces, gain, names, router, place, layer, copies):
    share, width = entry.shape
    top = names.shape[1]
    beside = 0 if layer else BESIDE
    count = router[0].shape[0]

    def kernel(at, entry_ref, a, b, c, d, gain_own, gain_other, names_ref, router_own, router_other,
               middle, out, shaped, gates):
        total = entry_ref[...].astype(F32)
        for ref in (a, b, c, d):
            total = total + ref[...].astype(F32)
        middle[...] = total
        rows = (total * inverse_level(total) * of_layer(layer, at[0], gain_own, gain_other)).astype(BF)
        shaped[...] = rows
        numbers = names_ref[...].astype(F32)
        lane = lax.broadcasted_iota(jnp.int32, (share, BESIDE), 1)
        extra = jnp.zeros((share, BESIDE), F32)
        for j in range(top):
            extra = jnp.where(lane == j, numbers[:, j : j + 1], extra)
        for k in range(copies):
            out[k, :, :width] = rows
            if beside:
                out[k, :, width:] = extra.astype(BF)
        table = of_layer(layer, at[0], router_own, router_other).astype(BF)
        gates[...] = gate_table(rows, numbers, table)

    return call(
        kernel,
        [((share, width), F32), ((copies, share, width + beside), BF), ((share, width), BF), ((share, count), F32)],
        [place, entry, *pieces, *gain, names, *router],
        [SCALARS] + [WHOLE] * 10,
    )


def leave_rows(middle, pieces):
    share, width = middle.shape

    def kernel(middle_ref, pieces_ref, out):
        total = middle_ref[...]
        for k in range(pieces_ref.shape[0]):
            total = total + pieces_ref[k].astype(F32)
        out[...] = total.astype(BF)

    return call(kernel, [((share, width), BF)], [middle, pieces], [WHOLE] * 2)[0]


def back_middle_rows(flow, pieces, middle, shaped, gates, gain, router, place, layer):
    share, width = middle.shape
    count = gates.shape[1]

    def kernel(at, flow_ref, pieces_ref, middle_ref, shaped_ref, gates_ref, gain_own, gain_other, router_own,
               router_other, back, rounded, small):
        total = jnp.zeros((share, width), F32)
        inner = jnp.zeros((share, count), F32)
        number = lax.broadcasted_iota(jnp.int32, (share, count), 1)
        for p in range(pieces_ref.shape[0]):
            total = total + pieces_ref[p, :, :width].astype(F32)
            beside = pieces_ref[p, :, width:].astype(F32)
            for k, e in enumerate((2 * p + at[0], 2 * p + 1 - at[0])):
                value = beside[:, 2 * k : 2 * k + 1] + beside[:, 2 * k + 1 : 2 * k + 2]
                inner = jnp.where(number == e, value, inner)
        own = gates_ref[...]
        slope = jnp.sum(own * inner, axis=-1, keepdims=True)
        logits = (own * (inner - slope)).astype(BF)
        table = of_layer(layer, at[0], router_own, router_other).astype(BF)
        total = total + dot(logits, table)
        gain_row = of_layer(layer, at[0], gain_own, gain_other)
        level, grad = norm_back(total, middle_ref[...], gain_row)
        total = flow_ref[...].astype(F32) + level
        back[...] = total
        rounded[...] = total.astype(BF)
        grad_router = contract_rows(logits, shaped_ref[...])
        row = lax.broadcasted_iota(jnp.int32, (64 - count, 128), 0)
        for i in range(width // 128):
            columns = slice(128 * i, 128 * (i + 1))
            small[64 * i : 64 * i + count, :] = grad_router[:, columns]
            small[64 * i + count : 64 * (i + 1), :] = jnp.where(row == 0, grad[:, columns], 0.0)

    return call(
        kernel,
        [((share, width), F32), ((share, width), BF), ((width // 2, 128), F32)],
        [place, flow, pieces, middle, shaped, gates, *gain, *router],
        [SCALARS] + [WHOLE] * 9,
    )


def back_entry_rows(back, pieces, entry, gain, place, layer, copies):
    share, width = back.shape

    def kernel(at, back_ref, a, b, c, d, entry_ref, gain_own, gain_other, out, grad_gain, *more):
        total = a[...].astype(F32) + b[...].astype(F32) + c[...].astype(F32) + d[...].astype(F32)
        level, grad = norm_back(
            total, entry_ref[...].astype(F32), of_layer(layer, at[0], gain_own, gain_other)
        )
        flow = (back_ref[...] + level).astype(BF)
        out[...] = flow
        grad_gain[...] = grad
        for ref in more:
            for k in range(copies):
                ref[k] = flow

    outs = [((share, width), BF), ((1, width), F32)]
    if copies:
        outs.append(((copies, share, width), BF))
    return call(
        kernel, outs, [place, back, *pieces, entry, *gain], [SCALARS] + [WHOLE] * 8
    )


def straight_rows(place, of_first, of_second):
    share, width = of_first[0].shape

    def kernel(at, *refs):
        blocks, (own, other) = refs[:8], refs[8:]
        for k in range(4):
            rows = pl.ds(pl.multiple_of(share * lax.rem(at[1] + k, 4), share), share)
            here = at[0] == 0
            own[rows, :] = jnp.where(here, blocks[k][...].astype(F32), blocks[4 + k][...].astype(F32)).astype(BF)
            other[rows, :] = jnp.where(here, blocks[4 + k][...].astype(F32), blocks[k][...].astype(F32)).astype(BF)

    return call(
        kernel,
        [((4 * share, width), BF)] * 2,
        [place, *of_first, *of_second],
        [SCALARS] + [WHOLE] * 8,
    )


def by_batch(place, own, other):
    rows, width = own.shape

    def kernel(at, own_ref, other_ref, out):
        out[0, at[0]] = own_ref[...]
        out[0, 1 - at[0]] = other_ref[...]

    return call(kernel, [((1, 2, rows, width), BF)], [place, own, other], [SCALARS] + [WHOLE] * 2)[0]


def per_device(
    inputs,
    cotangent,
    documents,
    routes,
    gain_attn,
    w_query,
    w_key,
    w_value,
    w_out,
    gain_moe,
    w_router,
    w_gate,
    w_up,
    w_down,
):
    section = lax.axis_index("section")
    expert = lax.axis_index("expert")
    tensor = lax.axis_index("tensor")
    sequences = lax.axis_size("expert")
    first = section == 0
    place = jnp.stack([section, tensor, expert]).astype(jnp.int32)
    rows, width = inputs.shape[1:]
    share = rows // 4
    expert_count = w_router.shape[2]
    own_weights = [w_query[0], w_key[0], w_value[0], w_out[0]]

    def own_rows(array):
        start = (section, share * tensor, 0)
        return lax.dynamic_slice(array, start, (1, share, array.shape[2]))[0]

    kept, given = prepare_experts(place, w_gate[0], w_up[0], w_down[0])
    given = [sibling(half) for half in given]
    low, high = (jnp.where(first, a, b) for a, b in zip(kept, given))
    one_low, three_high = shifted(low, "tensor", -1), shifted(high, "tensor", 1)
    weights = own_weights + [sibling(w) for w in own_weights]

    gains_a = [gain_attn, sibling(gain_attn)]
    gains_m = [gain_moe, sibling(gain_moe)]
    routers = [w_router[0].T, sibling(w_router[0].T)]
    tables = prepare_tables(place, documents, w_query.shape[2] + w_key.shape[2])
    names_own = own_rows(routes)
    top = routes.shape[2]
    flow = after(own_rows(cotangent), low, high)
    backs = [None, spread_e(flow).reshape(-1, width)]

    entry = [own_rows(inputs), None]
    attn_saved, middles, shapeds, gates_own, arrived = ([None, None] for _ in range(5))
    pieces, attn_saved[0] = attention_forward([after(inputs, low, high)], tables, weights, gains_a, place, 0)
    pieces = arrivals(pieces)
    middles[0], copies, shapeds[0], gates_own[0] = middle_rows(
        entry[0], pieces, gains_m, names_own, routers, place, 0, sequences
    )
    one_high = shifted(after(high, *pieces), "tensor", -1)
    three_low = shifted(after(low, *pieces), "tensor", 1)
    two_low = shifted(after(one_low, *pieces), "tensor", -1)
    two_high = shifted(after(three_high, *pieces), "tensor", 1)
    mine = [low, high, one_low, one_high, three_low, three_high, two_low, two_high]
    expert_weights = [[*mine, *[sibling(block) for block in mine]], None]
    copies = after(copies, backs[1])
    arrived[0] = exchange_e(copies).reshape(-1, width + BESIDE)
    low, high = (jnp.where(first, b, a) for a, b in zip(kept, given))
    low, high = after((low, high), two_low, two_high)
    one_low, three_low = shifted(low, "tensor", -1), shifted(low, "tensor", 1)
    terms, pre, gates, names = experts_forward(arrived[0], top, routers, expert_weights[0], place, 0)
    terms = after(terms, one_low, three_low)
    pieces = exchange_e(terms.reshape(-1, share, width))
    one_high, three_high = shifted(high, "tensor", -1), shifted(high, "tensor", 1)
    entry[1] = leave_rows(middles[0], after(pieces, one_high, three_high))

    blocks = gather_x(entry[1])
    outputs = [blocks, None]
    pieces, attn_saved[1] = attention_forward(blocks, tables, weights, gains_a, place, 1)
    pieces = arrivals(pieces)
    two_low = shifted(after(low, *pieces), "tensor", -2)
    two_high = shifted(after(high, *pieces), "tensor", -2)
    mine = [low, high, one_low, one_high, three_low, three_high, two_low, two_high]
    expert_weights[1] = [*mine, *[sibling(block) for block in mine]]
    middles[1], copies, shapeds[1], gates_own[1] = middle_rows(
        entry[1], pieces, gains_m, names_own, routers, place, 1, sequences
    )
    arrived[1] = exchange_e(copies).reshape(-1, width)
    terms, back_pre, hidden = experts_both(
        arrived[1], names, top, routers, backs[1], expert_weights[1], place, 1
    )

    def join(mines, others):
        half = width // 2
        return [
            [sum_of([mines[k, a : a + half], others[k, a : a + half]]) for a in (0, half)]
            for k in range(4)
        ]

    in_blocks, smalls, grads_gain = ([None, None] for _ in range(3))
    pieces = exchange_e(terms.reshape(-1, share, width + BESIDE))
    others = experts_grads(arrived[1], backs[1], back_pre, hidden, 1)
    mines = experts_grads(arrived[1], backs[1], back_pre, hidden, 0)
    outs = experts_out(hidden, expert_weights[1])
    back_middle, rounded, smalls[1] = back_middle_rows(
        flow, after(pieces, mines, others, outs), middles[1], shapeds[1], gates_own[1], gains_m, routers, place, 1
    )
    others = sibling(after(others, rounded))
    out_pieces = exchange_e(after(outs, rounded).reshape(-1, share, width))
    partial, branch, back_qkv = attention_backward(
        gather_x(rounded), attn_saved[1], tables, weights, place, 1
    )
    flow, grads_gain[1], copies = back_entry_rows(
        back_middle, arrivals(partial), entry[1], gains_a, place, 1, sequences
    )
    in_blocks[1] = gather_x(flow)
    mine_half, other_half = attention_grads(place, back_qkv, attn_saved[1], branch)
    copies = after(copies, out_pieces)
    backs[0] = exchange_e(copies).reshape(-1, width)
    last = leave_rows(middles[1], after(out_pieces, flow))
    outputs[1] = gather_x(last)
    joined = join(after(mines, last), others)
    half_one = sum_of([mine_half, sibling(other_half)])
    lows = after(tuple(block[0] for block in joined), *outputs[1], *in_blocks[1])
    highs = tuple(block[1] for block in joined)
    first_low, third_low = shifted(lows[1], "tensor", 1), shifted(lows[3], "tensor", 3)
    backs[0] = after(backs[0], half_one, first_low, third_low)
    highs = after(highs, first_low, third_low)
    first_high, third_high = shifted(highs[1], "tensor", 1), shifted(highs[3], "tensor", 3)

    piece = collect_e(after(half_one, backs[0]).reshape(sequences, -1, half_one.shape[1]))
    terms, back_pre, hidden = experts_backward(backs[0], pre, gates, expert_weights[0])
    terms = after(terms, piece, first_high, third_high)
    second_low, second_high = (
        shifted(after(block, first_high, third_high), "tensor", 2) for block in joined[2]
    )
    pieces = exchange_e(terms.reshape(-1, share, width + BESIDE))
    others = experts_grads(arrived[0], backs[0], back_pre, hidden, 1)
    mines = experts_grads(arrived[0], backs[0], back_pre, hidden, 0)
    sums = [
        None,
        [
            sum_of([lows[0], first_low, second_low, third_low]),
            sum_of([highs[0], first_high, second_high, third_high]),
        ],
    ]
    own, other = straight_rows(place, outputs[0], outputs[1])
    activations = by_batch(place, own, sibling(other))
    pieces = after(pieces, mines, others, sums[1][0], sums[1][1], activations)
    back_middle, rounded, smalls[0] = back_middle_rows(
        flow, pieces, middles[0], shapeds[0], gates_own[0], gains_m, routers, place, 0
    )
    others = sibling(after(others, rounded))
    columns = half_one.shape[1] // 2
    piece = after(piece, rounded)
    done_one = [spread_e(piece[:, a : a + columns]).reshape(-1, columns) for a in (0, columns)]
    gathered = gather_x(rounded)
    partial, branch, back_qkv = attention_backward(gathered, attn_saved[0], tables, weights, place, 0)
    mine_half, other_half = attention_grads(
        place, after(back_qkv, done_one[0]), attn_saved[0], branch
    )
    pieces = arrivals(partial)
    flow, grads_gain[0] = back_entry_rows(back_middle, pieces, entry[0], gains_a, place, 0, 0)

    def own_layer(of_first, of_second):
        own = jnp.where(first, of_first, of_second)
        return own + sibling(jnp.where(first, of_second, of_first).astype(BF)).astype(F32)

    small = own_layer(smalls[0], smalls[1]).astype(BF)
    half_zero = jnp.concatenate([sum_of([mine_half, sibling(other_half)]), small], axis=1)
    half_zero = after(half_zero, done_one[1])
    joined = join(after(mines, half_zero), others)
    first_zero = [shifted(half, "tensor", 1) for half in joined[1]]
    third_zero = [shifted(half, "tensor", 3) for half in joined[3]]
    piece = collect_e(half_zero.reshape(sequences, -1, half_zero.shape[1]))
    gain = own_layer(grads_gain[0], grads_gain[1]).reshape(width // 128, 128).astype(BF)
    gain = jnp.pad(gain, ((0, piece.shape[0] - width // 128), (0, 0)))
    piece = jnp.concatenate([piece, gain], axis=1)
    piece = after(piece, *first_zero, *third_zero)
    second_zero = [
        shifted(after(half, *first_zero, *third_zero), "tensor", 2) for half in joined[2]
    ]
    spread = spread_e(piece)
    gain = jnp.sum(spread[:, : width // 128, -128:].astype(F32), axis=0).astype(BF)
    done_zero = after(spread, *second_zero).reshape(half_one.shape[0], -1)
    small = jnp.concatenate([done_zero[:, -256:-128], gain], axis=0)
    grad_router, grad_gain_m, gain = small_finish(gather_x(small), expert_count)
    sums[0] = [
        sum_of([joined[0][n], first_zero[n], second_zero[n], third_zero[n]]) for n in range(2)
    ]
    grad_gate, grad_up, grad_down = experts_finish(
        place,
        [*sums[0], *sums[1], *[to_core(half, 0) for half in sums[0]], *[to_core(half, 1) for half in sums[1]]],
    )
    done_one = jnp.concatenate(done_one, axis=1)
    grad_query, grad_key, grad_value, grad_out = attention_finish(
        place,
        [done_zero, done_one, to_core(done_zero, 0), to_core(done_one, 1)],
        [w_query.shape[2], w_key.shape[2], w_value.shape[2]],
    )

    own, other = straight_rows(place, gather_x(flow), in_blocks[1])
    input_grads = by_batch(place, own, sibling(other))
    return (
        activations,
        input_grads,
        gain,
        grad_query,
        grad_key,
        grad_value,
        grad_out,
        grad_gain_m,
        grad_router.T[None],
        grad_gate,
        grad_up,
        grad_down,
    )


def solution(mesh):
    in_specs = (
        P(None, "expert", None),
        P(None, "expert", None),
        P(None, "expert", None),
        P(None, "expert", None),
        P("section", None),
        P("section", None, "tensor"),
        P("section", None, "tensor"),
        P("section", None, "tensor"),
        P("section", "tensor", None),
        P("section", None),
        P("section", None, None),
        P("section", "expert", None, "tensor"),
        P("section", "expert", None, "tensor"),
        P("section", "expert", "tensor", None),
    )
    out_specs = (
        P("section", None, "expert", None),
        P("section", None, "expert", None),
        P("section", None),
        P("section", None, "tensor"),
        P("section", None, "tensor"),
        P("section", None, "tensor"),
        P("section", "tensor", None),
        P("section", None),
        P("section", None, None),
        P("section", "expert", None, "tensor"),
        P("section", "expert", None, "tensor"),
        P("section", "expert", "tensor", None),
    )
    return jax.shard_map(
        per_device, mesh=mesh, in_specs=in_specs, out_specs=out_specs, check_vma=False
    )
```

time: 809 us -> 601 us (0.74)
  matrix products: 200 us -> 0 us
  Pallas kernels: 0 us -> 167 us
  other arithmetic: 90.2 us -> 32.8 us
  local copies, waits for them, and re-layouts: 80.8 us -> 28.5 us
  waiting for transfers between devices: 216 us -> 180 us
  blocking collectives: 30.1 us -> 0 us
    dot_general x130 -> x0, matrix products: 200 us -> none  [the longest x38 72.4 us: contract_rows(): lax.dot_general(left_rows, right_rows, (((0,), (0,)), ((), ())), preferre...]
    pallas_call x0 -> x31, Pallas kernels: none -> 167 us  [call(): pl.pallas_call(kernel, out_shape=[jax.ShapeDtypeStruct(shape, kind) for s...]
    all_to_all x13, waiting for transfers between devices: 87 us -> 31.9 us  [exchange_e(): return lax.all_to_all(blocks, 'expert', 0, 0, tiled=True)]
    all_to_all x1 -> x0, blocking collectives: 30.1 us -> none  [collect_e(): pieces = lax.all_to_all(blocks, 'expert', 0, 0, tiled=True)]
    ppermute x109 -> x90, waiting for transfers between devices: 129 us -> 149 us  [shifted(): lax.ppermute(array, axis, [(i, (i + by) % length) for i in range(length)])]
    reduce_sum x23 -> x3, other arithmetic: 18.1 us -> 1.23 us  [the longest x2 1.21 us: collect_e(): return jnp.sum(exchange_e(blocks).astype(F32), axis=0).astype(BF)]
    slice x29 -> x2, local copies, waits for them, and re-layouts: 13.6 us -> 0.02 us  [the longest x1 0.01 us: per_device(): small = jnp.concatenate([done_zero[:, -256:-128], gain], axis=0)]
    select_n x12 -> x2, other arithmetic: 16.9 us -> 3.37 us  [per_device(): low, high = (jnp.where(first, b, a) for a, b in zip(kept, given))]
  transfers between devices with their start and end apart: 122 -> 109, of which waited for: 36 -> 46; matrix products, arithmetic and copies ran while one was open for 39% -> 6% of each run, Pallas kernels for 0% -> 21%
where the time goes in v2:
time: 601 us; the launch traced here: 590 us
  waiting for transfers between devices  180 us (30%)
  starting transfers between devices  179 us (30%)
  Pallas kernels  167 us (28%)
  other arithmetic  32.8 us (5%)
  local copies, waits for them, and re-layouts  28.5 us (5%)
    pallas_call x31, Pallas kernels, call(): pl.pallas_call(kernel, out_shape=[jax.ShapeDtypeStruct(shape, kind) for s...  167 us
    ppermute x90, waiting for transfers between devices, shifted(): lax.ppermute(array, axis, [(i, (i + by) % length) for i in range(length)])  149 us
    ppermute x90, starting transfers between devices, shifted(): lax.ppermute(array, axis, [(i, (i + by) % length) for i in range(length)])  89 us
    all_to_all x13, starting transfers between devices, exchange_e(): return lax.all_to_all(blocks, 'expert', 0, 0, tiled=True)  78.1 us
    all_to_all x13, waiting for transfers between devices, exchange_e(): return lax.all_to_all(blocks, 'expert', 0, 0, tiled=True)  31.9 us
    convert_element_type x7, other arithmetic, sum_of(): return sum((block.astype(F32) for block in blocks)).astype(BF)  24.7 us
    unnamed x220, local copies, waits for them, and re-layouts  21.6 us
    ppermute x6, starting transfers between devices, to_core(): return lax.ppermute(array, 'section', [(1 - core, core)])  12.2 us
  transfers between devices with their start and end apart: 109, of which 46 were waited for; matrix products, arithmetic and copies ran while one was open for 6% of the time, Pallas kernels for 21%

profile of v2, /device:TPU:0, one launch (start us, length us, event | category | flops | bytes accessed | tf_op | source)
XLA Modules:
  0.0 590.1 jit_solution(9596063426873271818)
XLA Ops:
  11.5 8.3 %all-to-all-start = ((bf16[16,32,1536]{2,1,0:T(8,128)(2,1)}), bf16[16,32,1536]{2,1,0:T(8,128)(2,1)S(1)}, u32[]{:S(2)}, u32[]{:S(2)}) async-start(bf16[16,32,1536]{2,1,0:T(8,128)(2,1)} %broadcast_in_dim.10), calls=%async_computation | async-start | bytes 3145728 | tf_op jit(solution)/shard_map/all_to_all | solution.py:59
  27.2 7.0 %shard_map.231 = (bf16[32,1536]{1,0:T(8,128)(2,1)}, bf16[32,1536]{1,0:T(8,128)(2,1)}, bf16[32,1536]{1,0:T(8,128)(2,1)}, bf16[32,1536]{1,0:T(8,128)(2,1)}, bf16[1...) custom-call(s32[3]{0:T(128)} %pad_add_fusion.at, ...), custom_call_target="tpu_custom_call" | custom-call | flops 1 | bytes 1 | tf_op jit(solution)/shard_map/pallas_call | solution.py:80
  55.7 7.2 %all-to-all-start.1 = ((bf16[16,32,1664]{2,1,0:T(8,128)(2,1)}), bf16[16,32,1664]{2,1,0:T(8,128)(2,1)S(1)}, u32[]{:S(2)}, u32[]{:S(2)}) async-start(bf16[16,32,1664]{2,1,0:T(8,128)(2,1)} %get-tuple-element.149), calls=%async_computation.1 | async-start | bytes 3407872 | tf_op jit(solution)/shard_map/all_to_all | solution.py:59
  63.6 8.3 %collective-permute-done.16.refs_6_ = bf16[768,384]{1,0:T(8,128)(2,1)} collective-permute-done((bf16[768,384]{1,0:T(8,128)(2,1)}, bf16[768,384]{1,0:T(8,128)(2,1)}, u32[]{:S(2)}, u32[]{:S(2)}) %collective-permute-start.16) | collective-permute-done | bytes 589856 | tf_op jit(solution)/shard_map/ppermute | solution.py:26
  72.5 7.7 %collective-permute-done.14.refs_4_ = bf16[768,384]{1,0:T(8,128)(2,1)S(1)} collective-permute-done((bf16[768,384]{1,0:T(8,128)(2,1)}, bf16[768,384]{1,0:T(8,128)(2,1)S(1)}, u32[]{:S(2)}, u32[]{:S(2)}) %collective-permute-start.14) | collective-permute-done | bytes 589856 | tf_op jit(solution)/shard_map/ppermute | solution.py:26
  90.1 11.5 %shard_map.233 = (bf16[512,1536]{1,0:T(8,128)(2,1)}, bf16[512,2048]{1,0:T(8,128)(2,1)}, f32[512,128]{1,0:T(8,128)}, bf16[512,128]{1,0:T(8,128)(2,1)}) custom-call(s32[3]{0:T(128)} %pad_add_fusion.at, bf16[512,1664]{1,0:T(8,128)(2,1)} %bitcast.73, bf16[32,1536]{1,0:T(8,128)(2,1)} %bitcast.101, bf16[32,1536]{1,0:T(8,128)(2,1)} %copy-done.18, ...), custom_call_target="tpu_custom_call" | custom-call | flops 1 | bytes 1 | tf_op jit(solution)/shard_map/pallas_call | solution.py:80
  109.2 12.5 %collective-permute-done.29.refs_5_ = bf16[768,384]{1,0:T(8,128)(2,1)S(1)} collective-permute-done((bf16[768,384]{1,0:T(8,128)(2,1)S(1)}, bf16[768,384]{1,0:T(8,128)(2,1)S(1)}, u32[]{:S(2)}, u32[]{:S(2)}) %collective-permute-start.29) | collective-permute-done | bytes 589856 | tf_op jit(solution)/shard_map/ppermute | solution.py:26
  121.7 7.7 %all-to-all-done.2.pieces_ref = bf16[16,32,1536]{2,1,0:T(8,128)(2,1)S(1)} async-done(((bf16[16,32,1536]{2,1,0:T(8,128)(2,1)}), bf16[16,32,1536]{2,1,0:T(8,128)(2,1)S(1)}, u32[]{:S(2)}, u32[]{:S(2)}) %all-to-all-start.2) | async-done | bytes 1572896 | tf_op jit(solution)/shard_map/all_to_all | solution.py:59
  141.6 6.9 %shard_map.235 = (bf16[32,1536]{1,0:T(8,128)(2,1)}, bf16[32,1536]{1,0:T(8,128)(2,1)}, bf16[32,1536]{1,0:T(8,128)(2,1)}, bf16[32,1536]{1,0:T(8,128)(2,1)}, bf16[1...) custom-call(s32[3]{0:T(128)} %pad_add_fusion.at, ...), custom_call_target="tpu_custom_call" | custom-call | flops 1 | bytes 1 | tf_op jit(solution)/shard_map/pallas_call | solution.py:80
  169.8 13.4 %collective-permute-done.36.refs_6_ = bf16[768,384]{1,0:T(8,128)(2,1)S(1)} collective-permute-done((bf16[768,384]{1,0:T(8,128)(2,1)S(1)}, bf16[768,384]{1,0:T(8,128)(2,1)S(1)}, u32[]{:S(2)}, u32[]{:S(2)}) %collective-permute-start.36) | collective-permute-done | bytes 589856 | tf_op jit(solution)/shard_map/ppermute | solution.py:26
  183.2 12.2 %collective-permute-done.37.refs_7_ = bf16[768,384]{1,0:T(8,128)(2,1)S(1)} collective-permute-done((bf16[768,384]{1,0:T(8,128)(2,1)S(1)}, bf16[768,384]{1,0:T(8,128)(2,1)S(1)}, u32[]{:S(2)}, u32[]{:S(2)}) %collective-permute-start.37) | collective-permute-done | bytes 589856 | tf_op jit(solution)/shard_map/ppermute | solution.py:26
  198.7 15.7 %shard_map.237 = (bf16[512,1664]{1,0:T(8,128)(2,1)}, bf16[512,2048]{1,0:T(8,128)(2,1)}, bf16[512,1024]{1,0:T(8,128)(2,1)}) custom-call(s32[3]{0:T(128)} %pad_add_fusion.at, bf16[512,1536]{1,0:T(8,128)(2,1)} %bitcast.82, bf16[512,128]{1,0:T(8,128)(2,1)} %get-tuple-element.165.names_ref, bf16[32,1536]{1,0:T(8,128)(2,1)} %bitcast.103, ...), custom_call_target="tpu_custom_call" | custom-call | flops 1 | bytes 1 | tf_op jit(solution)/shard_map/pallas_call | solution.py:80
  214.4 7.3 %all-to-all-start.4 = ((bf16[16,32,1664]{2,1,0:T(8,128)(2,1)}), bf16[16,32,1664]{2,1,0:T(8,128)(2,1)S(1)}, u32[]{:S(2)}, u32[]{:S(2)}) async-start(bf16[16,32,1664]{2,1,0:T(8,128)(2,1)} %bitcast.110), calls=%async_computation.4 | async-start | bytes 3407872 | tf_op jit(solution)/shard_map/all_to_all | solution.py:59
  221.8 8.4 %shard_map.240 = bf16[4,1536,384]{2,1,0:T(8,128)(2,1)} custom-call(bf16[512,1536]{1,0:T(8,128)(2,1)} %bitcast.83, bf16[512,1536]{1,0:T(8,128)(2,1)} %bitcast.77, bf16[512,2048]{1,0:T(8,128)(2,1)} %get-tuple-element.170.pre_ref, bf16[512,1024]{1,0:T(8,128)(2,1)} %get-tuple-element.168.hidden_ref), custom_call_target="tpu_custom_call" | custom-call | flops 1 | bytes 1 | tf_op jit(solution)/shard_map/pallas_call | solution.py:80
  230.2 8.4 %shard_map.239 = bf16[4,1536,384]{2,1,0:T(8,128)(2,1)} custom-call(bf16[512,1536]{1,0:T(8,128)(2,1)} %bitcast.84, bf16[512,1536]{1,0:T(8,128)(2,1)} %bitcast.78, bf16[512,2048]{1,0:T(8,128)(2,1)} %get-tuple-element.170.pre_ref, bf16[512,1024]{1,0:T(8,128)(2,1)} %get-tuple-element.168.hidden_ref), custom_call_target="tpu_custom_call" | custom-call | flops 1 | bytes 1 | tf_op jit(solution)/shard_map/pallas_call | solution.py:80
  266.5 8.8 %shard_map.242 = (bf16[32,1536]{1,0:T(8,128)(2,1)}, bf16[32,1536]{1,0:T(8,128)(2,1)}, bf16[32,1536]{1,0:T(8,128)(2,1)}, bf16[32,1536]{1,0:T(8,128)(2,1)}, bf16[1...) custom-call(s32[3]{0:T(128)} %pad_add_fusion.at, bf16[32,1536]{1,0:T(8,128)(2,1)} %get-tuple-element.174.b0, ...), custom_call_target="tpu_custom_call" | custom-call | flops 1 | bytes 1 | tf_op jit(solution)/shard_map/pallas_call | solution.py:80
  292.9 6.9 %all-to-all-start.6 = ((bf16[16,32,1536]{2,1,0:T(8,128)(2,1)}), bf16[16,32,1536]{2,1,0:T(8,128)(2,1)S(1)}, u32[]{:S(2)}, u32[]{:S(2)}) async-start(bf16[16,32,1536]{2,1,0:T(8,128)(2,1)} %get-tuple-element.188), calls=%async_computation.6 | async-start | bytes 3145728 | tf_op jit(solution)/shard_map/all_to_all | solution.py:59
  324.6 8.2 %collective-permute-done.61 = bf16[768,384]{1,0:T(8,128)(2,1)S(1)} collective-permute-done((bf16[768,384]{1,0:T(8,128)(2,1)S(1)}, bf16[768,384]{1,0:T(8,128)(2,1)S(1)}, u32[]{:S(2)}, u32[]{:S(2)}) %collective-permute-start.61) | collective-permute-done | bytes 589856 | tf_op jit(solution)/shard_map/ppermute | solution.py:26
  333.6 6.9 %all-to-all-start.7 = ((bf16[16,48,1024]{2,1,0:T(8,128)(2,1)}), bf16[16,48,1024]{2,1,0:T(8,128)(2,1)S(1)}, u32[]{:S(2)}, u32[]{:S(2)}) async-start(bf16[16,48,1024]{2,1,0:T(8,128)(2,1)} %bitcast.88), calls=%async_computation.7 | async-start | bytes 3145728 | tf_op jit(solution)/shard_map/all_to_all | solution.py:59
  343.9 11.9 %shard_map.248 = (bf16[512,1664]{1,0:T(8,128)(2,1)}, bf16[512,2048]{1,0:T(8,128)(2,1)}, bf16[512,1024]{1,0:T(8,128)(2,1)}) custom-call(bf16[512,1536]{1,0:T(8,128)(2,1)} %bitcast.79, bf16[512,2048]{1,0:T(8,128)(2,1)} %get-tuple-element.200.pre_ref, f32[512,128]{1,0:T(8,128)} %get-tuple-element.201.gates_ref, bf16[768,384]{1,0:T(8,128)(2,1)} %get-tuple-element.151.refs_0_, ...), custom_call_target="tpu_custom_call" | custom-call | flops 1 | bytes 1 | tf_op jit(solution)/shard_map/pallas_call | solution.py:80
  375.8 8.4 %shard_map.250 = bf16[4,1536,384]{2,1,0:T(8,128)(2,1)} custom-call(bf16[512,1664]{1,0:T(8,128)(2,1)} %bitcast.74, bf16[512,1536]{1,0:T(8,128)(2,1)} %bitcast.80, bf16[512,2048]{1,0:T(8,128)(2,1)} %get-tuple-element.207.pre_ref, bf16[512,1024]{1,0:T(8,128)(2,1)} %get-tuple-element.208.hidden_ref), custom_call_target="tpu_custom_call" | custom-call | flops 1 | bytes 1 | tf_op jit(solution)/shard_map/pallas_call | solution.py:80
  384.2 8.5 %shard_map.249 = bf16[4,1536,384]{2,1,0:T(8,128)(2,1)} custom-call(bf16[512,1664]{1,0:T(8,128)(2,1)} %bitcast.75, bf16[512,1536]{1,0:T(8,128)(2,1)} %bitcast.81, bf16[512,2048]{1,0:T(8,128)(2,1)} %get-tuple-element.207.pre_ref, bf16[512,1024]{1,0:T(8,128)(2,1)} %get-tuple-element.208.hidden_ref), custom_call_target="tpu_custom_call" | custom-call | flops 1 | bytes 1 | tf_op jit(solution)/shard_map/pallas_call | solution.py:80
  403.2 7.3 %all-to-all-start.9 = ((bf16[16,48,512]{2,1,0:T(8,128)(2,1)}), bf16[16,48,512]{2,1,0:T(8,128)(2,1)S(1)}, u32[]{:S(2)}, u32[]{:S(2)}) async-start(bf16[16,48,512]{2,1,0:T(8,128)(2,1)} %broadcast_in_dim.11), calls=%async_computation.9 | async-start | bytes 1572864 | tf_op jit(solution)/shard_map/all_to_all | solution.py:59
  420.0 8.8 %shard_map.252 = (bf16[32,1536]{1,0:T(8,128)(2,1)}, bf16[32,1536]{1,0:T(8,128)(2,1)}, bf16[32,1536]{1,0:T(8,128)(2,1)}, bf16[32,1536]{1,0:T(8,128)(2,1)}, bf16[1...) custom-call(s32[3]{0:T(128)} %pad_add_fusion.at, bf16[32,1536]{1,0:T(8,128)(2,1)} %get-tuple-element.217.b0, ...), custom_call_target="tpu_custom_call" | custom-call | flops 1 | bytes 1 | tf_op jit(solution)/shard_map/pallas_call | solution.py:80
  434.0 7.1 %all-to-all-start.10 = ((bf16[16,48,512]{2,1,0:T(8,128)(2,1)}), bf16[16,48,512]{2,1,0:T(8,128)(2,1)S(1)}, u32[]{:S(2)}, u32[]{:S(2)}) async-start(bf16[16,48,512]{2,1,0:T(8,128)(2,1)} %broadcast_in_dim.12), calls=%async_computation.10 | async-start | bytes 1572864 | tf_op jit(solution)/shard_map/all_to_all | solution.py:59
  445.1 10.7 %all-to-all-done.10 = bf16[16,48,512]{2,1,0:T(8,128)(2,1)S(1)} async-done(((bf16[16,48,512]{2,1,0:T(8,128)(2,1)}), bf16[16,48,512]{2,1,0:T(8,128)(2,1)S(1)}, u32[]{:S(2)}, u32[]{:S(2)}) %all-to-all-start.10) | async-done | bytes 786464 | tf_op jit(solution)/shard_map/all_to_all | solution.py:59
  485.3 8.3 %collective-permute-done.84 = bf16[768,384]{1,0:T(8,128)(2,1)S(1)} collective-permute-done((bf16[768,384]{1,0:T(8,128)(2,1)}, bf16[768,384]{1,0:T(8,128)(2,1)S(1)}, u32[]{:S(2)}, u32[]{:S(2)}) %collective-permute-start.84) | collective-permute-done | bytes 589856 | tf_op jit(solution)/shard_map/ppermute | solution.py:26
  493.6 8.5 %collective-permute-done.83 = bf16[768,384]{1,0:T(8,128)(2,1)} collective-permute-done((bf16[768,384]{1,0:T(8,128)(2,1)}, bf16[768,384]{1,0:T(8,128)(2,1)}, u32[]{:S(2)}, u32[]{:S(2)}) %collective-permute-start.83) | collective-permute-done | bytes 589856 | tf_op jit(solution)/shard_map/ppermute | solution.py:26
  507.5 6.6 %all-to-all-start.12 = ((bf16[16,48,1280]{2,1,0:T(8,128)(2,1)}), bf16[16,48,1280]{2,1,0:T(8,128)(2,1)S(1)}, u32[]{:S(2)}, u32[]{:S(2)}) async-start(bf16[16,48,1280]{2,1,0:T(8,128)(2,1)} %broadcast_in_dim.13), calls=%async_computation.12 | async-start | bytes 3932160 | tf_op jit(solution)/shard_map/all_to_all | solution.py:59
  517.7 14.4 %collective-permute-done.85 = bf16[768,384]{1,0:T(8,128)(2,1)S(1)} collective-permute-done((bf16[768,384]{1,0:T(8,128)(2,1)}, bf16[768,384]{1,0:T(8,128)(2,1)S(1)}, u32[]{:S(2)}, u32[]{:S(2)}) %collective-permute-start.85) | collective-permute-done | bytes 589856 | tf_op jit(solution)/shard_map/ppermute | solution.py:26
  533.0 6.8 %collective-permute-done.86 = bf16[768,384]{1,0:T(8,128)(2,1)} collective-permute-done((bf16[768,384]{1,0:T(8,128)(2,1)}, bf16[768,384]{1,0:T(8,128)(2,1)}, u32[]{:S(2)}, u32[]{:S(2)}) %collective-permute-start.86) | collective-permute-done | bytes 589856 | tf_op jit(solution)/shard_map/ppermute | solution.py:26
  583.4 6.4 %shard_map.258 = (f32[1,1536,384]{2,1,0:T(8,128)}, f32[1,1536,128]{2,1,0:T(8,128)}, f32[1,1536,128]{2,1,0:T(8,128)}, f32[1,384,1536]{2,1,0:T(8,128)}) custom-call(s32[3]{0:T(128)} %pad_add_fusion.at, bf16[768,1280]{1,0:T(8,128)(2,1)} %bitcast.87, bf16[768,1024]{1,0:T(8,128)(2,1)} %pad_maximum_fusion.1.h1, bf16[768,1280]{1,0:T(8,128)(2,1)} %collective-permute-done.90.h2, ...), custom_call_target="tpu_custom_call" | custom-call | flops 1 | bytes 1 | tf_op jit(solution)/shard_map/pallas_call | solution.py:80
  (468 shorter events, 300.6 us)
Async XLA Ops:
  11.5 43.0 %all-to-all-start = ((bf16[16,32,1536]{2,1,0:T(8,128)(2,1)}), bf16[16,32,1536]{2,1,0:T(8,128)(2,1)S(1)}, u32[]{:S(2)}, u32[]{:S(2)}) async-start(bf16[16,32,1536]{2,1,0:T(8,128)(2,1)} %broadcast_in_dim.10), calls=%async_computation | async-start | bytes 3145728 | tf_op jit(solution)/shard_map/all_to_all | solution.py:59
  21.9 21.8 %collective-permute-start.12 = (bf16[768,384]{1,0:T(8,128)(2,1)}, bf16[768,384]{1,0:T(8,128)(2,1)}, u32[]{:S(2)}, u32[]{:S(2)}) collective-permute-start(bf16[768,384]{1,0:T(8,128)(2,1)} %get-tuple-element.151.refs_0_), channel_id=1, source_target_pairs={{0,3},{1,0},{2,1},{3,2},{4,7},{5,4},{6,5},{7,6},{8,11},{9,8},{10,9... | collective-permute-start | bytes 1769480 | tf_op jit(solution)/shard_map/ppermute | solution.py:26
  46.2 25.6 %collective-permute-start.16 = (bf16[768,384]{1,0:T(8,128)(2,1)}, bf16[768,384]{1,0:T(8,128)(2,1)}, u32[]{:S(2)}, u32[]{:S(2)}) collective-permute-start(bf16[768,384]{1,0:T(8,128)(2,1)} %collective-permute-done.12.refs_2_), channel_id=1, source_target_pairs={{0,3},{1,0},{2,1},{3,2},{4,7},{5,4},{6,5},{7,6},{8,11},{9,8},{10,9... | collective-permute-start | bytes 1769480 | tf_op jit(solution)/shard_map/ppermute | solution.py:26
  46.3 25.6 %collective-permute-start.17 = (bf16[768,384]{1,0:T(8,128)(2,1)}, bf16[768,384]{1,0:T(8,128)(2,1)}, u32[]{:S(2)}, u32[]{:S(2)}) collective-permute-start(bf16[768,384]{1,0:T(8,128)(2,1)} %collective-permute-done.15.refs_5_), channel_id=1, source_target_pairs={{0,1},{1,2},{2,3},{3,0},{4,5},{5,6},{6,7},{7,4},{8,9},{9,10},{10,1... | collective-permute-start | bytes 1769480 | tf_op jit(solution)/shard_map/ppermute | solution.py:26
  55.7 33.2 %all-to-all-start.1 = ((bf16[16,32,1664]{2,1,0:T(8,128)(2,1)}), bf16[16,32,1664]{2,1,0:T(8,128)(2,1)S(1)}, u32[]{:S(2)}, u32[]{:S(2)}) async-start(bf16[16,32,1664]{2,1,0:T(8,128)(2,1)} %get-tuple-element.149), calls=%async_computation.1 | async-start | bytes 3407872 | tf_op jit(solution)/shard_map/all_to_all | solution.py:59
  101.7 27.8 %all-to-all-start.2 = ((bf16[16,32,1536]{2,1,0:T(8,128)(2,1)}), bf16[16,32,1536]{2,1,0:T(8,128)(2,1)S(1)}, u32[]{:S(2)}, u32[]{:S(2)}) async-start(bf16[16,32,1536]{2,1,0:T(8,128)(2,1)} %bitcast.111), calls=%async_computation.2 | async-start | bytes 3145728 | tf_op jit(solution)/shard_map/all_to_all | solution.py:59
  161.0 36.4 %all-to-all-start.3 = ((bf16[16,32,1536]{2,1,0:T(8,128)(2,1)}), bf16[16,32,1536]{2,1,0:T(8,128)(2,1)S(1)}, u32[]{:S(2)}, u32[]{:S(2)}) async-start(bf16[16,32,1536]{2,1,0:T(8,128)(2,1)} %get-tuple-element.164), calls=%async_computation.3 | async-start | bytes 3145728 | tf_op jit(solution)/shard_map/all_to_all | solution.py:59
  166.7 28.7 %collective-permute-start.37 = (bf16[768,384]{1,0:T(8,128)(2,1)S(1)}, bf16[768,384]{1,0:T(8,128)(2,1)S(1)}, u32[]{:S(2)}, u32[]{:S(2)}) collective-permute-start(bf16[768,384]{1,0:T(8,128)(2,1)S(1)} %copy-done.16), channel_id=1, source_target_pairs={{0,2},{1,3},{2,0},{3,1},{4,6},{5,7},{6,4},{7,5},{8,10},{9,11},{10,... | collective-permute-start | bytes 1769480 | tf_op jit(solution)/shard_map/ppermute | solution.py:26
  169.1 26.3 %collective-permute-start.40 = (bf16[768,384]{1,0:T(8,128)(2,1)}, bf16[768,384]{1,0:T(8,128)(2,1)S(1)}, u32[]{:S(2)}, u32[]{:S(2)}) collective-permute-start(bf16[768,384]{1,0:T(8,128)(2,1)} %collective-permute-done.26.refs_2_), channel_id=1, source_target_pairs={{0,64},{64,0},{1,65},{65,1},{2,66},{66,2},{3,67},{67,3},{4,68},{68... | collective-permute-start | bytes 1769480 | tf_op jit(solution)/shard_map/ppermute | solution.py:26
  169.2 26.3 %collective-permute-start.43 = (bf16[768,384]{1,0:T(8,128)(2,1)S(1)}, bf16[768,384]{1,0:T(8,128)(2,1)S(1)}, u32[]{:S(2)}, u32[]{:S(2)}) collective-permute-start(bf16[768,384]{1,0:T(8,128)(2,1)S(1)} %collective-permute-done.29.refs_5_), channel_id=1, source_target_pairs={{0,64},{64,0},{1,65},{65,1},{2,66},{66,2},{3,67},{67,3},{4,68},{68... | collective-permute-start | bytes 1769480 | tf_op jit(solution)/shard_map/ppermute | solution.py:26
  169.7 25.7 %collective-permute-start.41 = (bf16[768,384]{1,0:T(8,128)(2,1)}, bf16[768,384]{1,0:T(8,128)(2,1)S(1)}, u32[]{:S(2)}, u32[]{:S(2)}) collective-permute-start(bf16[768,384]{1,0:T(8,128)(2,1)} %copy-done.29), channel_id=1, source_target_pairs={{0,64},{64,0},{1,65},{65,1},{2,66},{66,2},{3,67},{67,3},{4,68},{68... | collective-permute-start | bytes 1769480 | tf_op jit(solution)/shard_map/ppermute | solution.py:26
  214.4 33.3 %all-to-all-start.4 = ((bf16[16,32,1664]{2,1,0:T(8,128)(2,1)}), bf16[16,32,1664]{2,1,0:T(8,128)(2,1)S(1)}, u32[]{:S(2)}, u32[]{:S(2)}) async-start(bf16[16,32,1664]{2,1,0:T(8,128)(2,1)} %bitcast.110), calls=%async_computation.4 | async-start | bytes 3407872 | tf_op jit(solution)/shard_map/all_to_all | solution.py:59
  252.1 58.2 %collective-permute-start.57 = (bf16[4,1536,384]{2,1,0:T(8,128)(2,1)}, bf16[4,1536,384]{2,1,0:T(8,128)(2,1)}, u32[]{:S(2)}, u32[]{:S(2)}) collective-permute-start(bf16[4,1536,384]{2,1,0:T(8,128)(2,1)} %shard_map.240), channel_id=1, source_target_pairs={{0,64},{64,0},{1,65},{65,1},{2,66},{66,2},{3,67},{67,3},{4,68},{68... | collective-permute-start | bytes 14155784 | tf_op jit(solution)/shard_map/ppermute | solution.py:26
  252.2 39.6 %all-to-all-start.5 = ((bf16[16,32,1536]{2,1,0:T(8,128)(2,1)}), bf16[16,32,1536]{2,1,0:T(8,128)(2,1)S(1)}, u32[]{:S(2)}, u32[]{:S(2)}) async-start(bf16[16,32,1536]{2,1,0:T(8,128)(2,1)} %bitcast.89), calls=%async_computation.5 | async-start | bytes 3145728 | tf_op jit(solution)/shard_map/all_to_all | solution.py:59
  278.9 42.5 %collective-permute-start.56 = (bf16[768,1024]{1,0:T(8,128)(2,1)}, bf16[768,1024]{1,0:T(8,128)(2,1)}, u32[]{:S(2)}, u32[]{:S(2)}) collective-permute-start(bf16[768,1024]{1,0:T(8,128)(2,1)} %get-tuple-element.194), channel_id=1, source_target_pairs={{0,64},{64,0},{1,65},{65,1},{2,66},{66,2},{3,67},{67,3},{4,68},{68... | collective-permute-start | bytes 4718600 | tf_op jit(solution)/shard_map/ppermute | solution.py:26
  292.9 31.7 %all-to-all-start.6 = ((bf16[16,32,1536]{2,1,0:T(8,128)(2,1)}), bf16[16,32,1536]{2,1,0:T(8,128)(2,1)S(1)}, u32[]{:S(2)}, u32[]{:S(2)}) async-start(bf16[16,32,1536]{2,1,0:T(8,128)(2,1)} %get-tuple-element.188), calls=%async_computation.6 | async-start | bytes 3145728 | tf_op jit(solution)/shard_map/all_to_all | solution.py:59
  333.6 27.4 %all-to-all-start.7 = ((bf16[16,48,1024]{2,1,0:T(8,128)(2,1)}), bf16[16,48,1024]{2,1,0:T(8,128)(2,1)S(1)}, u32[]{:S(2)}, u32[]{:S(2)}) async-start(bf16[16,48,1024]{2,1,0:T(8,128)(2,1)} %bitcast.88), calls=%async_computation.7 | async-start | bytes 3145728 | tf_op jit(solution)/shard_map/all_to_all | solution.py:59
  340.6 21.4 %collective-permute-start.63 = (bf16[768,384]{1,0:T(8,128)(2,1)}, bf16[768,384]{1,0:T(8,128)(2,1)S(1)}, u32[]{:S(2)}, u32[]{:S(2)}) collective-permute-start(bf16[768,384]{1,0:T(8,128)(2,1)} %get-tuple-element.204), channel_id=1, source_target_pairs={{0,1},{1,2},{2,3},{3,0},{4,5},{5,6},{6,7},{7,4},{8,9},{9,10},{10,1... | collective-permute-start | bytes 1769480 | tf_op jit(solution)/shard_map/ppermute | solution.py:26
  363.0 34.6 %all-to-all-start.8 = ((bf16[16,32,1664]{2,1,0:T(8,128)(2,1)}), bf16[16,32,1664]{2,1,0:T(8,128)(2,1)S(1)}, u32[]{:S(2)}, u32[]{:S(2)}) async-start(bf16[16,32,1664]{2,1,0:T(8,128)(2,1)} %bitcast.109), calls=%async_computation.8 | async-start | bytes 3407872 | tf_op jit(solution)/shard_map/all_to_all | solution.py:59
  366.8 25.9 %collective-permute-start.65 = (bf16[768,384]{1,0:T(8,128)(2,1)S(1)}, bf16[768,384]{1,0:T(8,128)(2,1)}, u32[]{:S(2)}, u32[]{:S(2)}) collective-permute-start(bf16[768,384]{1,0:T(8,128)(2,1)S(1)} %copy-done.50), channel_id=1, source_target_pairs={{0,2},{1,3},{2,0},{3,1},{4,6},{5,7},{6,4},{7,5},{8,10},{9,11},{10,... | collective-permute-start | bytes 1769480 | tf_op jit(solution)/shard_map/ppermute | solution.py:26
  370.1 25.3 %collective-permute-start.66 = (bf16[768,384]{1,0:T(8,128)(2,1)S(1)}, bf16[768,384]{1,0:T(8,128)(2,1)}, u32[]{:S(2)}, u32[]{:S(2)}) collective-permute-start(bf16[768,384]{1,0:T(8,128)(2,1)S(1)} %copy-done.49), channel_id=1, source_target_pairs={{0,2},{1,3},{2,0},{3,1},{4,6},{5,7},{6,4},{7,5},{8,10},{9,11},{10,... | collective-permute-start | bytes 1769480 | tf_op jit(solution)/shard_map/ppermute | solution.py:26
  402.0 69.8 %collective-permute-start.80 = (bf16[4,1536,384]{2,1,0:T(8,128)(2,1)}, bf16[4,1536,384]{2,1,0:T(8,128)(2,1)}, u32[]{:S(2)}, u32[]{:S(2)}) collective-permute-start(bf16[4,1536,384]{2,1,0:T(8,128)(2,1)} %shard_map.250), channel_id=1, source_target_pairs={{0,64},{64,0},{1,65},{65,1},{2,66},{66,2},{3,67},{67,3},{4,68},{68... | collective-permute-start | bytes 14155784 | tf_op jit(solution)/shard_map/ppermute | solution.py:26
  403.2 25.7 %all-to-all-start.9 = ((bf16[16,48,512]{2,1,0:T(8,128)(2,1)}), bf16[16,48,512]{2,1,0:T(8,128)(2,1)S(1)}, u32[]{:S(2)}, u32[]{:S(2)}) async-start(bf16[16,48,512]{2,1,0:T(8,128)(2,1)} %broadcast_in_dim.11), calls=%async_computation.9 | async-start | bytes 1572864 | tf_op jit(solution)/shard_map/all_to_all | solution.py:59
  434.0 21.8 %all-to-all-start.10 = ((bf16[16,48,512]{2,1,0:T(8,128)(2,1)}), bf16[16,48,512]{2,1,0:T(8,128)(2,1)S(1)}, u32[]{:S(2)}, u32[]{:S(2)}) async-start(bf16[16,48,512]{2,1,0:T(8,128)(2,1)} %broadcast_in_dim.12), calls=%async_computation.10 | async-start | bytes 1572864 | tf_op jit(solution)/shard_map/all_to_all | solution.py:59
  456.7 28.4 %all-to-all-start.11 = ((bf16[16,48,1152]{2,1,0:T(8,128)(2,1)}), bf16[16,48,1152]{2,1,0:T(8,128)(2,1)S(1)}, u32[]{:S(2)}, u32[]{:S(2)}) async-start(bf16[16,48,1152]{2,1,0:T(8,128)(2,1)} %bitcast.35), calls=%async_computation.11 | async-start | bytes 3538944 | tf_op jit(solution)/shard_map/all_to_all | solution.py:59
  479.1 23.1 %collective-permute-start.83 = (bf16[768,384]{1,0:T(8,128)(2,1)}, bf16[768,384]{1,0:T(8,128)(2,1)}, u32[]{:S(2)}, u32[]{:S(2)}) collective-permute-start(bf16[768,384]{1,0:T(8,128)(2,1)} %get-tuple-element.261), channel_id=1, source_target_pairs={{0,3},{1,0},{2,1},{3,2},{4,7},{5,4},{6,5},{7,6},{8,11},{9,8},{10,9... | collective-permute-start | bytes 1769480 | tf_op jit(solution)/shard_map/ppermute | solution.py:26
  479.2 22.9 %collective-permute-start.82 = (bf16[768,384]{1,0:T(8,128)(2,1)}, bf16[768,384]{1,0:T(8,128)(2,1)}, u32[]{:S(2)}, u32[]{:S(2)}) collective-permute-start(bf16[768,384]{1,0:T(8,128)(2,1)} %get-tuple-element.262), channel_id=1, source_target_pairs={{0,1},{1,2},{2,3},{3,0},{4,5},{5,6},{6,7},{7,4},{8,9},{9,10},{10,1... | collective-permute-start | bytes 1769480 | tf_op jit(solution)/shard_map/ppermute | solution.py:26
  481.1 25.0 %collective-permute-start.81 = (bf16[768,384]{1,0:T(8,128)(2,1)}, bf16[768,384]{1,0:T(8,128)(2,1)}, u32[]{:S(2)}, u32[]{:S(2)}) collective-permute-start(bf16[768,384]{1,0:T(8,128)(2,1)} %get-tuple-element.263), channel_id=1, source_target_pairs={{0,1},{1,2},{2,3},{3,0},{4,5},{5,6},{6,7},{7,4},{8,9},{9,10},{10,1... | collective-permute-start | bytes 1769480 | tf_op jit(solution)/shard_map/ppermute | solution.py:26
  507.5 32.3 %all-to-all-start.12 = ((bf16[16,48,1280]{2,1,0:T(8,128)(2,1)}), bf16[16,48,1280]{2,1,0:T(8,128)(2,1)S(1)}, u32[]{:S(2)}, u32[]{:S(2)}) async-start(bf16[16,48,1280]{2,1,0:T(8,128)(2,1)} %broadcast_in_dim.13), calls=%async_computation.12 | async-start | bytes 3932160 | tf_op jit(solution)/shard_map/all_to_all | solution.py:59
  514.4 25.4 %collective-permute-start.86 = (bf16[768,384]{1,0:T(8,128)(2,1)}, bf16[768,384]{1,0:T(8,128)(2,1)}, u32[]{:S(2)}, u32[]{:S(2)}) collective-permute-start(bf16[768,384]{1,0:T(8,128)(2,1)} %get-tuple-element.244), channel_id=1, source_target_pairs={{0,2},{1,3},{2,0},{3,1},{4,6},{5,7},{6,4},{7,5},{8,10},{9,11},{10,... | collective-permute-start | bytes 1769480 | tf_op jit(solution)/shard_map/ppermute | solution.py:26
  539.8 43.6 %collective-permute-start.90 = (bf16[768,1280]{1,0:T(8,128)(2,1)S(1)}, bf16[768,1280]{1,0:T(8,128)(2,1)}, u32[]{:S(2)}, u32[]{:S(2)}) collective-permute-start(bf16[768,1280]{1,0:T(8,128)(2,1)S(1)} %bitcast.85), channel_id=1, source_target_pairs={{64,0},{65,1},{66,2},{67,3},{68,4},{69,5},{70,6},{71,7},{72,8},{73... | collective-permute-start | bytes 5898248 | tf_op jit(solution)/shard_map/ppermute | solution.py:34
  547.1 36.3 %collective-permute-start.91 = (bf16[768,1024]{1,0:T(8,128)(2,1)}, bf16[768,1024]{1,0:T(8,128)(2,1)}, u32[]{:S(2)}, u32[]{:S(2)}) collective-permute-start(bf16[768,1024]{1,0:T(8,128)(2,1)} %pad_maximum_fusion.1.h1), channel_id=1, source_target_pairs={{0,64},{1,65},{2,66},{3,67},{4,68},{5,69},{6,70},{7,71},{8,72},{9,... | collective-permute-start | bytes 4718600 | tf_op jit(solution)/shard_map/ppermute | solution.py:34
  (187 other events, 1471.8 us)

commit v3 on v2

--- a/solution.py
+++ b/solution.py
@@ -41,6 +41,18 @@
 def gather_x(block):
     ahead = {k: shifted(block, "tensor", -k) for k in (1, 3, 2)}
     return [block, ahead[1], ahead[2], ahead[3]]
+
+
+def start_gather(upper, lower):
+    return shifted(upper, "tensor", -1), shifted(lower, "tensor", 1)
+
+
+def end_gather(block, one, three):
+    part = block.shape[0] // 4
+    return (
+        shifted(jnp.concatenate([block[3 * part :], one[: 2 * part]], axis=0), "tensor", -1),
+        shifted(jnp.concatenate([block[:part], three[part:]], axis=0), "tensor", 1),
+    )
 
 
 def arrivals(blocks):
@@ -371,40 +383,70 @@
 
 def prepare_experts(place, w_gate, w_up, w_down):
     _, width, deep = w_gate.shape
-    half = width // 2
-
-    def kernel(at, gate, up, down, kept_low, kept_high, given_low, given_high):
-        for outs, which in (((given_low, given_high), 1 - at[0]), ((kept_low, kept_high), at[0])):
-            for out, start in zip(outs, (0, half)):
-                out[:, :deep] = gate[which, start : start + half, :]
-                out[:, deep : 2 * deep] = up[which, start : start + half, :]
-                out[:, 2 * deep :] = down[which, :, start : start + half].T
-
-    results = call(
-        kernel,
-        [((half, 3 * deep), BF)] * 4,
+
+    def kernel(at, gate, up, down, kept, given):
+        for out, which in ((given, 1 - at[0]), (kept, at[0])):
+            out[:, :deep] = gate[which]
+            out[:, deep : 2 * deep] = up[which]
+            out[:, 2 * deep :] = down[which].T
+
+    return call(
+        kernel,
+        [((width, 3 * deep), BF)] * 2,
         [place, w_gate, w_up, w_down],
         [SCALARS] + [WHOLE] * 3,
     )
-    return results[:2], results[2:]
+
+
+def choose_experts(place, kept, given, layer):
+    width, cols = kept.shape
+    part = width // 4
+
+    def kernel(at, kept_ref, given_ref, whole, upper, lower):
+        def store(ref):
+            whole[...] = ref[...]
+            upper[...] = ref[: 3 * part, :]
+            lower[...] = ref[part:, :]
+
+        pl.when(at[0] == layer)(lambda: store(kept_ref))
+        pl.when(at[0] != layer)(lambda: store(given_ref))
+
+    return call(
+        kernel,
+        [((width, cols), BF), ((3 * part, cols), BF), ((3 * part, cols), BF)],
+        [place, kept, given],
+        [SCALARS] + [WHOLE] * 2,
+    )
 
 
 def load_experts(refs, gate_up, down, sems):
     each = len(refs) // 2
     width, deep = down.shape[0], refs[0].shape[1] // 3
-    half = width // 2
-    spots = [(block, low, low + half) for block in (0, 1, 3, 2) for low in (0, half)]
+    part = width // 4
+    spots = [
+        [(0, (0, width), 0)],
+        [(1, (0, 3 * part), 0)],
+        [(3, (part, 3 * part), 0)],
+        [(1, (3 * part, part), 0), (2, (0, 2 * part), part)],
+        [(3, (0, part), 0), (2, (2 * part, 2 * part), part)],
+    ]
     up_copies, down_copies = [[], []], [[], []]
     sem = 0
     for k in range(2):
-        for ref, (block, low, high) in zip(refs[each * k : each * (k + 1)], spots):
-            at = 4 * k + block
-            if gate_up is not None:
-                target = gate_up.at[low:high, 2 * deep * at : 2 * deep * (at + 1)]
-                up_copies[k].append(pltpu.make_async_copy(ref.at[:, : 2 * deep], target, sems.at[sem]))
-            target = down.at[low:high, deep * at : deep * (at + 1)]
-            down_copies[k].append(pltpu.make_async_copy(ref.at[:, 2 * deep :], target, sems.at[sem + 1]))
-            sem += 2
+        for ref, pieces in zip(refs[each * k : each * (k + 1)], spots):
+            for block, (start, count), source in pieces:
+                at = 4 * k + block
+                rows, taken = slice(start, start + count), slice(source, source + count)
+                if gate_up is not None:
+                    target = gate_up.at[rows, 2 * deep * at : 2 * deep * (at + 1)]
+                    up_copies[k].append(
+                        pltpu.make_async_copy(ref.at[taken, : 2 * deep], target, sems.at[sem])
+                    )
+                target = down.at[rows, deep * at : deep * (at + 1)]
+                down_copies[k].append(
+                    pltpu.make_async_copy(ref.at[taken, 2 * deep :], target, sems.at[sem + 1])
+                )
+                sem += 2
     return up_copies, down_copies
 
 
@@ -520,7 +562,7 @@
             pltpu.VMEM((width, 16 * deep), BF),
             pltpu.VMEM((width, 8 * deep), BF),
             pltpu.VMEM((count, 8 * deep), BF),
-            pltpu.SemaphoreType.DMA((2 * used,)),
+            pltpu.SemaphoreType.DMA((28,)),
         ],
     )
 
@@ -550,7 +592,7 @@
         [
             pltpu.VMEM((width, 16 * deep), BF),
             pltpu.VMEM((width, 8 * deep), BF),
-            pltpu.SemaphoreType.DMA((2 * used,)),
+            pltpu.SemaphoreType.DMA((28,)),
         ],
     )
 
@@ -593,14 +635,14 @@
             pltpu.VMEM((width, 8 * deep), BF),
             pltpu.VMEM((count, 16 * deep), F32),
             pltpu.VMEM((count, 128), F32),
-            pltpu.SemaphoreType.DMA((2 * used,)),
+            pltpu.SemaphoreType.DMA((28,)),
         ],
     )
 
 
 def experts_out(hidden, weights):
     count = hidden.shape[0]
-    width, deep = 2 * weights[0].shape[0], weights[0].shape[1] // 3
+    width, deep = weights[0].shape[0], weights[0].shape[1] // 3
     used = len(weights)
 
     def kernel(hidden_ref, *refs):
@@ -615,67 +657,73 @@
         [((count, width), BF)],
         [hidden, *weights],
         [WHOLE] + [ANY] * used,
-        [pltpu.VMEM((width, 8 * deep), BF), pltpu.SemaphoreType.DMA((2 * used,))],
+        [pltpu.VMEM((width, 8 * deep), BF), pltpu.SemaphoreType.DMA((28,))],
     )[0]
 
 
-def experts_grads(rows, back, back_pre, hidden, which):
+def experts_grads(rows, back, back_pre, hidden):
     count, width = back.shape
     deep = hidden.shape[1] // 8
 
-    def kernel(x, back_ref, pre_ref, hidden_ref, out, rows_turned, back_turned):
-        @pl.when(pl.program_id(0) == 0)
+    def kernel(x, back_ref, pre_ref, hidden_ref, mine, other, rows_turned, back_turned):
+        step = pl.program_id(0)
+
+        @pl.when(step == 0)
         def _():
             rows_turned[...] = x[:, :width].T
             back_turned[...] = back_ref[...].T
 
-        for a in range(0, width, 512):
-            out[0, a : a + 512, : 2 * deep] = dot(rows_turned[a : a + 512, :], pre_ref[...]).astype(BF)
-            out[0, a : a + 512, 2 * deep :] = dot(back_turned[a : a + 512, :], hidden_ref[...]).astype(BF)
-
-    return call(
-        kernel,
-        [((4, width, 3 * deep), BF)],
+        def store(out):
+            for a in range(0, width, 512):
+                out[0, a : a + 512, : 2 * deep] = dot(rows_turned[a : a + 512, :], pre_ref[...]).astype(BF)
+                out[0, a : a + 512, 2 * deep :] = dot(back_turned[a : a + 512, :], hidden_ref[...]).astype(BF)
+
+        pl.when(step < 4)(lambda: store(other))
+        pl.when(step >= 4)(lambda: store(mine))
+
+    return call(
+        kernel,
+        [((4, width, 3 * deep), BF)] * 2,
         [rows, back, back_pre, hidden],
         [
             WHOLE,
             WHOLE,
-            pl.BlockSpec((count, 2 * deep), lambda i: (0, i + 4 * which)),
-            pl.BlockSpec((count, deep), lambda i: (0, i + 4 * which)),
+            pl.BlockSpec((count, 2 * deep), lambda i: (0, (i + 4) % 8)),
+            pl.BlockSpec((count, deep), lambda i: (0, (i + 4) % 8)),
         ],
         [pltpu.VMEM((width, count), BF)] * 2,
-        grid=(4,),
-        out_specs=[pl.BlockSpec((1, width, 3 * deep), lambda i: (i, 0, 0))],
-    )[0]
+        grid=(8,),
+        out_specs=[
+            pl.BlockSpec((1, width, 3 * deep), lambda i: (jnp.maximum(i - 4, 0), 0, 0)),
+            pl.BlockSpec((1, width, 3 * deep), lambda i: (jnp.minimum(i, 3), 0, 0)),
+        ],
+    )
 
 
 def experts_finish(place, sums):
-    half, deep = sums[0].shape[0], sums[0].shape[1] // 3
-
-    def kernel(at, *refs):
-        sums, (grad_gate, grad_up, grad_down) = refs[:8], refs[8:]
-
-        def store(halves, which):
-            for ref, rows in zip(halves, (slice(0, half), slice(half, 2 * half))):
-                grad_gate[0, which, rows, :] = ref[:, :deep].astype(F32)
-                grad_up[0, which, rows, :] = ref[:, deep : 2 * deep].astype(F32)
-                grad_down[0, which, :, rows] = ref[:, 2 * deep :].astype(F32).T
+    width, deep = sums[0].shape[0], sums[0].shape[1] // 3
+
+    def kernel(at, s0, s1, s2, s3, grad_gate, grad_up, grad_down):
+        def store(ref, which):
+            grad_gate[0, which] = ref[:, :deep].astype(F32)
+            grad_up[0, which] = ref[:, deep : 2 * deep].astype(F32)
+            grad_down[0, which] = ref[:, 2 * deep :].astype(F32).T
 
         @pl.when(at[0] == 0)
         def _():
-            store(sums[0:2], 0)
-            store(sums[4:6], 1)
+            store(s0, 0)
+            store(s2, 1)
 
         @pl.when(at[0] == 1)
         def _():
-            store(sums[2:4], 1)
-            store(sums[6:8], 0)
-
-    return call(
-        kernel,
-        [((1, 2, 2 * half, deep), F32)] * 2 + [((1, 2, deep, 2 * half), F32)],
+            store(s1, 1)
+            store(s3, 0)
+
+    return call(
+        kernel,
+        [((1, 2, width, deep), F32)] * 2 + [((1, 2, deep, width), F32)],
         [place, *sums],
-        [SCALARS] + [WHOLE] * 8,
+        [SCALARS] + [WHOLE] * 4,
     )
 
 
@@ -713,16 +761,21 @@
     )
 
 
-def leave_rows(middle, pieces):
+def leave_rows(middle, pieces, beside=()):
     share, width = middle.shape
-
-    def kernel(middle_ref, pieces_ref, out):
+    extra = len(beside)
+
+    def kernel(middle_ref, pieces_ref, *refs):
         total = middle_ref[...]
         for k in range(pieces_ref.shape[0]):
             total = total + pieces_ref[k].astype(F32)
-        out[...] = total.astype(BF)
-
-    return call(kernel, [((share, width), BF)], [middle, pieces], [WHOLE] * 2)[0]
+        refs[-1][:share, :] = total.astype(BF)
+        for k in range(extra):
+            refs[-1][share * (k + 1) : share * (k + 2), :] = refs[k][...]
+
+    return call(
+        kernel, [((share * (1 + extra), width), BF)], [middle, pieces, *beside], [WHOLE] * (2 + extra)
+    )[0]
 
 
 def back_middle_rows(flow, pieces, middle, shaped, gates, gain, router, place, layer):
@@ -765,56 +818,76 @@
     )
 
 
-def back_entry_rows(back, pieces, entry, gain, place, layer, copies):
+def back_entry_rows(back, pieces, entry, gain, place, layer, copies, beside=()):
     share, width = back.shape
-
-    def kernel(at, back_ref, a, b, c, d, entry_ref, gain_own, gain_other, out, grad_gain, *more):
+    extra = sum(rows.shape[0] for rows in beside)
+
+    def kernel(at, back_ref, a, b, c, d, entry_ref, gain_own, gain_other, *refs):
+        more, (out, grad_gain, *spread) = refs[: len(beside)], refs[len(beside) :]
         total = a[...].astype(F32) + b[...].astype(F32) + c[...].astype(F32) + d[...].astype(F32)
         level, grad = norm_back(
             total, entry_ref[...].astype(F32), of_layer(layer, at[0], gain_own, gain_other)
         )
         flow = (back_ref[...] + level).astype(BF)
-        out[...] = flow
+        out[:share, :] = flow
+        start = share
+        for ref in more:
+            out[start : start + ref.shape[0], :] = ref[...]
+            start += ref.shape[0]
         grad_gain[...] = grad
-        for ref in more:
+        for ref in spread:
             for k in range(copies):
                 ref[k] = flow
 
-    outs = [((share, width), BF), ((1, width), F32)]
+    outs = [((share + extra, width), BF), ((1, width), F32)]
     if copies:
         outs.append(((copies, share, width), BF))
     return call(
-        kernel, outs, [place, back, *pieces, entry, *gain], [SCALARS] + [WHOLE] * 8
-    )
-
-
-def straight_rows(place, of_first, of_second):
-    share, width = of_first[0].shape
+        kernel,
+        outs,
+        [place, back, *pieces, entry, *gain, *beside],
+        [SCALARS] + [WHOLE] * (8 + len(beside)),
+    )
+
+
+def straight_rows(place, entered, final):
+    share, width = entered[0].shape
+    rows = 4 * share
 
     def kernel(at, *refs):
-        blocks, (own, other) = refs[:8], refs[8:]
+        blocks, finals, (own, other) = refs[:4], refs[4:8], refs[8:]
+        here = at[0] == 0
         for k in range(4):
-            rows = pl.ds(pl.multiple_of(share * lax.rem(at[1] + k, 4), share), share)
-            here = at[0] == 0
-            own[rows, :] = jnp.where(here, blocks[k][...].astype(F32), blocks[4 + k][...].astype(F32)).astype(BF)
-            other[rows, :] = jnp.where(here, blocks[4 + k][...].astype(F32), blocks[k][...].astype(F32)).astype(BF)
-
-    return call(
-        kernel,
-        [((4 * share, width), BF)] * 2,
-        [place, *of_first, *of_second],
+            start = share * lax.rem(at[1] + k, 4)
+            values = blocks[k][...].astype(F32), finals[k][...].astype(F32)
+            pairs = (
+                (values[0], values[1][share : 2 * share]),
+                (values[1][:share], values[1][2 * share :]),
+            )
+            for n, (zero, one) in enumerate(pairs):
+                spot = pl.ds(pl.multiple_of(rows * n + start, share), share)
+                own[spot, :] = jnp.where(here, zero, one).astype(BF)
+                other[spot, :] = jnp.where(here, one, zero).astype(BF)
+
+    return call(
+        kernel,
+        [((2 * rows, width), BF)] * 2,
+        [place, *entered, *final],
         [SCALARS] + [WHOLE] * 8,
     )
 
 
 def by_batch(place, own, other):
-    rows, width = own.shape
-
-    def kernel(at, own_ref, other_ref, out):
-        out[0, at[0]] = own_ref[...]
-        out[0, 1 - at[0]] = other_ref[...]
-
-    return call(kernel, [((1, 2, rows, width), BF)], [place, own, other], [SCALARS] + [WHOLE] * 2)[0]
+    rows, width = own.shape[0] // 2, own.shape[1]
+
+    def kernel(at, own_ref, other_ref, activations, input_grads):
+        for n, out in enumerate((activations, input_grads)):
+            out[0, at[0]] = own_ref[rows * n : rows * (n + 1), :]
+            out[0, 1 - at[0]] = other_ref[rows * n : rows * (n + 1), :]
+
+    return call(
+        kernel, [((1, 2, rows, width), BF)] * 2, [place, own, other], [SCALARS] + [WHOLE] * 2
+    )
 
 
 def per_device(
@@ -849,9 +922,9 @@
         return lax.dynamic_slice(array, start, (1, share, array.shape[2]))[0]
 
     kept, given = prepare_experts(place, w_gate[0], w_up[0], w_down[0])
-    given = [sibling(half) for half in given]
-    low, high = (jnp.where(first, a, b) for a, b in zip(kept, given))
-    one_low, three_high = shifted(low, "tensor", -1), shifted(high, "tensor", 1)
+    given = sibling(given)
+    quarter, *parts = choose_experts(place, kept, given, 0)
+    sides = start_gather(*parts)
     weights = own_weights + [sibling(w) for w in own_weights]
 
     gains_a = [gain_attn, sibling(gain_attn)]
@@ -860,41 +933,33 @@
     tables = prepare_tables(place, documents, w_query.shape[2] + w_key.shape[2])
     names_own = own_rows(routes)
     top = routes.shape[2]
-    flow = after(own_rows(cotangent), low, high)
-    backs = [None, spread_e(flow).reshape(-1, width)]
+    flow = own_rows(cotangent)
 
     entry = [own_rows(inputs), None]
     attn_saved, middles, shapeds, gates_own, arrived = ([None, None] for _ in range(5))
-    pieces, attn_saved[0] = attention_forward([after(inputs, low, high)], tables, weights, gains_a, place, 0)
-    pieces = arrivals(pieces)
+    pieces, attn_saved[0] = attention_forward([after(inputs, quarter)], tables, weights, gains_a, place, 0)
+    pieces = arrivals(after(pieces, *sides))
     middles[0], copies, shapeds[0], gates_own[0] = middle_rows(
         entry[0], pieces, gains_m, names_own, routers, place, 0, sequences
     )
-    one_high = shifted(after(high, *pieces), "tensor", -1)
-    three_low = shifted(after(low, *pieces), "tensor", 1)
-    two_low = shifted(after(one_low, *pieces), "tensor", -1)
-    two_high = shifted(after(three_high, *pieces), "tensor", 1)
-    mine = [low, high, one_low, one_high, three_low, three_high, two_low, two_high]
+    mine = [quarter, *sides, *end_gather(after(quarter, *pieces), *sides)]
     expert_weights = [[*mine, *[sibling(block) for block in mine]], None]
-    copies = after(copies, backs[1])
     arrived[0] = exchange_e(copies).reshape(-1, width + BESIDE)
-    low, high = (jnp.where(first, b, a) for a, b in zip(kept, given))
-    low, high = after((low, high), two_low, two_high)
-    one_low, three_low = shifted(low, "tensor", -1), shifted(low, "tensor", 1)
+    backs = [None, spread_e(after(flow, copies)).reshape(-1, width)]
+    arrived[0] = after(arrived[0], *mine[3:])
+    quarter, *parts = choose_experts(place, kept, after(given, *mine[3:]), 1)
+    sides = start_gather(*parts)
     terms, pre, gates, names = experts_forward(arrived[0], top, routers, expert_weights[0], place, 0)
-    terms = after(terms, one_low, three_low)
+    terms = after(terms, backs[1])
     pieces = exchange_e(terms.reshape(-1, share, width))
-    one_high, three_high = shifted(high, "tensor", -1), shifted(high, "tensor", 1)
-    entry[1] = leave_rows(middles[0], after(pieces, one_high, three_high))
+    mine = [quarter, *sides, *end_gather(quarter, *sides)]
+    expert_weights[1] = [*mine, *[sibling(block) for block in mine]]
+    entry[1] = leave_rows(middles[0], after(pieces, *mine[3:]))
 
     blocks = gather_x(entry[1])
     outputs = [blocks, None]
     pieces, attn_saved[1] = attention_forward(blocks, tables, weights, gains_a, place, 1)
     pieces = arrivals(pieces)
-    two_low = shifted(after(low, *pieces), "tensor", -2)
-    two_high = shifted(after(high, *pieces), "tensor", -2)
-    mine = [low, high, one_low, one_high, three_low, three_high, two_low, two_high]
-    expert_weights[1] = [*mine, *[sibling(block) for block in mine]]
     middles[1], copies, shapeds[1], gates_own[1] = middle_rows(
         entry[1], pieces, gains_m, names_own, routers, place, 1, sequences
     )
@@ -903,17 +968,28 @@
         arrived[1], names, top, routers, backs[1], expert_weights[1], place, 1
     )
 
-    def join(mines, others):
+    def start_ring(mines, others):
         half = width // 2
-        return [
-            [sum_of([mines[k, a : a + half], others[k, a : a + half]]) for a in (0, half)]
-            for k in range(4)
-        ]
+        two = sum_of([mines[2], others[2]])
+        return shifted(two[:half], "tensor", 1), shifted(two[half:], "tensor", -1)
+
+    def ring_parts(mines, others, low, high):
+        half = width // 2
+        return (
+            jnp.concatenate(
+                [sum_of([mines[1, :half], others[1, :half], low]), sum_of([mines[1, half:], others[1, half:]])]
+            ),
+            jnp.concatenate(
+                [sum_of([mines[3, :half], others[3, :half]]), sum_of([mines[3, half:], others[3, half:], high])]
+            ),
+        )
+
+    def end_ring(first, third):
+        return shifted(first, "tensor", 1), shifted(third, "tensor", -1)
 
     in_blocks, smalls, grads_gain = ([None, None] for _ in range(3))
     pieces = exchange_e(terms.reshape(-1, share, width + BESIDE))
-    others = experts_grads(arrived[1], backs[1], back_pre, hidden, 1)
-    mines = experts_grads(arrived[1], backs[1], back_pre, hidden, 0)
+    mines, others = experts_grads(arrived[1], backs[1], back_pre, hidden)
     outs = experts_out(hidden, expert_weights[1])
     back_middle, rounded, smalls[1] = back_middle_rows(
         flow, after(pieces, mines, others, outs), middles[1], shapeds[1], gates_own[1], gains_m, routers, place, 1
@@ -926,94 +1002,80 @@
     flow, grads_gain[1], copies = back_entry_rows(
         back_middle, arrivals(partial), entry[1], gains_a, place, 1, sequences
     )
-    in_blocks[1] = gather_x(flow)
-    mine_half, other_half = attention_grads(place, back_qkv, attn_saved[1], branch)
     copies = after(copies, out_pieces)
     backs[0] = exchange_e(copies).reshape(-1, width)
-    last = leave_rows(middles[1], after(out_pieces, flow))
-    outputs[1] = gather_x(last)
-    joined = join(after(mines, last), others)
+    last = leave_rows(middles[1], out_pieces, (flow,))
+    mine_half, other_half = attention_grads(place, after(back_qkv, last), attn_saved[1], branch)
+    mines = after(mines, last)
+    twos = start_ring(mines, others)
     half_one = sum_of([mine_half, sibling(other_half)])
-    lows = after(tuple(block[0] for block in joined), *outputs[1], *in_blocks[1])
-    highs = tuple(block[1] for block in joined)
-    first_low, third_low = shifted(lows[1], "tensor", 1), shifted(lows[3], "tensor", 3)
-    backs[0] = after(backs[0], half_one, first_low, third_low)
-    highs = after(highs, first_low, third_low)
-    first_high, third_high = shifted(highs[1], "tensor", 1), shifted(highs[3], "tensor", 3)
+    backs[0] = after(backs[0], half_one, *twos)
+    ends = end_ring(*ring_parts(mines, others, *twos))
+    own = sum_of([mines[0], others[0]])
 
     piece = collect_e(after(half_one, backs[0]).reshape(sequences, -1, half_one.shape[1]))
     terms, back_pre, hidden = experts_backward(backs[0], pre, gates, expert_weights[0])
-    terms = after(terms, piece, first_high, third_high)
-    second_low, second_high = (
-        shifted(after(block, first_high, third_high), "tensor", 2) for block in joined[2]
-    )
+    terms = after(terms, piece)
     pieces = exchange_e(terms.reshape(-1, share, width + BESIDE))
-    others = experts_grads(arrived[0], backs[0], back_pre, hidden, 1)
-    mines = experts_grads(arrived[0], backs[0], back_pre, hidden, 0)
-    sums = [
-        None,
-        [
-            sum_of([lows[0], first_low, second_low, third_low]),
-            sum_of([highs[0], first_high, second_high, third_high]),
-        ],
-    ]
-    own, other = straight_rows(place, outputs[0], outputs[1])
-    activations = by_batch(place, own, sibling(other))
-    pieces = after(pieces, mines, others, sums[1][0], sums[1][1], activations)
+    mines, others = experts_grads(arrived[0], backs[0], back_pre, hidden)
+    sums = [None, sum_of([own, *ends])]
+    piece_one = piece
+    pieces = after(pieces, mines, others, sums[1])
     back_middle, rounded, smalls[0] = back_middle_rows(
         flow, pieces, middles[0], shapeds[0], gates_own[0], gains_m, routers, place, 0
     )
     others = sibling(after(others, rounded))
-    columns = half_one.shape[1] // 2
-    piece = after(piece, rounded)
-    done_one = [spread_e(piece[:, a : a + columns]).reshape(-1, columns) for a in (0, columns)]
-    gathered = gather_x(rounded)
-    partial, branch, back_qkv = attention_backward(gathered, attn_saved[0], tables, weights, place, 0)
-    mine_half, other_half = attention_grads(
-        place, after(back_qkv, done_one[0]), attn_saved[0], branch
-    )
-    pieces = arrivals(partial)
-    flow, grads_gain[0] = back_entry_rows(back_middle, pieces, entry[0], gains_a, place, 0, 0)
 
     def own_layer(of_first, of_second):
         own = jnp.where(first, of_first, of_second)
         return own + sibling(jnp.where(first, of_second, of_first).astype(BF)).astype(F32)
 
     small = own_layer(smalls[0], smalls[1]).astype(BF)
+    gathered = after(gather_x(rounded), small)
+    partial, branch, back_qkv = attention_backward(gathered, attn_saved[0], tables, weights, place, 0)
+    mine_half, other_half = attention_grads(place, back_qkv, attn_saved[0], branch)
+    pieces = arrivals(partial)
+    final, grads_gain[0] = back_entry_rows(
+        back_middle, pieces, entry[0], gains_a, place, 0, 0, (last,)
+    )
+
     half_zero = jnp.concatenate([sum_of([mine_half, sibling(other_half)]), small], axis=1)
-    half_zero = after(half_zero, done_one[1])
-    joined = join(after(mines, half_zero), others)
-    first_zero = [shifted(half, "tensor", 1) for half in joined[1]]
-    third_zero = [shifted(half, "tensor", 3) for half in joined[3]]
-    piece = collect_e(half_zero.reshape(sequences, -1, half_zero.shape[1]))
+    finals = gather_x(final)
+    twos = start_ring(after(mines, *finals[1:]), others)
+    cut = half_zero.shape[1]
+    both = exchange_e(
+        jnp.concatenate(
+            [
+                half_zero.reshape(sequences, -1, cut),
+                jnp.broadcast_to(piece_one[None], (sequences, *piece_one.shape)),
+            ],
+            axis=2,
+        )
+    )
+    piece = jnp.sum(both[:, :, :cut].astype(F32), axis=0).astype(BF)
+    done_one = both.reshape(half_one.shape[0], -1)[:, cut:]
     gain = own_layer(grads_gain[0], grads_gain[1]).reshape(width // 128, 128).astype(BF)
     gain = jnp.pad(gain, ((0, piece.shape[0] - width // 128), (0, 0)))
     piece = jnp.concatenate([piece, gain], axis=1)
-    piece = after(piece, *first_zero, *third_zero)
-    second_zero = [
-        shifted(after(half, *first_zero, *third_zero), "tensor", 2) for half in joined[2]
-    ]
-    spread = spread_e(piece)
+    parts = ring_parts(mines, others, *twos)
+    ends = end_ring(*parts)
+    sums[0] = sum_of([mines[0], others[0], *ends])
+    grad_gate, grad_up, grad_down = experts_finish(
+        place, [*sums, to_core(sums[0], 0), to_core(sums[1], 1)]
+    )
+    mine, other = straight_rows(place, outputs[0], finals)
+    activations, input_grads = by_batch(place, mine, sibling(other))
+    spread = after(spread_e(piece), grad_gate, activations)
     gain = jnp.sum(spread[:, : width // 128, -128:].astype(F32), axis=0).astype(BF)
-    done_zero = after(spread, *second_zero).reshape(half_one.shape[0], -1)
+    done_zero = spread.reshape(half_one.shape[0], -1)
     small = jnp.concatenate([done_zero[:, -256:-128], gain], axis=0)
-    grad_router, grad_gain_m, gain = small_finish(gather_x(small), expert_count)
-    sums[0] = [
-        sum_of([joined[0][n], first_zero[n], second_zero[n], third_zero[n]]) for n in range(2)
-    ]
-    grad_gate, grad_up, grad_down = experts_finish(
-        place,
-        [*sums[0], *sums[1], *[to_core(half, 0) for half in sums[0]], *[to_core(half, 1) for half in sums[1]]],
-    )
-    done_one = jnp.concatenate(done_one, axis=1)
+    blocks = gather_x(small)
     grad_query, grad_key, grad_value, grad_out = attention_finish(
         place,
         [done_zero, done_one, to_core(done_zero, 0), to_core(done_one, 1)],
         [w_query.shape[2], w_key.shape[2], w_value.shape[2]],
     )
-
-    own, other = straight_rows(place, gather_x(flow), in_blocks[1])
-    input_grads = by_batch(place, own, sibling(other))
+    grad_router, grad_gain_m, gain = small_finish(after(blocks, grad_query), expert_count)
     return (
         activations,
         input_grads,

time: 601 us -> 542 us (0.902)
  starting transfers between devices: 179 us -> 134 us
  waiting for transfers between devices: 180 us -> 168 us
    ppermute x90 -> x68, waiting for transfers between devices: 149 us -> 96.9 us  [shifted(): lax.ppermute(array, axis, [(i, (i + by) % length) for i in range(length)])]
    all_to_all x13 -> x11, waiting for transfers between devices: 31.9 us -> 70.7 us  [exchange_e(): return lax.all_to_all(blocks, 'expert', 0, 0, tiled=True)]
    ppermute x90 -> x68, starting transfers between devices: 89 us -> 63.6 us  [shifted(): lax.ppermute(array, axis, [(i, (i + by) % length) for i in range(length)])]
    all_to_all x13 -> x11, starting transfers between devices: 78.1 us -> 60.6 us  [exchange_e(): return lax.all_to_all(blocks, 'expert', 0, 0, tiled=True)]
    concatenate x1 -> x9, other arithmetic: 1.38 us -> 8.73 us  [the longest x2 2.28 us: ring_parts(): jnp.concatenate([sum_of([mines[1, :half], others[1, :half], low]), sum_of...]
    unnamed x220 -> x122, local copies, waits for them, and re-layouts: 21.6 us -> 16.9 us
    ppermute x6 -> x4, starting transfers between devices: 12.2 us -> 9.31 us  [to_core(): return lax.ppermute(array, 'section', [(1 - core, core)])]
    pallas_call x31 -> x29, Pallas kernels: 167 us -> 164 us  [call(): pl.pallas_call(kernel, out_shape=[jax.ShapeDtypeStruct(shape, kind) for s...]
  transfers between devices with their start and end apart: 109 -> 83, of which waited for: 46 -> 46; matrix products, arithmetic and copies ran while one was open for 6% -> 9% of each run, Pallas kernels for 21% -> 23%
where the time goes in v3:
time: 542 us; the launch traced here: 531 us
  waiting for transfers between devices  168 us (31%)
  Pallas kernels  164 us (30%)
  starting transfers between devices  134 us (25%)
  other arithmetic  36 us (7%)
  local copies, waits for them, and re-layouts  28.2 us (5%)
    pallas_call x29, Pallas kernels, call(): pl.pallas_call(kernel, out_shape=[jax.ShapeDtypeStruct(shape, kind) for s...  164 us
    ppermute x68, waiting for transfers between devices, shifted(): lax.ppermute(array, axis, [(i, (i + by) % length) for i in range(length)])  96.9 us
    all_to_all x11, waiting for transfers between devices, exchange_e(): return lax.all_to_all(blocks, 'expert', 0, 0, tiled=True)  70.7 us
    ppermute x68, starting transfers between devices, shifted(): lax.ppermute(array, axis, [(i, (i + by) % length) for i in range(length)])  63.6 us
    all_to_all x11, starting transfers between devices, exchange_e(): return lax.all_to_all(blocks, 'expert', 0, 0, tiled=True)  60.6 us
    convert_element_type x10, other arithmetic, sum_of(): return sum((block.astype(F32) for block in blocks)).astype(BF)  23.9 us
    unnamed x122, local copies, waits for them, and re-layouts  16.9 us
  transfers between devices with their start and end apart: 83, of which 46 were waited for; matrix products, arithmetic and copies ran while one was open for 9% of the time, Pallas kernels for 23%

profile of v3, /device:TPU:0, one launch (start us, length us, event | category | flops | bytes accessed | tf_op | source)
XLA Modules:
  0.0 531.2 jit_solution(8848438642974464512)
XLA Ops:
  23.8 7.0 %shard_map.232 = (bf16[32,1536]{1,0:T(8,128)(2,1)}, bf16[32,1536]{1,0:T(8,128)(2,1)}, bf16[32,1536]{1,0:T(8,128)(2,1)}, bf16[32,1536]{1,0:T(8,128)(2,1)}, bf16[1...) custom-call(s32[3]{0:T(128)} %pad_add_fusion.at, ...), custom_call_target="tpu_custom_call" | custom-call | flops 1 | bytes 1 | tf_op jit(solution)/shard_map/pallas_call | solution.py:92
  49.3 8.0 %all-to-all-start = ((bf16[16,32,1664]{2,1,0:T(8,128)(2,1)}), bf16[16,32,1664]{2,1,0:T(8,128)(2,1)S(1)}, u32[]{:S(2)}, u32[]{:S(2)}) async-start(bf16[16,32,1664]{2,1,0:T(8,128)(2,1)} %get-tuple-element.152), calls=%async_computation | async-start | bytes 3407872 | tf_op jit(solution)/shard_map/all_to_all | solution.py:71
  64.3 16.0 %all-to-all-done = bf16[16,32,1664]{2,1,0:T(8,128)(2,1)S(1)} async-done(((bf16[16,32,1664]{2,1,0:T(8,128)(2,1)}), bf16[16,32,1664]{2,1,0:T(8,128)(2,1)S(1)}, u32[]{:S(2)}, u32[]{:S(2)}) %all-to-all-start) | async-done | bytes 1703968 | tf_op jit(solution)/shard_map/all_to_all | solution.py:71
  82.0 4.5 all-to-all-start.1
  94.2 11.5 %shard_map.234 = (bf16[512,1536]{1,0:T(8,128)(2,1)}, bf16[512,2048]{1,0:T(8,128)(2,1)}, f32[512,128]{1,0:T(8,128)}, bf16[512,128]{1,0:T(8,128)(2,1)}) custom-call(s32[3]{0:T(128)} %pad_add_fusion.at, bf16[512,1664]{1,0:T(8,128)(2,1)} %bitcast.87, bf16[32,1536]{1,0:T(8,128)(2,1)} %bitcast.103, bf16[32,1536]{1,0:T(8,128)(2,1)} %copy-done.18, ...), custom_call_target="tpu_custom_call" | custom-call | flops 1 | bytes 1 | tf_op jit(solution)/shard_map/pallas_call | solution.py:92
  107.1 5.9 %all-to-all-start.2 = ((bf16[16,32,1536]{2,1,0:T(8,128)(2,1)}), bf16[16,32,1536]{2,1,0:T(8,128)(2,1)}, u32[]{:S(2)}, u32[]{:S(2)}) async-start(bf16[16,32,1536]{2,1,0:T(8,128)(2,1)} %bitcast.110), calls=%async_computation.2 | async-start | bytes 3145728 | tf_op jit(solution)/shard_map/all_to_all | solution.py:71
  117.9 17.1 %collective-permute-done.21.refs_3_ = bf16[1152,384]{1,0:T(8,128)(2,1)} collective-permute-done((bf16[1152,384]{1,0:T(8,128)(2,1)S(1)}, bf16[1152,384]{1,0:T(8,128)(2,1)}, u32[]{:S(2)}, u32[]{:S(2)}) %collective-permute-start.21) | collective-permute-done | bytes 884768 | tf_op jit(solution)/shard_map/ppermute | solution.py:26
  135.0 4.8 collective-permute-done.23.refs_4_
  150.8 6.9 %shard_map.237 = (bf16[32,1536]{1,0:T(8,128)(2,1)}, bf16[32,1536]{1,0:T(8,128)(2,1)}, bf16[32,1536]{1,0:T(8,128)(2,1)}, bf16[32,1536]{1,0:T(8,128)(2,1)}, bf16[1...) custom-call(s32[3]{0:T(128)} %pad_add_fusion.at, ...), custom_call_target="tpu_custom_call" | custom-call | flops 1 | bytes 1 | tf_op jit(solution)/shard_map/pallas_call | solution.py:92
  170.0 7.1 %all-to-all-start.3 = ((bf16[16,32,1536]{2,1,0:T(8,128)(2,1)}), bf16[16,32,1536]{2,1,0:T(8,128)(2,1)S(1)}, u32[]{:S(2)}, u32[]{:S(2)}) async-start(bf16[16,32,1536]{2,1,0:T(8,128)(2,1)} %get-tuple-element.167), calls=%async_computation.3 | async-start | bytes 3145728 | tf_op jit(solution)/shard_map/all_to_all | solution.py:71
  186.2 9.7 %all-to-all-done.3 = bf16[16,32,1536]{2,1,0:T(8,128)(2,1)S(1)} async-done(((bf16[16,32,1536]{2,1,0:T(8,128)(2,1)}), bf16[16,32,1536]{2,1,0:T(8,128)(2,1)S(1)}, u32[]{:S(2)}, u32[]{:S(2)}) %all-to-all-start.3) | async-done | bytes 1572896 | tf_op jit(solution)/shard_map/all_to_all | solution.py:71
  197.1 15.5 %shard_map.239 = (bf16[512,1664]{1,0:T(8,128)(2,1)}, bf16[512,2048]{1,0:T(8,128)(2,1)}, bf16[512,1024]{1,0:T(8,128)(2,1)}) custom-call(s32[3]{0:T(128)} %pad_add_fusion.at, bf16[512,1536]{1,0:T(8,128)(2,1)} %bitcast.91, bf16[512,128]{1,0:T(8,128)(2,1)} %get-tuple-element.168.names_ref, bf16[32,1536]{1,0:T(8,128)(2,1)} %bitcast.105, ...), custom_call_target="tpu_custom_call" | custom-call | flops 1 | bytes 1 | tf_op jit(solution)/shard_map/pallas_call | solution.py:92
  216.7 13.6 %shard_map.240 = (bf16[4,1536,384]{2,1,0:T(8,128)(2,1)}, bf16[4,1536,384]{2,1,0:T(8,128)(2,1)}) custom-call(bf16[512,1536]{1,0:T(8,128)(2,1)} %bitcast.92, bf16[512,1536]{1,0:T(8,128)(2,1)} %bitcast.17.back_ref, bf16[512,2048]{1,0:T(8,128)(2,1)} %get-tuple-element.170.pre_ref, bf16[512,1024]{1,0:T(8,128)(2,1)} %get-tuple-element.171.hidden_ref), custom_call_target="tpu_custom_call" | custom-call | flops 1 | bytes 1 | tf_op jit(solution)/shard_map/pallas_call | solution.py:92
  230.3 6.3 %shard_map.241 = bf16[512,1536]{1,0:T(8,128)(2,1)} custom-call(bf16[512,1024]{1,0:T(8,128)(2,1)} %get-tuple-element.171.hidden_ref, bf16[1536,384]{1,0:T(8,128)(2,1)} %get-tuple-element.159.refs_0_, bf16[1152,384]{1,0:T(8,128)(2,1)} %copy-done.11, bf16[1152,384]{1,0:T(8,128)(2,1)} %collective-permute-done.22.refs_2_, ...), custom_call_target="tpu_custom_call" | custom-call | flops 1 | bytes 1 | tf_op jit(solution)/shard_map/pallas_call | solution.py:92
  242.8 5.6 %all-to-all-start.5 = ((bf16[16,32,1536]{2,1,0:T(8,128)(2,1)}), bf16[16,32,1536]{2,1,0:T(8,128)(2,1)S(1)}, u32[]{:S(2)}, u32[]{:S(2)}) async-start(bf16[16,32,1536]{2,1,0:T(8,128)(2,1)} %bitcast.21), calls=%async_computation.5 | async-start | bytes 3145728 | tf_op jit(solution)/shard_map/all_to_all | solution.py:71
  257.9 8.8 %shard_map.243 = (bf16[32,1536]{1,0:T(8,128)(2,1)}, bf16[32,1536]{1,0:T(8,128)(2,1)}, bf16[32,1536]{1,0:T(8,128)(2,1)}, bf16[32,1536]{1,0:T(8,128)(2,1)}, bf16[1...) custom-call(s32[3]{0:T(128)} %pad_add_fusion.at, bf16[32,1536]{1,0:T(8,128)(2,1)} %get-tuple-element.179.b0, ...), custom_call_target="tpu_custom_call" | custom-call | flops 1 | bytes 1 | tf_op jit(solution)/shard_map/pallas_call | solution.py:92
  286.1 6.9 %all-to-all-start.6 = ((bf16[16,32,1536]{2,1,0:T(8,128)(2,1)}), bf16[16,32,1536]{2,1,0:T(8,128)(2,1)S(1)}, u32[]{:S(2)}, u32[]{:S(2)}) async-start(bf16[16,32,1536]{2,1,0:T(8,128)(2,1)} %get-tuple-element.189), calls=%async_computation.6 | async-start | bytes 3145728 | tf_op jit(solution)/shard_map/all_to_all | solution.py:71
  300.2 18.2 %all-to-all-done.6 = bf16[16,32,1536]{2,1,0:T(8,128)(2,1)S(1)} async-done(((bf16[16,32,1536]{2,1,0:T(8,128)(2,1)}), bf16[16,32,1536]{2,1,0:T(8,128)(2,1)S(1)}, u32[]{:S(2)}, u32[]{:S(2)}) %all-to-all-start.6) | async-done | bytes 1572896 | tf_op jit(solution)/shard_map/all_to_all | solution.py:71
  331.8 11.8 %shard_map.247 = (bf16[512,1664]{1,0:T(8,128)(2,1)}, bf16[512,2048]{1,0:T(8,128)(2,1)}, bf16[512,1024]{1,0:T(8,128)(2,1)}) custom-call(bf16[512,1536]{1,0:T(8,128)(2,1)} %bitcast.89, bf16[512,2048]{1,0:T(8,128)(2,1)} %get-tuple-element.200.pre_ref, f32[512,128]{1,0:T(8,128)} %get-tuple-element.201.gates_ref, bf16[1536,384]{1,0:T(8,128)(2,1)} %get-tuple-element.153.refs_0_, ...), custom_call_target="tpu_custom_call" | custom-call | flops 1 | bytes 1 | tf_op jit(solution)/shard_map/pallas_call | solution.py:92
  346.4 4.9 all-to-all-start.8
  351.3 13.8 %shard_map.248 = (bf16[4,1536,384]{2,1,0:T(8,128)(2,1)}, bf16[4,1536,384]{2,1,0:T(8,128)(2,1)}) custom-call(bf16[512,1664]{1,0:T(8,128)(2,1)} %bitcast.88, bf16[512,1536]{1,0:T(8,128)(2,1)} %bitcast.90, bf16[512,2048]{1,0:T(8,128)(2,1)} %get-tuple-element.205.pre_ref, bf16[512,1024]{1,0:T(8,128)(2,1)} %get-tuple-element.206.hidden_ref), custom_call_target="tpu_custom_call" | custom-call | flops 1 | bytes 1 | tf_op jit(solution)/shard_map/pallas_call | solution.py:92
  369.1 5.6 %all-to-all-done.8.pieces_ref = bf16[16,32,1664]{2,1,0:T(8,128)(2,1)S(1)} async-done(((bf16[16,32,1664]{2,1,0:T(8,128)(2,1)}), bf16[16,32,1664]{2,1,0:T(8,128)(2,1)S(1)}, u32[]{:S(2)}, u32[]{:S(2)}) %all-to-all-start.8) | async-done | bytes 1703968 | tf_op jit(solution)/shard_map/all_to_all | solution.py:71
  380.8 4.3 collective-permute-start.48
  390.8 8.8 %shard_map.250 = (bf16[32,1536]{1,0:T(8,128)(2,1)}, bf16[32,1536]{1,0:T(8,128)(2,1)}, bf16[32,1536]{1,0:T(8,128)(2,1)}, bf16[32,1536]{1,0:T(8,128)(2,1)}, bf16[1...) custom-call(s32[3]{0:T(128)} %pad_add_fusion.at, bf16[32,1536]{1,0:T(8,128)(2,1)} %get-tuple-element.216.b0, ...), custom_call_target="tpu_custom_call" | custom-call | flops 1 | bytes 1 | tf_op jit(solution)/shard_map/pallas_call | solution.py:92
  424.1 4.4 all-to-all-start.9
  428.5 4.5 collective-permute-done.55.refs_6_
  440.2 10.5 %collective-permute-done.61 = bf16[768,384]{1,0:T(8,128)(2,1)S(1)} collective-permute-done((bf16[768,384]{1,0:T(8,128)(2,1)S(1)}, bf16[768,384]{1,0:T(8,128)(2,1)S(1)}, u32[]{:S(2)}, u32[]{:S(2)}) %collective-permute-start.61) | collective-permute-done | bytes 589856 | tf_op jit(solution)/shard_map/ppermute | solution.py:26
  459.4 14.3 %all-to-all-done.9 = bf16[16,48,2176]{2,1,0:T(8,128)(2,1)S(1)} async-done(((bf16[16,48,2176]{2,1,0:T(8,128)(2,1)}), bf16[16,48,2176]{2,1,0:T(8,128)(2,1)S(1)}, u32[]{:S(2)}, u32[]{:S(2)}) %all-to-all-start.9) | async-done | bytes 3342368 | tf_op jit(solution)/shard_map/all_to_all | solution.py:71
  475.4 5.4 %all-to-all-start.10 = ((bf16[16,48,1280]{2,1,0:T(8,128)(2,1)}), bf16[16,48,1280]{2,1,0:T(8,128)(2,1)}, u32[]{:S(2)}, u32[]{:S(2)}) async-start(bf16[16,48,1280]{2,1,0:T(8,128)(2,1)} %broadcast_in_dim.10), calls=%async_computation.10 | async-start | bytes 3932160 | tf_op jit(solution)/shard_map/all_to_all | solution.py:71
  500.4 5.0 shard_map.255
  509.4 4.4 collective-permute-start.71
  520.2 6.4 %shard_map.256 = (f32[1,1536,384]{2,1,0:T(8,128)}, f32[1,1536,128]{2,1,0:T(8,128)}, f32[1,1536,128]{2,1,0:T(8,128)}, f32[1,384,1536]{2,1,0:T(8,128)}) custom-call(s32[3]{0:T(128)} %pad_add_fusion.at, bf16[768,1280]{1,0:T(8,128)(2,1)} %bitcast.40.h0, bf16[768,1024]{1,0:T(8,128)(2,1)} %copy-done.13, bf16[768,1280]{1,0:T(8,128)(2,1)} %collective-permute-done.70.h2, ...), custom_call_target="tpu_custom_call" | custom-call | flops 1 | bytes 1 | tf_op jit(solution)/shard_map/pallas_call | solution.py:92
  (332 shorter events, 251.9 us)
Async XLA Ops:
  4.9 18.5 %collective-permute-start.2 = (bf16[1536,384]{1,0:T(8,128)(2,1)S(1)}, bf16[1536,384]{1,0:T(8,128)(2,1)}, u32[]{:S(2)}, u32[]{:S(2)}) collective-permute-start(bf16[1536,384]{1,0:T(8,128)(2,1)S(1)} %bitcast.81), channel_id=1, source_target_pairs={{0,64},{64,0},{1,65},{65,1},{2,66},{66,2},{3,67},{67,3},{4,68},{68... | collective-permute-start | bytes 3538952 | tf_op jit(solution)/shard_map/ppermute | solution.py:26
  12.2 22.4 %collective-permute-start.6 = (bf16[1152,384]{1,0:T(8,128)(2,1)}, bf16[1152,384]{1,0:T(8,128)(2,1)}, u32[]{:S(2)}, u32[]{:S(2)}) collective-permute-start(bf16[1152,384]{1,0:T(8,128)(2,1)} %get-tuple-element.145), channel_id=1, source_target_pairs={{0,3},{1,0},{2,1},{3,2},{4,7},{5,4},{6,5},{7,6},{8,11},{9,8},{10,9... | collective-permute-start | bytes 2654216 | tf_op jit(solution)/shard_map/ppermute | solution.py:26
  15.1 22.9 %collective-permute-start.7 = (bf16[1152,384]{1,0:T(8,128)(2,1)}, bf16[1152,384]{1,0:T(8,128)(2,1)}, u32[]{:S(2)}, u32[]{:S(2)}) collective-permute-start(bf16[1152,384]{1,0:T(8,128)(2,1)} %get-tuple-element.146), channel_id=1, source_target_pairs={{0,1},{1,2},{2,3},{3,0},{4,5},{5,6},{6,7},{7,4},{8,9},{9,10},{10,1... | collective-permute-start | bytes 2654216 | tf_op jit(solution)/shard_map/ppermute | solution.py:26
  23.0 19.0 %collective-permute-start.11 = (bf16[1,1536]{1,0:T(2,128)(2,1)S(1)}, bf16[1,1536]{1,0:T(2,128)(2,1)S(1)}, u32[]{:S(2)}, u32[]{:S(2)}) collective-permute-start(bf16[1,1536]{1,0:T(2,128)(2,1)S(1)} %copy-done.42), channel_id=1, source_target_pairs={{0,64},{64,0},{1,65},{65,1},{2,66},{66,2},{3,67},{67,3},{4,68},{68... | collective-permute-start | bytes 9224 | tf_op jit(solution)/shard_map/ppermute | solution.py:26
  23.4 18.5 %collective-permute-start.12 = (bf16[32,1536]{1,0:T(8,128)(2,1)}, bf16[32,1536]{1,0:T(8,128)(2,1)S(1)}, u32[]{:S(2)}, u32[]{:S(2)}) collective-permute-start(bf16[32,1536]{1,0:T(8,128)(2,1)} %bitcast.101), channel_id=1, source_target_pairs={{0,64},{64,0},{1,65},{65,1},{2,66},{66,2},{3,67},{67,3},{4,68},{68... | collective-permute-start | bytes 294920 | tf_op jit(solution)/shard_map/ppermute | solution.py:26
  49.3 30.9 %all-to-all-start = ((bf16[16,32,1664]{2,1,0:T(8,128)(2,1)}), bf16[16,32,1664]{2,1,0:T(8,128)(2,1)S(1)}, u32[]{:S(2)}, u32[]{:S(2)}) async-start(bf16[16,32,1664]{2,1,0:T(8,128)(2,1)} %get-tuple-element.152), calls=%async_computation | async-start | bytes 3407872 | tf_op jit(solution)/shard_map/all_to_all | solution.py:71
  57.4 33.7 %collective-permute-start.15 = (bf16[1536,384]{1,0:T(8,128)(2,1)}, bf16[1536,384]{1,0:T(8,128)(2,1)}, u32[]{:S(2)}, u32[]{:S(2)}) collective-permute-start(bf16[1536,384]{1,0:T(8,128)(2,1)} %get-tuple-element.153.refs_0_), channel_id=1, source_target_pairs={{0,64},{64,0},{1,65},{65,1},{2,66},{66,2},{3,67},{67,3},{4,68},{68... | collective-permute-start | bytes 3538952 | tf_op jit(solution)/shard_map/ppermute | solution.py:26
  60.9 26.2 %collective-permute-start.13 = (bf16[1152,384]{1,0:T(8,128)(2,1)}, bf16[1152,384]{1,0:T(8,128)(2,1)S(1)}, u32[]{:S(2)}, u32[]{:S(2)}) collective-permute-start(bf16[1152,384]{1,0:T(8,128)(2,1)} %pad_maximum_fusion.6), channel_id=1, source_target_pairs={{0,3},{1,0},{2,1},{3,2},{4,7},{5,4},{6,5},{7,6},{8,11},{9,8},{10,9... | collective-permute-start | bytes 2654216 | tf_op jit(solution)/shard_map/ppermute | solution.py:26
  64.3 23.2 %collective-permute-start.14 = (bf16[1152,384]{1,0:T(8,128)(2,1)}, bf16[1152,384]{1,0:T(8,128)(2,1)}, u32[]{:S(2)}, u32[]{:S(2)}) collective-permute-start(bf16[1152,384]{1,0:T(8,128)(2,1)} %pad_maximum_fusion.7), channel_id=1, source_target_pairs={{0,1},{1,2},{2,3},{3,0},{4,5},{5,6},{6,7},{7,4},{8,9},{9,10},{10,1... | collective-permute-start | bytes 2654216 | tf_op jit(solution)/shard_map/ppermute | solution.py:26
  82.0 25.2 %all-to-all-start.1 = ((bf16[16,32,1536]{2,1,0:T(8,128)(2,1)}), bf16[16,32,1536]{2,1,0:T(8,128)(2,1)}, u32[]{:S(2)}, u32[]{:S(2)}) async-start(bf16[16,32,1536]{2,1,0:T(8,128)(2,1)} %broadcast_in_dim.8), calls=%async_computation.1 | async-start | bytes 3145728 | tf_op jit(solution)/shard_map/all_to_all | solution.py:71
  91.1 22.3 %collective-permute-start.20 = (bf16[1152,384]{1,0:T(8,128)(2,1)}, bf16[1152,384]{1,0:T(8,128)(2,1)S(1)}, u32[]{:S(2)}, u32[]{:S(2)}) collective-permute-start(bf16[1152,384]{1,0:T(8,128)(2,1)} %get-tuple-element.160), channel_id=1, source_target_pairs={{0,3},{1,0},{2,1},{3,2},{4,7},{5,4},{6,5},{7,6},{8,11},{9,8},{10,9... | collective-permute-start | bytes 2654216 | tf_op jit(solution)/shard_map/ppermute | solution.py:26
  93.3 23.3 %collective-permute-start.22 = (bf16[1152,384]{1,0:T(8,128)(2,1)}, bf16[1152,384]{1,0:T(8,128)(2,1)}, u32[]{:S(2)}, u32[]{:S(2)}) collective-permute-start(bf16[1152,384]{1,0:T(8,128)(2,1)} %get-tuple-element.161), channel_id=1, source_target_pairs={{0,1},{1,2},{2,3},{3,0},{4,5},{5,6},{6,7},{7,4},{8,9},{9,10},{10,1... | collective-permute-start | bytes 2654216 | tf_op jit(solution)/shard_map/ppermute | solution.py:26
  107.1 32.6 %all-to-all-start.2 = ((bf16[16,32,1536]{2,1,0:T(8,128)(2,1)}), bf16[16,32,1536]{2,1,0:T(8,128)(2,1)}, u32[]{:S(2)}, u32[]{:S(2)}) async-start(bf16[16,32,1536]{2,1,0:T(8,128)(2,1)} %bitcast.110), calls=%async_computation.2 | async-start | bytes 3145728 | tf_op jit(solution)/shard_map/all_to_all | solution.py:71
  113.6 21.4 %collective-permute-start.21 = (bf16[1152,384]{1,0:T(8,128)(2,1)S(1)}, bf16[1152,384]{1,0:T(8,128)(2,1)}, u32[]{:S(2)}, u32[]{:S(2)}) collective-permute-start(bf16[1152,384]{1,0:T(8,128)(2,1)S(1)} %pad_maximum_fusion.8), channel_id=1, source_target_pairs={{0,3},{1,0},{2,1},{3,2},{4,7},{5,4},{6,5},{7,6},{8,11},{9,8},{10,9... | collective-permute-start | bytes 2654216 | tf_op jit(solution)/shard_map/ppermute | solution.py:26
  117.9 21.9 %collective-permute-start.23 = (bf16[1152,384]{1,0:T(8,128)(2,1)S(1)}, bf16[1152,384]{1,0:T(8,128)(2,1)}, u32[]{:S(2)}, u32[]{:S(2)}) collective-permute-start(bf16[1152,384]{1,0:T(8,128)(2,1)S(1)} %pad_maximum_fusion.9), channel_id=1, source_target_pairs={{0,1},{1,2},{2,3},{3,0},{4,5},{5,6},{6,7},{7,4},{8,9},{9,10},{10,1... | collective-permute-start | bytes 2654216 | tf_op jit(solution)/shard_map/ppermute | solution.py:26
  170.0 25.9 %all-to-all-start.3 = ((bf16[16,32,1536]{2,1,0:T(8,128)(2,1)}), bf16[16,32,1536]{2,1,0:T(8,128)(2,1)S(1)}, u32[]{:S(2)}, u32[]{:S(2)}) async-start(bf16[16,32,1536]{2,1,0:T(8,128)(2,1)} %get-tuple-element.167), calls=%async_computation.3 | async-start | bytes 3145728 | tf_op jit(solution)/shard_map/all_to_all | solution.py:71
  212.5 25.8 %all-to-all-start.4 = ((bf16[16,32,1664]{2,1,0:T(8,128)(2,1)}), bf16[16,32,1664]{2,1,0:T(8,128)(2,1)S(1)}, u32[]{:S(2)}, u32[]{:S(2)}) async-start(bf16[16,32,1664]{2,1,0:T(8,128)(2,1)} %bitcast.109), calls=%async_computation.4 | async-start | bytes 3407872 | tf_op jit(solution)/shard_map/all_to_all | solution.py:71
  242.8 50.3 %collective-permute-start.42 = (bf16[4,1536,384]{2,1,0:T(8,128)(2,1)}, bf16[4,1536,384]{2,1,0:T(8,128)(2,1)}, u32[]{:S(2)}, u32[]{:S(2)}) collective-permute-start(bf16[4,1536,384]{2,1,0:T(8,128)(2,1)} %get-tuple-element.198), channel_id=1, source_target_pairs={{0,64},{64,0},{1,65},{65,1},{2,66},{66,2},{3,67},{67,3},{4,68},{68... | collective-permute-start | bytes 14155784 | tf_op jit(solution)/shard_map/ppermute | solution.py:26
  242.8 36.4 %all-to-all-start.5 = ((bf16[16,32,1536]{2,1,0:T(8,128)(2,1)}), bf16[16,32,1536]{2,1,0:T(8,128)(2,1)S(1)}, u32[]{:S(2)}, u32[]{:S(2)}) async-start(bf16[16,32,1536]{2,1,0:T(8,128)(2,1)} %bitcast.21), calls=%async_computation.5 | async-start | bytes 3145728 | tf_op jit(solution)/shard_map/all_to_all | solution.py:71
  286.1 32.2 %all-to-all-start.6 = ((bf16[16,32,1536]{2,1,0:T(8,128)(2,1)}), bf16[16,32,1536]{2,1,0:T(8,128)(2,1)S(1)}, u32[]{:S(2)}, u32[]{:S(2)}) async-start(bf16[16,32,1536]{2,1,0:T(8,128)(2,1)} %get-tuple-element.189), calls=%async_computation.6 | async-start | bytes 3145728 | tf_op jit(solution)/shard_map/all_to_all | solution.py:71
  296.1 22.2 %collective-permute-start.44 = (bf16[768,384]{1,0:T(8,128)(2,1)}, bf16[768,384]{1,0:T(8,128)(2,1)}, u32[]{:S(2)}, u32[]{:S(2)}) collective-permute-start(bf16[768,384]{1,0:T(8,128)(2,1)} %get-tuple-element.266), channel_id=1, source_target_pairs={{0,3},{1,0},{2,1},{3,2},{4,7},{5,4},{6,5},{7,6},{8,11},{9,8},{10,9... | collective-permute-start | bytes 1769480 | tf_op jit(solution)/shard_map/ppermute | solution.py:26
  298.3 20.0 %collective-permute-start.43 = (bf16[768,384]{1,0:T(8,128)(2,1)}, bf16[768,384]{1,0:T(8,128)(2,1)}, u32[]{:S(2)}, u32[]{:S(2)}) collective-permute-start(bf16[768,384]{1,0:T(8,128)(2,1)} %get-tuple-element.267), channel_id=1, source_target_pairs={{0,1},{1,2},{2,3},{3,0},{4,5},{5,6},{6,7},{7,4},{8,9},{9,10},{10,1... | collective-permute-start | bytes 1769480 | tf_op jit(solution)/shard_map/ppermute | solution.py:26
  319.5 26.6 %all-to-all-start.7 = ((bf16[16,48,1024]{2,1,0:T(8,128)(2,1)}), bf16[16,48,1024]{2,1,0:T(8,128)(2,1)S(1)}, u32[]{:S(2)}, u32[]{:S(2)}) async-start(bf16[16,48,1024]{2,1,0:T(8,128)(2,1)} %bitcast.95), calls=%async_computation.7 | async-start | bytes 3145728 | tf_op jit(solution)/shard_map/all_to_all | solution.py:71
  328.6 36.5 %collective-permute-start.46 = (bf16[1536,384]{1,0:T(8,128)(2,1)}, bf16[1536,384]{1,0:T(8,128)(2,1)}, u32[]{:S(2)}, u32[]{:S(2)}) collective-permute-start(bf16[1536,384]{1,0:T(8,128)(2,1)} %pad_maximum_fusion.3), channel_id=1, source_target_pairs={{0,3},{1,0},{2,1},{3,2},{4,7},{5,4},{6,5},{7,6},{8,11},{9,8},{10,9... | collective-permute-start | bytes 3538952 | tf_op jit(solution)/shard_map/ppermute | solution.py:26
  331.8 33.3 %collective-permute-start.45 = (bf16[1536,384]{1,0:T(8,128)(2,1)}, bf16[1536,384]{1,0:T(8,128)(2,1)}, u32[]{:S(2)}, u32[]{:S(2)}) collective-permute-start(bf16[1536,384]{1,0:T(8,128)(2,1)} %pad_maximum_fusion.2), channel_id=1, source_target_pairs={{0,1},{1,2},{2,3},{3,0},{4,5},{5,6},{6,7},{7,4},{8,9},{9,10},{10,1... | collective-permute-start | bytes 3538952 | tf_op jit(solution)/shard_map/ppermute | solution.py:26
  346.4 28.3 %all-to-all-start.8 = ((bf16[16,32,1664]{2,1,0:T(8,128)(2,1)}), bf16[16,32,1664]{2,1,0:T(8,128)(2,1)S(1)}, u32[]{:S(2)}, u32[]{:S(2)}) async-start(bf16[16,32,1664]{2,1,0:T(8,128)(2,1)} %bitcast.108), calls=%async_computation.8 | async-start | bytes 3407872 | tf_op jit(solution)/shard_map/all_to_all | solution.py:71
  379.1 53.9 %collective-permute-start.60 = (bf16[4,1536,384]{2,1,0:T(8,128)(2,1)}, bf16[4,1536,384]{2,1,0:T(8,128)(2,1)}, u32[]{:S(2)}, u32[]{:S(2)}) collective-permute-start(bf16[4,1536,384]{2,1,0:T(8,128)(2,1)} %get-tuple-element.239), channel_id=1, source_target_pairs={{0,64},{64,0},{1,65},{65,1},{2,66},{66,2},{3,67},{67,3},{4,68},{68... | collective-permute-start | bytes 14155784 | tf_op jit(solution)/shard_map/ppermute | solution.py:26
  424.1 49.6 %all-to-all-start.9 = ((bf16[16,48,2176]{2,1,0:T(8,128)(2,1)}), bf16[16,48,2176]{2,1,0:T(8,128)(2,1)S(1)}, u32[]{:S(2)}, u32[]{:S(2)}) async-start(bf16[16,48,2176]{2,1,0:T(8,128)(2,1)} %pad_maximum_fusion), calls=%async_computation.9 | async-start | bytes 6684672 | tf_op jit(solution)/shard_map/all_to_all | solution.py:71
  453.9 29.2 %collective-permute-start.64 = (bf16[1536,384]{1,0:T(8,128)(2,1)}, bf16[1536,384]{1,0:T(8,128)(2,1)}, u32[]{:S(2)}, u32[]{:S(2)}) collective-permute-start(bf16[1536,384]{1,0:T(8,128)(2,1)} %pad_maximum_fusion.5), channel_id=1, source_target_pairs={{0,3},{1,0},{2,1},{3,2},{4,7},{5,4},{6,5},{7,6},{8,11},{9,8},{10,9... | collective-permute-start | bytes 3538952 | tf_op jit(solution)/shard_map/ppermute | solution.py:26
  458.1 27.2 %collective-permute-start.62 = (bf16[1536,384]{1,0:T(8,128)(2,1)}, bf16[1536,384]{1,0:T(8,128)(2,1)}, u32[]{:S(2)}, u32[]{:S(2)}) collective-permute-start(bf16[1536,384]{1,0:T(8,128)(2,1)} %pad_maximum_fusion.4), channel_id=1, source_target_pairs={{0,1},{1,2},{2,3},{3,0},{4,5},{5,6},{6,7},{7,4},{8,9},{9,10},{10,1... | collective-permute-start | bytes 3538952 | tf_op jit(solution)/shard_map/ppermute | solution.py:26
  475.4 31.4 %all-to-all-start.10 = ((bf16[16,48,1280]{2,1,0:T(8,128)(2,1)}), bf16[16,48,1280]{2,1,0:T(8,128)(2,1)}, u32[]{:S(2)}, u32[]{:S(2)}) async-start(bf16[16,48,1280]{2,1,0:T(8,128)(2,1)} %broadcast_in_dim.10), calls=%async_computation.10 | async-start | bytes 3932160 | tf_op jit(solution)/shard_map/all_to_all | solution.py:71
  480.8 19.6 %collective-permute-start.66 = (bf16[1536,384]{1,0:T(8,128)(2,1)}, bf16[1536,384]{1,0:T(8,128)(2,1)}, u32[]{:S(2)}, u32[]{:S(2)}) collective-permute-start(bf16[1536,384]{1,0:T(8,128)(2,1)} %fusion.1.s1), channel_id=1, source_target_pairs={{0,64},{1,65},{2,66},{3,67},{4,68},{5,69},{6,70},{7,71},{8,72},{9,... | collective-permute-start | bytes 3538952 | tf_op jit(solution)/shard_map/ppermute | solution.py:34
  (112 other events, 726.1 us)
